TPU v7x, 32 devices: a whole 2x2x4 slice. The times are simulated.
32 devices in a mesh: dom: 16 (over z, y, x), rep: 2 (over core).
Axes of the slice: x: 2, y: 2, z: 4, core: 2. Of those that a mesh axis runs over, the one named last changes fastest.
Arguments:
- node_state: bfloat16 [8192, 384], P(('rep', 'dom')), parts along dimension 0, may hold values from -6 to 6
- edge_state: bfloat16 [32768, 384], P(('rep', 'dom')), parts along dimension 0, may hold values from -6 to 6
- edge_source: int32 [32768], P(('rep', 'dom')), parts along dimension 0, may hold values from 0 to 383
- contact_block: int32 [128], P(('rep', 'dom')), parts along dimension 0, may hold values from 0 to 1
- contact_host: int32 [128, 1], P(('rep', 'dom')), parts along dimension 0, may hold values from 0 to 15; in each aligned block of 4 rows (0 to 3, 4 to 7, ...) at most 2 rows name the same one
- contact_remote: int32 [128], P(('rep', 'dom')), parts along dimension 0, may hold values from 0 to 1
- w_edge_in: bfloat16 [2304, 384], P('rep'), parts along dimension 0, may hold values from -0.1875 to 0.1875
- w_edge_out: bfloat16 [768, 384], P('rep'), parts along dimension 0, may hold values from -0.3125 to 0.3125
- w_node_in: bfloat16 [2304, 384], P('rep'), parts along dimension 0, may hold values from -0.1875 to 0.1875
- w_node_out: bfloat16 [768, 384], P('rep'), parts along dimension 0, may hold values from -0.3125 to 0.3125
- w_contact_in: bfloat16 [1536, 384], P('rep'), parts along dimension 0, may hold values from -0.21875 to 0.21875
- w_contact_out: bfloat16 [768, 384], P('rep'), parts along dimension 0, may hold values from -0.3125 to 0.3125
- node_cot: bfloat16 [8192, 384], P(('rep', 'dom')), parts along dimension 0, may hold values from -6 to 6
- edge_cot: bfloat16 [32768, 384], P(('rep', 'dom')), parts along dimension 0, may hold values from -6 to 6
Outputs:
- node_out: bfloat16 [8192, 384], P(('rep', 'dom')), parts along dimension 0
- edge_out: bfloat16 [32768, 384], P(('rep', 'dom')), parts along dimension 0
- node_grad: bfloat16 [8192, 384], P(('rep', 'dom')), parts along dimension 0
- edge_grad: bfloat16 [32768, 384], P(('rep', 'dom')), parts along dimension 0
- grad_edge_in: float32 [2304, 384], P('rep'), parts along dimension 0
- grad_edge_out: float32 [768, 384], P('rep'), parts along dimension 0
- grad_node_in: float32 [2304, 384], P('rep'), parts along dimension 0
- grad_node_out: float32 [768, 384], P('rep'), parts along dimension 0
- grad_contact_in: float32 [1536, 384], P('rep'), parts along dimension 0
- grad_contact_out: float32 [768, 384], P('rep'), parts along dimension 0
There are 2 independent parts, one for each index of `rep`. A program takes and returns all parts, laid end to end along the dimension named above; each array names one. Nothing has to cross between parts.
Inputs may be any that keep to these rules, and one draw needn't show every extreme that they name: `contact_host`: the 4 rows of one partition name any one host partition at most 2 times, and 2 times in some partition.
All inputs are finite; a program needn't handle non-finite values.
Results may differ from a plain program's by a relative error of at most 0.0082.
Values may be sent and summed in bfloat16 or wider, within the bound.
No kernel may reach another device: no remote copies, remote signals or barrier semaphores. Data moves between devices by JAX's collectives and lax.ppermute only.
A program may use at most 128 MiB of HBM per device.

v0:
```python
import jax
import jax.numpy as jnp
from jax import lax
from jax.sharding import PartitionSpec as P

BLOCK = 128
EPN = 4
RIM = 64
CAP = 2


norm_eps = 1e-05


def with_halo(value, sides, width):
    for axis, dim in sides:
        peers, length = (lax.axis_size(axis), value.shape[dim])
        up = [(i, (i + 1) % peers) for i in range(peers - 1)]
        down = [(j, i) for i, j in up]
        last = lax.slice_in_dim(value, length - width, length, axis=dim)
        initial = lax.slice_in_dim(value, 0, width, axis=dim)
        before = lax.ppermute(last, axis, up)
        after = lax.ppermute(initial, axis, down)
        value = jnp.concatenate([before, value, after], axis=dim)
    return value


def layer_norm(values):
    center = values - jnp.mean(values, axis=-1, keepdims=True)
    scale = lax.rsqrt(jnp.mean(center * center, axis=-1, keepdims=True) + norm_eps)
    return center * scale


def layer_norm_back(values, upstream):
    center = values - jnp.mean(values, axis=-1, keepdims=True)
    scale = lax.rsqrt(jnp.mean(center * center, axis=-1, keepdims=True) + norm_eps)
    normed = center * scale
    first = jnp.mean(upstream, axis=-1, keepdims=True)
    second = jnp.mean(upstream * normed, axis=-1, keepdims=True)
    return scale * (upstream - first - normed * second)


def forward_mlp(inputs, w_first, w_second):
    hidden_pre = jnp.dot(inputs, w_first, preferred_element_type=jnp.float32)
    hidden = jax.nn.silu(hidden_pre).astype(jnp.bfloat16)
    linear = jnp.dot(hidden, w_second, preferred_element_type=jnp.float32)
    return (hidden_pre, hidden, linear, layer_norm(linear))


def backward_mlp(inputs, hidden_pre, hidden, linear, w_second, upstream):
    d_linear = layer_norm_back(linear, upstream).astype(jnp.bfloat16)
    grad_second = jnp.dot(hidden.T, d_linear, preferred_element_type=jnp.float32)
    d_hidden = jnp.dot(d_linear, w_second.T, preferred_element_type=jnp.float32)
    sigma = jax.nn.sigmoid(hidden_pre)
    d_pre = (d_hidden * sigma * (1.0 + hidden_pre * (1.0 - sigma))).astype(jnp.bfloat16)
    grad_first = jnp.dot(inputs.T, d_pre, preferred_element_type=jnp.float32)
    return (d_pre, grad_first, grad_second)


def on_device(
    node_state,
    edge_state,
    edge_source,
    contact_block,
    contact_host,
    contact_remote,
    w_edge_in,
    w_edge_out,
    w_node_in,
    w_node_out,
    w_contact_in,
    w_contact_out,
    node_cot,
    edge_cot,
):
    node_count = node_state.shape[0]
    latent = node_state.shape[1]
    groups = lax.axis_size("dom")
    blocks = node_count // BLOCK
    slot_count = groups * CAP
    row_count = contact_block.shape[0]
    extended = with_halo(node_state, (("dom", 0),), RIM)
    source_rows = extended[edge_source]
    target_rows = jnp.repeat(node_state, EPN, axis=0)
    edge_input = jnp.concatenate([edge_state, source_rows, target_rows], axis=1)
    e_pre, e_hidden, e_linear, e_normed = forward_mlp(edge_input, w_edge_in, w_edge_out)
    edge_out = (edge_state.astype(jnp.float32) + e_normed).astype(jnp.bfloat16)
    mesh_sum = (
        edge_out.astype(jnp.float32)
        .reshape(node_count, EPN, latent)
        .sum(axis=1)
        .astype(jnp.bfloat16)
    )
    host_part = contact_host[:, 0]
    peer_ids = lax.iota(jnp.int32, groups)
    to_peer = (host_part[:, None] == peer_ids[None, :]).astype(jnp.int32)
    slot_rank = jnp.sum((jnp.cumsum(to_peer, axis=0) - to_peer) * to_peer, axis=1)
    slot_index = host_part * CAP + slot_rank
    slot_hit = slot_index[None, :] == lax.iota(jnp.int32, slot_count)[:, None]
    wanted = jnp.sum(slot_hit.astype(jnp.int32) * (contact_remote[None, :] + 1), axis=1).reshape(
        groups, CAP
    )
    asked_ids = lax.all_to_all(wanted, "dom", split_axis=0, concat_axis=0, tiled=True).reshape(
        slot_count
    )
    asked_block = jnp.maximum(asked_ids - 1, 0)
    asked_live = asked_ids > 0
    block_rows = node_state.reshape(blocks, BLOCK * latent)
    reply_rows = jnp.where(
        asked_live[:, None], block_rows[asked_block], jnp.zeros((), jnp.bfloat16)
    )
    arrived = lax.all_to_all(
        reply_rows.reshape(groups, CAP, BLOCK * latent),
        "dom",
        split_axis=0,
        concat_axis=0,
        tiled=True,
    )
    remote_rows = arrived.reshape(slot_count, BLOCK * latent)[slot_index].reshape(
        row_count * BLOCK, latent
    )
    own_rows = block_rows[contact_block].reshape(row_count * BLOCK, latent)
    contact_input = jnp.concatenate([own_rows, remote_rows], axis=1)
    c_pre, c_hidden, c_linear, c_normed = forward_mlp(contact_input, w_contact_in, w_contact_out)
    message = c_normed.astype(jnp.bfloat16)
    block_hit = contact_block[None, :] == lax.iota(jnp.int32, blocks)[:, None]
    contact_sum = jnp.dot(
        block_hit.astype(jnp.bfloat16),
        message.reshape(row_count, BLOCK * latent),
        preferred_element_type=jnp.float32,
    )
    contact_sum = contact_sum.reshape(node_count, latent).astype(jnp.bfloat16)
    node_input = jnp.concatenate([node_state, mesh_sum, contact_sum], axis=1)
    n_pre, n_hidden, n_linear, n_normed = forward_mlp(node_input, w_node_in, w_node_out)
    node_out = (node_state.astype(jnp.float32) + n_normed).astype(jnp.bfloat16)
    d_node_pre, grad_node_in, grad_node_out = backward_mlp(
        node_input, n_pre, n_hidden, n_linear, w_node_out, node_cot.astype(jnp.float32)
    )
    dx_node = jnp.dot(d_node_pre, w_node_in.T, preferred_element_type=jnp.float32)
    grad_h = node_cot.astype(jnp.float32) + dx_node[:, :latent]
    d_mesh = dx_node[:, latent : 2 * latent].astype(jnp.bfloat16)
    d_contact = dx_node[:, 2 * latent :].astype(jnp.bfloat16)
    d_edge = edge_cot.astype(jnp.float32) + jnp.repeat(d_mesh.astype(jnp.float32), EPN, axis=0)
    d_edge_pre, grad_edge_in, grad_edge_out = backward_mlp(
        edge_input, e_pre, e_hidden, e_linear, w_edge_out, d_edge
    )
    dx_edge = jnp.dot(d_edge_pre, w_edge_in.T, preferred_element_type=jnp.float32)
    edge_grad = (d_edge + dx_edge[:, :latent]).astype(jnp.bfloat16)
    grad_h = grad_h + dx_edge[:, 2 * latent :].reshape(node_count, EPN, latent).sum(axis=1)
    spread = jax.ops.segment_sum(dx_edge[:, latent : 2 * latent], edge_source, node_count + 2 * RIM)
    rim_terms = jnp.concatenate([spread[:RIM], spread[node_count + RIM :]], axis=0)
    rim_back = with_halo(rim_terms.astype(jnp.bfloat16), (("dom", 0),), RIM).astype(rim_terms.dtype)
    middle = jnp.zeros((node_count - 2 * RIM, latent), jnp.float32)
    grad_h = (
        grad_h
        + spread[RIM : RIM + node_count]
        + jnp.concatenate([rim_back[:RIM], middle, rim_back[3 * RIM :]], axis=0)
    )
    d_message = (
        d_contact.reshape(blocks, BLOCK * latent)[contact_block]
        .reshape(row_count * BLOCK, latent)
        .astype(jnp.float32)
    )
    d_contact_pre, grad_contact_in, grad_contact_out = backward_mlp(
        contact_input, c_pre, c_hidden, c_linear, w_contact_out, d_message
    )
    d_own = jnp.dot(d_contact_pre, w_contact_in[:latent].T, preferred_element_type=jnp.float32)
    own_sum = jnp.dot(
        block_hit.astype(jnp.float32),
        d_own.reshape(row_count, BLOCK * latent),
        precision=lax.Precision.HIGHEST,
        preferred_element_type=jnp.float32,
    )
    grad_h = grad_h + own_sum.reshape(node_count, latent)
    slot_place = slot_hit.astype(jnp.bfloat16)
    d_remote = jnp.dot(
        d_contact_pre, w_contact_in[latent:].T, preferred_element_type=jnp.float32
    ).astype(jnp.bfloat16)
    outgoing = d_remote.reshape(row_count, BLOCK * latent)
    payload = jnp.dot(slot_place, outgoing, preferred_element_type=jnp.float32).astype(jnp.bfloat16)
    returned = lax.all_to_all(
        payload.reshape(groups, CAP, BLOCK * latent), "dom", split_axis=0, concat_axis=0, tiled=True
    )
    served = returned.reshape(slot_count, BLOCK * latent)
    owner_hit = (asked_block[None, :] == lax.iota(jnp.int32, blocks)[:, None]) & asked_live[None, :]
    remote_sum = jnp.dot(owner_hit.astype(jnp.bfloat16), served, preferred_element_type=jnp.float32)
    grad_h = grad_h + remote_sum.reshape(node_count, latent)
    node_grad = grad_h.astype(jnp.bfloat16)
    summed = lax.psum(
        (
            grad_edge_in,
            grad_edge_out,
            grad_node_in,
            grad_node_out,
            grad_contact_in,
            grad_contact_out,
        ),
        "dom",
    )
    return (
        node_out,
        edge_out,
        node_grad,
        edge_grad,
        summed[0],
        summed[1],
        summed[2],
        summed[3],
        summed[4],
        summed[5],
    )


def solution(mesh):
    in_specs = (
        P(("rep", "dom"), None),
        P(("rep", "dom"), None),
        P(("rep", "dom")),
        P(("rep", "dom")),
        P(("rep", "dom"), None),
        P(("rep", "dom")),
        P("rep", None),
        P("rep", None),
        P("rep", None),
        P("rep", None),
        P("rep", None),
        P("rep", None),
        P(("rep", "dom"), None),
        P(("rep", "dom"), None),
    )
    out_specs = (
        P(("rep", "dom"), None),
        P(("rep", "dom"), None),
        P(("rep", "dom"), None),
        P(("rep", "dom"), None),
        P("rep", None),
        P("rep", None),
        P("rep", None),
        P("rep", None),
        P("rep", None),
        P("rep", None),
    )
    return jax.shard_map(
        on_device, mesh=mesh, in_specs=in_specs, out_specs=out_specs, check_vma=False
    )
```

profile of v0, /device:TPU:0, one launch (start us, length us, event | category | flops | bytes accessed | tf_op | source)
XLA Modules:
  0.0 504.1 jit_solution(14457036049560026708)
XLA Ops:
  11.0 8.3 %all-to-all-start = ((s32[16,1,2]{2,1,0:T(1,128)}), s32[16,1,2]{2,1,0:T(1,128)S(1)}, u32[]{:S(2)}, u32[]{:S(2)}) async-start(s32[16,1,2]{2,1,0:T(1,128)} %bitcast.1), calls=%async_computation | async-start | bytes 16384 | tf_op jit(solution)/shard_map/all_to_all | solution.py:103
  20.9 5.6 %all-to-all-done = s32[16,1,2]{2,1,0:T(1,128)S(1)} async-done(((s32[16,1,2]{2,1,0:T(1,128)}), s32[16,1,2]{2,1,0:T(1,128)S(1)}, u32[]{:S(2)}, u32[]{:S(2)}) %all-to-all-start) | async-done | bytes 160 | tf_op jit(solution)/shard_map/all_to_all | solution.py:103
  26.6 4.3 gather_fusion.2
  30.9 5.1 %gather.20 = bf16[16,2,49152]{2,1,0:T(2,128)(2,1)} reshape(bf16[32,49152]{1,0:T(8,128)(2,1)} %gather_fusion.2) | data formatting | bytes 6291456 | tf_op jit(solution)/shard_map/gather | solution.py:110
  36.2 6.1 %broadcast_select_fusion = bf16[16,2,49152]{2,1,0:T(2,128)(2,1)} fusion(bf16[16,2,49152]{2,1,0:T(2,128)(2,1)} %gather.20, pred[16,2]{1,0:T(8,128)(4,1)S(1)} %copy.39), kind=kLoop, calls=%fused_computation.8 | loop fusion | flops 1572864 | bytes 6291488 | tf_op jit(solution)/shard_map/jit(_where)/select_n | solution.py:109
  42.4 4.6 all-to-all-start.1
  47.0 3.8 collective-permute-start
  58.7 3.9 gather_fusion
  64.6 4.4 multiply_convert_fusion.2
  75.1 32.3 %all-to-all-done.1 = bf16[16,2,49152]{2,1,0:T(2,128)(2,1)} async-done(((bf16[16,2,49152]{2,1,0:T(2,128)(2,1)}), bf16[16,2,49152]{2,1,0:T(2,128)(2,1)}, u32[]{:S(2)}, u32[]{:S(2)}) %all-to-all-start.1) | async-done | bytes 3145760 | tf_op jit(solution)/shard_map/all_to_all | solution.py:112
  107.3 4.9 reshape.210
  112.2 4.3 gather_fusion.3
  119.6 2.8 multiply_convert_fusion.4
  159.3 2.8 reshape.213
  174.3 5.1 %reshape.219 = bf16[16,2,49152]{2,1,0:T(2,128)(2,1)} reshape(bf16[32,49152]{1,0:T(8,128)(2,1)} %convolution_convert_fusion) | data formatting | bytes 6291456 | tf_op jit(solution)/shard_map/reshape | solution.py:182
  179.5 30.8 %all-to-all-start.2 = ((bf16[16,2,49152]{2,1,0:T(2,128)(2,1)}), bf16[16,2,49152]{2,1,0:T(2,128)(2,1)}, u32[]{:S(2)}, u32[]{:S(2)}) async-start(bf16[16,2,49152]{2,1,0:T(2,128)(2,1)} %reshape.219), calls=%async_computation.2 | async-start | bytes 6291456 | tf_op jit(solution)/shard_map/all_to_all | solution.py:181
  211.6 3.6 fusion.50
  215.2 7.4 %scatter_custom_fusion = f32[384,384]{1,0:T(8,128)S(1)} fusion(s32[1024]{0:T(1024)S(1)} %copy-done.39, f32[1024,1152]{1,0:T(8,128)} %fusion.50, f32[]{:T(128)} %constant.25.clone.1), kind=kCustom, calls=%fused_computation.11 | custom fusion | flops 393216 | bytes 2163200 | tf_op jit(solution)/shard_map/scatter-add | solution.py:150
  223.5 3.9 collective-permute-start.2
  233.5 3.7 fusion
  242.8 67.8 %all-to-all-done.2 = bf16[16,2,49152]{2,1,0:T(2,128)(2,1)} async-done(((bf16[16,2,49152]{2,1,0:T(2,128)(2,1)}), bf16[16,2,49152]{2,1,0:T(2,128)(2,1)}, u32[]{:S(2)}, u32[]{:S(2)}) %all-to-all-start.2) | async-done | bytes 3145760 | tf_op jit(solution)/shard_map/all_to_all | solution.py:181
  310.6 4.7 reshape.220
  320.0 169.1 %all-reduce.3.cloned.1.call-done = (f32[1152,384]{1,0:T(8,128)}, f32[384,384]{1,0:T(8,128)}, f32[1152,384]{1,0:T(8,128)}, f32[384,384]{1,0:T(8,128)}, f32[768,384]{1,0:T(8,128)}, /*index=5*/f32[384,384]{1,0:T(8,128)}) async-done(((f32[1152,384]{1,0:T(8,128)}, f32[384,384]{1,0:T(8,128)}, f32[1152,384]{1,0:T(8,128)}, f32[384,384]{1,0:T(8,128)}, f32[768,384]{1,0:T(8,128)}, /*index=5*/f32[384,384]{1,0:T(8,128)}), ...) | async-done | bytes 6488080 | tf_op jit(solution)/shard_map/psum | solution.py:189
  489.1 2.9 copy.52
  (205 shorter events, 96.8 us)
Async XLA Ops:
  7.2 57.5 %copy-start = (bf16[1152,384]{1,0:T(8,128)(2,1)S(1)}, bf16[1152,384]{1,0:T(8,128)(2,1)}, u32[]{:S(2)}) copy-start(bf16[1152,384]{1,0:T(8,128)(2,1)} %param.20) | copy-start | bytes 2654212
  11.0 15.5 %all-to-all-start = ((s32[16,1,2]{2,1,0:T(1,128)}), s32[16,1,2]{2,1,0:T(1,128)S(1)}, u32[]{:S(2)}, u32[]{:S(2)}) async-start(s32[16,1,2]{2,1,0:T(1,128)} %bitcast.1), calls=%async_computation | async-start | bytes 16384 | tf_op jit(solution)/shard_map/all_to_all | solution.py:103
  42.4 4.6 copy-start.4
  42.4 65.0 %all-to-all-start.1 = ((bf16[16,2,49152]{2,1,0:T(2,128)(2,1)}), bf16[16,2,49152]{2,1,0:T(2,128)(2,1)}, u32[]{:S(2)}, u32[]{:S(2)}) async-start(bf16[16,2,49152]{2,1,0:T(2,128)(2,1)} %broadcast_select_fusion), calls=%async_computation.1 | async-start | bytes 6291456 | tf_op jit(solution)/shard_map/all_to_all | solution.py:112
  47.0 8.3 %copy-start.40 = (s32[4,1]{0,1:T(1,128)S(1)}, s32[4,1]{0,1:T(1,128)}, u32[]{:S(2)}) copy-start(s32[4,1]{0,1:T(1,128)} %param.18) | copy-start | bytes 52
  47.0 8.4 %copy-start.9 = (bf16[1024,384]{1,0:T(8,128)(2,1)S(1)}, bf16[1024,384]{1,0:T(8,128)(2,1)}, u32[]{:S(2)}) copy-start(bf16[1024,384]{1,0:T(8,128)(2,1)} %param.15) | copy-start | bytes 2359300
  47.0 11.4 %collective-permute-start = (bf16[64,384]{1,0:T(8,128)(2,1)S(1)}, bf16[64,384]{1,0:T(8,128)(2,1)S(1)}, u32[]{:S(2)}, u32[]{:S(2)}) collective-permute-start(bf16[64,384]{1,0:T(8,128)(2,1)S(1)} %get-tuple-element.30), channel_id=1, source_target_pairs={{0,2},{2,4},{4,6},{6,8},{8,10},{10,12},{12,14},{14,16},{16,18},{18... | collective-permute-start | bytes 147464 | tf_op jit(solution)/shard_map/ppermute | solution.py:22
  50.8 7.9 %collective-permute-start.1 = (bf16[64,384]{1,0:T(8,128)(2,1)S(1)}, bf16[64,384]{1,0:T(8,128)(2,1)S(1)}, u32[]{:S(2)}, u32[]{:S(2)}) collective-permute-start(bf16[64,384]{1,0:T(8,128)(2,1)S(1)} %get-tuple-element.31), channel_id=1, source_target_pairs={{2,0},{4,2},{6,4},{8,6},{10,8},{12,10},{14,12},{16,14},{18,16},{20... | collective-permute-start | bytes 147464 | tf_op jit(solution)/shard_map/ppermute | solution.py:23
  64.6 4.4 copy-start.33
  112.2 6.3 %copy-start.14 = (bf16[512,768]{1,0:T(8,128)(2,1)S(1)}, bf16[512,768]{1,0:T(8,128)(2,1)}, u32[]{:S(2)}) copy-start(bf16[512,768]{1,0:T(8,128)(2,1)} %constant_dynamic-update-slice_fusion.4) | copy-start | bytes 2359300
  119.6 3.6 copy-start.31
  123.8 4.7 copy-start.41
  179.5 30.8 %copy-start.37 = (bf16[256,384]{1,0:T(8,128)(2,1)S(1)}, bf16[256,384]{1,0:T(8,128)(2,1)}, u32[]{:S(2)}) copy-start(bf16[256,384]{1,0:T(8,128)(2,1)} %copy-done.36) | copy-start | bytes 589828
  179.5 30.8 %copy-start.44 = (f32[256,384]{1,0:T(8,128)S(1)}, f32[256,384]{1,0:T(8,128)}, u32[]{:S(2)}) copy-start(f32[256,384]{1,0:T(8,128)} %copy-done.43) | copy-start | bytes 1179652
  179.5 131.1 %all-to-all-start.2 = ((bf16[16,2,49152]{2,1,0:T(2,128)(2,1)}), bf16[16,2,49152]{2,1,0:T(2,128)(2,1)}, u32[]{:S(2)}, u32[]{:S(2)}) async-start(bf16[16,2,49152]{2,1,0:T(2,128)(2,1)} %reshape.219), calls=%async_computation.2 | async-start | bytes 6291456 | tf_op jit(solution)/shard_map/all_to_all | solution.py:181
  210.2 278.9 %all-reduce.3.cloned.1.call-start = ((), (), s32[]{:S(2)}) async-start(), calls=%async_computation.3 | async-start | bytes 12976128 | tf_op jit(solution)/shard_map/psum | solution.py:189
  223.5 10.0 %copy-start.2 = (f32[1024,384]{1,0:T(8,128)S(1)}, f32[1024,384]{1,0:T(8,128)}, u32[]{:S(2)}) copy-start(f32[1024,384]{1,0:T(8,128)} %reshape.213) | copy-start | bytes 4718596
  223.5 17.8 %collective-permute-start.2 = (bf16[64,384]{1,0:T(8,128)(2,1)S(1)}, bf16[64,384]{1,0:T(8,128)(2,1)S(1)}, u32[]{:S(2)}, u32[]{:S(2)}) collective-permute-start(bf16[64,384]{1,0:T(8,128)(2,1)S(1)} %get-tuple-element.26), channel_id=1, source_target_pairs={{0,2},{2,4},{4,6},{6,8},{8,10},{10,12},{12,14},{14,16},{16,18},{18... | collective-permute-start | bytes 147464 | tf_op jit(solution)/shard_map/ppermute | solution.py:22
  227.4 14.5 %collective-permute-start.3 = (bf16[64,384]{1,0:T(8,128)(2,1)S(1)}, bf16[64,384]{1,0:T(8,128)(2,1)}, u32[]{:S(2)}, u32[]{:S(2)}) collective-permute-start(bf16[64,384]{1,0:T(8,128)(2,1)S(1)} %get-tuple-element.27), channel_id=1, source_target_pairs={{2,0},{4,2},{6,4},{8,6},{10,8},{12,10},{14,12},{16,14},{18,16},{20... | collective-permute-start | bytes 147464 | tf_op jit(solution)/shard_map/ppermute | solution.py:23
  233.5 3.7 copy-start.8
  315.3 2.9 copy-start.6
  315.3 2.9 copy-start.13
  489.1 3.0 copy-start.29
  489.1 3.8 copy-start.11
  (31 other events, 54.2 us)
Sparse Core Ops, SparseCore 0:
  218.1 270.9 all-reduce.2
where the time goes:
time: 511 us; the launch traced here: 504 us
  waiting for transfers between devices  275 us (54%)
  local copies, waits for them, and re-layouts  82 us (16%)
  starting transfers between devices  54.5 us (11%)
  matrix products  38.9 us (8%)
  other arithmetic  38.6 us (8%)
  between operations  15 us (3%)
    psum x1, waiting for transfers between devices, on_device(): lax.psum((grad_edge_in, grad_edge_out, grad_node_in, grad_node_out, grad_...  169 us
    all_to_all x1, waiting for transfers between devices, on_device(): lax.all_to_all(payload.reshape(groups, CAP, BLOCK * latent), 'dom', split...  67.8 us
    all_to_all x1, waiting for transfers between devices, on_device(): lax.all_to_all(reply_rows.reshape(groups, CAP, BLOCK * latent), 'dom', sp...  32.3 us
    all_to_all x1, starting transfers between devices, on_device(): lax.all_to_all(payload.reshape(groups, CAP, BLOCK * latent), 'dom', split...  30.8 us
    unnamed x103, local copies, waits for them, and re-layouts  15.9 us
  transfers between devices with their start and end apart: 8, of which 5 were waited for; matrix products, arithmetic and copies ran while one was open for 12% of the time, Pallas kernels for 0%

commit v1 on v0

v1 whole, which is shorter than its diff:
```python
import functools

import jax
import jax.numpy as jnp
from jax import lax
from jax.experimental import pallas as pl
from jax.experimental.pallas import tpu as pltpu
from jax.sharding import PartitionSpec as P

BLOCK = 128
EPN = 4
RIM = 64
EDGE_ROWS = 512
LABEL = 16
TILE = 32
STREAMS = 3
VMEM_LIMIT = 50 * 2**20
BF16 = jnp.bfloat16
F32 = jnp.float32


norm_eps = 1e-05


def exchange_orders(groups):
    bits = groups.bit_length() - 1
    low = list(range(bits - 1))
    turns = [r % max(1, len(low)) for r in range(STREAMS)]
    return [low[r:] + low[:r] + [bits - 1] for r in turns]


def return_orders(orders):
    heads = [(o[0], o[-2]) if s % 2 == 0 else (o[-2], o[0]) for s, o in enumerate(orders)]
    return [[*head, *o[1:-2], o[-1]] for head, o in zip(heads, orders)]


def places(order):
    bits = len(order)
    return [
        sum(((q >> (bits - 1 - i)) & 1) << b for i, b in enumerate(order)) for q in range(1 << bits)
    ]


def place_of(order, offset):
    bits = len(order)
    return sum(((offset >> b) & 1) << (bits - 1 - i) for i, b in enumerate(order))


def swap(value, bit):
    peers = lax.axis_size("dom")
    return lax.ppermute(value, "dom", [(i, i ^ (1 << bit)) for i in range(peers)])


def joined(values):
    return list(lax.optimization_barrier(tuple(values)))


def gather_step(held, orders, step):
    return [swap(value, order[-1 - step]) for value, order in zip(held, orders)]


def both(held, arrived):
    return [jnp.concatenate(pair, axis=0) for pair in zip(held, arrived)]


def added(halves, arrived):
    totals = [kept.astype(F32) + value.astype(F32) for (kept, _), value in zip(halves, arrived)]
    cut = totals[0].shape[0] // 2
    return [(total[:cut], total[cut:].astype(BF16)) for total in totals]


def dot(a, b):
    return jnp.dot(a, b, preferred_element_type=F32)


def dot_t(a, b):
    return lax.dot_general(a, b, (((1,), (1,)), ((), ())), preferred_element_type=F32)


def t_dot(a, b):
    return lax.dot_general(a, b, (((0,), (0,)), ((), ())), preferred_element_type=F32)


def sigmoid(z):
    return 0.5 * jnp.tanh(0.5 * z) + 0.5


def normed(values):
    center = values - jnp.mean(values, axis=-1, keepdims=True)
    scale = lax.rsqrt(jnp.mean(center * center, axis=-1, keepdims=True) + norm_eps)
    return center * scale, scale


def norm_back(values, upstream):
    unit, scale = normed(values)
    first = jnp.mean(upstream, axis=-1, keepdims=True)
    second = jnp.mean(upstream * unit, axis=-1, keepdims=True)
    return scale * (upstream - first - unit * second)


def tiles(rows):
    return [slice(i, i + TILE) for i in range(0, rows, TILE)]


def silu_tiles(z_ref, a_ref):
    for t in tiles(z_ref.shape[0]):
        z = z_ref[t]
        a_ref[t] = (z * sigmoid(z)).astype(BF16)


def silu_and_slope(z):
    s = sigmoid(z)
    a = z * s
    return a.astype(BF16), s + a * (1.0 - s)


def one_hot(condition):
    return jnp.where(condition, 1.0, 0.0).astype(BF16)


def iota(shape, axis):
    return lax.broadcasted_iota(jnp.int32, shape, axis)


def repeat_matrix(rows):
    shape = (rows, rows // EPN)
    return one_hot((iota(shape, 0) >> 2) == iota(shape, 1))


def sum_matrix(rows):
    shape = (rows // EPN, rows)
    return one_hot((iota(shape, 1) >> 2) == iota(shape, 0))


def parts_of(first, second, groups):
    shares = first // groups, second // groups
    if all(share % 8 == 0 and share * groups == size for share, size in zip(shares, (first, second))):
        return [(0, shares[0]), (first, shares[1])]
    return [(0, -(-(first + second) // (groups * 16)) * 16)]


def chunk_rows(parts):
    return -(-sum(rows for _, rows in parts) // 16) * 16


def total_rows(parts, groups):
    return max(base + rows * groups for base, rows in parts)


def starts_of(parts, device):
    return [pl.multiple_of(base + device * rows, 8) for base, rows in parts]


def deal(total_ref, kept_ref, sent_ref, order, parts, me):
    half, width = kept_ref.shape[0], kept_ref.shape[2]
    rows = kept_ref.shape[1] // STREAMS
    spare = rows - sum(count for _, count in parts)
    for q, offset in enumerate(places(order)):
        starts = starts_of(parts, me ^ offset)
        for s in range(STREAMS):
            columns = slice(s * width, (s + 1) * width)
            values = [
                total_ref[pl.ds(start, count), columns] for start, (_, count) in zip(starts, parts)
            ]
            if spare:
                values.append(jnp.zeros((spare, width), F32))
            value = jnp.concatenate(values, axis=0) if len(values) > 1 else values[0]
            if q < half:
                kept_ref[q, s * rows : (s + 1) * rows] = value.astype(kept_ref.dtype)
            else:
                sent_ref[q - half, s * rows : (s + 1) * rows] = value.astype(BF16)


def edge_forward(src_ref, before_ref, node_ref, after_ref, edge_ref, w_in_ref, w_out_ref,
                 out_ref, sum_ref, z_ref, y_ref, ext_ref, x_ref, a_ref):
    step = pl.program_id(0)
    count, latent = node_ref.shape
    rows = edge_ref.shape[0]
    targets = rows // EPN

    @pl.when(step == 0)
    def _():
        ext_ref[:RIM] = before_ref[...]
        ext_ref[RIM : RIM + count] = node_ref[...]
        ext_ref[RIM + count :] = after_ref[...]

    hit = one_hot(iota((count + 2 * RIM, rows), 0) == src_ref[0])
    own = node_ref[pl.ds(pl.multiple_of(step * targets, targets), targets), :]
    x_ref[:, :latent] = edge_ref[...]
    x_ref[:, latent : 2 * latent] = t_dot(hit, ext_ref[...]).astype(BF16)
    x_ref[:, 2 * latent :] = dot(repeat_matrix(rows), own).astype(BF16)
    z_ref[...] = dot(x_ref[...], w_in_ref[...])
    silu_tiles(z_ref, a_ref)
    y_ref[...] = dot(a_ref[...], w_out_ref[...])
    for t in tiles(rows):
        out_ref[t] = (edge_ref[t].astype(F32) + normed(y_ref[t])[0]).astype(BF16)
    sum_ref[...] = dot(sum_matrix(rows), out_ref[...]).astype(BF16)


def edge_backward(orders, parts, me_ref, src_ref, before_ref, node_ref, after_ref, edge_ref, z_ref, y_ref,
                  cot_ref, mesh_ref, partial_ref, w_in_ref, w_out_ref,
                  grad_ref, h_ref, low_ref, high_ref, kept_ref, sent_ref,
                  ext_ref, by_source_ref, by_target_ref, total_ref):
    step = pl.program_id(0)
    count, latent = node_ref.shape
    rows = edge_ref.shape[0]
    targets = rows // EPN

    @pl.when(step == 0)
    def _():
        by_source_ref[...] = jnp.zeros_like(by_source_ref)
        total_ref[...] = jnp.zeros_like(total_ref)

    upstream = cot_ref[...].astype(F32) + dot(repeat_matrix(rows), mesh_ref[...])
    d_y = norm_back(y_ref[...], upstream).astype(BF16)
    a, slope = silu_and_slope(z_ref[...])
    total_ref[3 * latent : 4 * latent] += t_dot(a, d_y)
    d_z = (dot_t(d_y, w_out_ref[...]) * slope).astype(BF16)
    total_ref[:latent] += t_dot(edge_ref[...], d_z)
    grad_ref[...] = (upstream + dot_t(d_z, w_in_ref[:latent])).astype(BF16)
    hit = one_hot(iota((count + 2 * RIM, rows), 0) == src_ref[0])
    by_source_ref[...] += dot(hit, d_z)
    place = pl.ds(pl.multiple_of(step * targets, targets), targets)
    by_target_ref[place, :] = dot(sum_matrix(rows), d_z)

    @pl.when(step == pl.num_programs(0) - 1)
    def _():
        ext_ref[:RIM] = before_ref[...]
        ext_ref[RIM : RIM + count] = node_ref[...]
        ext_ref[RIM + count :] = after_ref[...]
        by_source = by_source_ref[...].astype(BF16)
        total_ref[latent : 2 * latent] = t_dot(ext_ref[...], by_source)
        back = dot_t(by_source, w_in_ref[latent : 2 * latent])
        low_ref[...] = back[:RIM].astype(BF16)
        high_ref[...] = back[RIM + count :].astype(BF16)
        by_target = by_target_ref[...].astype(BF16)
        total_ref[2 * latent : 3 * latent] = t_dot(node_ref[...], by_target)
        h_ref[...] = (
            partial_ref[...] + back[RIM : RIM + count] + dot_t(by_target, w_in_ref[2 * latent :])
        )
        deal(total_ref, kept_ref, sent_ref, orders[0], parts, me_ref[0])


def node_and_contact(orders, node_parts, contact_parts, row_count, me_ref, host_ref, remote_ref, block_ref, *refs):
    count = 2 * STREAMS * row_count
    far = refs[:count]
    (node_ref, mesh_ref, cot_ref, nw_in_ref, nw_out_ref, cw_in_ref, cw_out_ref,
     out_ref, h_ref, d_mesh_ref, nkept_ref, nsent_ref, ckept_ref, csent_ref,
     *slab_refs) = refs[count : count + 16]
    (x_ref, z_ref, y_ref, sum_ref, total_ref, x_node_ref, d_contact_ref, g_ref,
     nw_in, nw_out, nkept, nsent, sems) = refs[count + 16 :]
    loads = [
        pltpu.make_async_copy(nw_in_ref, nw_in, sems.at[0]),
        pltpu.make_async_copy(nw_out_ref, nw_out, sems.at[1]),
    ]
    stores = [
        pltpu.make_async_copy(nkept, nkept_ref, sems.at[2]),
        pltpu.make_async_copy(nsent, nsent_ref, sems.at[3]),
    ]
    for copy in loads:
        copy.start()
    latent = node_ref.shape[1]
    width = latent // STREAMS
    me = me_ref[0]
    chunk = min(4, row_count)
    blocks = node_ref.shape[0] // BLOCK
    half = nkept_ref.shape[0]

    def own_rows(row):
        return pl.ds(pl.multiple_of(block_ref[row] * BLOCK, BLOCK), BLOCK)

    sum_ref[...] = jnp.zeros_like(sum_ref)
    for row in range(row_count):
        rows = slice(row * BLOCK, (row + 1) * BLOCK)
        x_ref[rows, :latent] = node_ref[own_rows(row), :]
        for s, order in enumerate(orders):
            columns = slice(latent + s * width, latent + (s + 1) * width)
            near, away = far[2 * (row * STREAMS + s)], far[2 * (row * STREAMS + s) + 1]
            is_near = place_of(order, host_ref[row] ^ me) < half

            @pl.when(is_near)
            def _():
                x_ref[rows, columns] = near[0]

            @pl.when(jnp.logical_not(is_near))
            def _():
                x_ref[rows, columns] = away[0]
    for first in range(0, row_count, chunk):
        rows = slice(first * BLOCK, (first + chunk) * BLOCK)
        z = dot(x_ref[rows], cw_in_ref[...])
        y = dot(silu_and_slope(z)[0], cw_out_ref[...])
        z_ref[rows] = z
        y_ref[rows] = y
        message = normed(y)[0].astype(BF16).astype(F32)
        for row in range(first, first + chunk):
            part = message[(row - first) * BLOCK : (row - first + 1) * BLOCK]
            sum_ref[own_rows(row), :] += part

    for copy in loads:
        copy.wait()
    node = node_ref[...]
    x_node_ref[:, :latent] = node
    x_node_ref[:, latent : 2 * latent] = mesh_ref[...]
    x_node_ref[:, 2 * latent :] = sum_ref[...].astype(BF16)
    z = dot(x_node_ref[...], nw_in[...])
    a, slope = silu_and_slope(z)
    y = dot(a, nw_out[...])
    out_ref[...] = (node.astype(F32) + normed(y)[0]).astype(BF16)
    upstream = cot_ref[...].astype(F32)
    d_y = norm_back(y, upstream).astype(BF16)
    total_ref[3 * latent : 4 * latent] = t_dot(a, d_y)
    d_z = (dot_t(d_y, nw_out[...]) * slope).astype(BF16)
    total_ref[: 3 * latent] = t_dot(x_node_ref[...], d_z)
    if total_ref.shape[0] > 4 * latent:
        total_ref[4 * latent :] = jnp.zeros((total_ref.shape[0] - 4 * latent, latent), F32)
    d_x = dot_t(d_z, nw_in[...])
    h_ref[...] = upstream + d_x[:, :latent]
    d_mesh_ref[...] = d_x[:, latent : 2 * latent].astype(BF16)
    d_contact_ref[...] = d_x[:, 2 * latent :].astype(BF16).astype(F32)
    deal(total_ref, nkept, nsent, orders[1], node_parts, me)
    for copy in stores:
        copy.start()

    total_ref[: 3 * latent] = jnp.zeros((3 * latent, latent), F32)
    if total_ref.shape[0] > 3 * latent:
        total_ref[3 * latent :] = jnp.zeros((total_ref.shape[0] - 3 * latent, latent), F32)
    for first in range(0, row_count, chunk):
        rows = slice(first * BLOCK, (first + chunk) * BLOCK)
        for row in range(first, first + chunk):
            part = slice((row - first) * BLOCK, (row - first + 1) * BLOCK)
            g_ref[part, :latent] = d_contact_ref[own_rows(row), :]
        d_y = norm_back(y_ref[rows], g_ref[:, :latent]).astype(BF16)
        a, slope = silu_and_slope(z_ref[rows])
        total_ref[2 * latent : 3 * latent] += t_dot(a, d_y)
        d_z = (dot_t(d_y, cw_out_ref[...]) * slope).astype(BF16)
        total_ref[: 2 * latent] += t_dot(x_ref[rows], d_z)
        g_ref[...] = dot_t(d_z, cw_in_ref[...])
        for row in range(first, first + chunk):
            part = slice((row - first) * BLOCK, (row - first + 1) * BLOCK)
            h_ref[own_rows(row), :] += g_ref[part, :latent]
            label = (host_ref[row] * blocks + remote_ref[row]).astype(F32)
            cut = latent
            for ref in slab_refs:
                columns = ref.shape[2]
                ref[row, :BLOCK] = g_ref[part, cut : cut + columns].astype(BF16)
                ref[row, BLOCK:] = jnp.full((LABEL, columns), label, F32).astype(BF16)
                cut += columns
    deal(total_ref, ckept_ref, csent_ref, orders[2], contact_parts, me)
    for copy in stores:
        copy.wait()


def pick_blocks(orders, blocks, row_count, me_ref, *refs):
    named, slabs, outs, sems = refs[:3], refs[3:6], refs[6:9], refs[9]
    copies = []
    for s, order in enumerate(orders):
        for i in range(row_count):
            spot = place_of(order, named[s][i] ^ me_ref[0])
            spot = jnp.where(spot < slabs[s].shape[0] // blocks, spot, 0)
            block = spot * blocks + named[s][row_count + i]
            copies.append(
                pltpu.make_async_copy(slabs[s].at[block], outs[s].at[i], sems.at[len(copies)])
            )
            copies[-1].start()
    for copy in copies:
        copy.wait()


def add_to_places(orders, blocks, half, me_ref, host_ref, remote_ref, *refs):
    own, arrived, outs = refs[:2], refs[2:4], refs[4:]
    row_count = own[0].shape[0]
    width = outs[0].shape[2]
    views = [(0, slice(0, width)), (0, slice(width, 2 * width)), (1, slice(0, width))]
    me = me_ref[0]
    for s, order in enumerate(orders):
        bits = len(order)
        out = outs[s]
        slots = out.shape[0]
        first = half * slots
        array, columns = views[s]
        marks = [arrived[array][i, BLOCK:, columns].astype(F32)[:1] for i in range(row_count)]

        def step(slot, carry):
            place = (first + slot) // blocks
            offset = sum(((place >> (bits - 1 - i)) & 1) << b for i, b in enumerate(order))
            label = ((me ^ offset) * blocks + slot % blocks).astype(F32)
            value = jnp.zeros((BLOCK, out.shape[2]), F32)
            for i, mark in enumerate(marks):
                hit = jnp.where(mark == label, 1.0, 0.0)
                value = value + arrived[array][i, :BLOCK, columns].astype(F32) * hit
            out[slot] = value.astype(out.dtype)
            return carry

        lax.fori_loop(0, slots, step, 0)
        for i in range(row_count):
            spot = place_of(order, host_ref[i] ^ me) * blocks + remote_ref[i] - first

            @pl.when(jnp.logical_and(spot >= 0, spot < slots))
            def _():
                total = out[spot].astype(F32) + own[array][i, :BLOCK, columns].astype(F32)
                out[spot] = total.astype(out.dtype)


def unpack(orders, parts, half_index, me_ref, *refs):
    halves, rest = refs[:STREAMS], refs[STREAMS:]
    outs, rows_refs, sems = rest[-3 * STREAMS - 1 : -STREAMS - 1], rest[-STREAMS - 1 : -1], rest[-1]
    copies = []
    for s, order in enumerate(orders):
        count, width = halves[s].shape[0], halves[s].shape[2]
        rows = halves[s].shape[1] // STREAMS
        for q in range(count):
            for c in range(STREAMS):
                value = halves[s][q, c * rows : (c + 1) * rows].astype(F32)
                rows_refs[s][q, :, c * width : (c + 1) * width] = value
            device = me_ref[0] ^ places(order)[half_index * count + q]
            done = 0
            for p, (_, share) in enumerate(parts[s]):
                start = pl.multiple_of(device * share, 8)
                copy = pltpu.make_async_copy(
                    rows_refs[s].at[q, pl.ds(done, share)],
                    outs[2 * s + p].at[pl.ds(start, share)],
                    sems.at[len(copies)],
                )
                copy.start()
                copies.append(copy)
                done += share
    for copy in copies:
        copy.wait()


def unpack_whole(order, me_ref, near_ref, far_ref, first_ref, second_ref, total_ref):
    half, width = near_ref.shape[0], near_ref.shape[2]
    rows = near_ref.shape[1] // STREAMS
    for q, offset in enumerate(places(order)):
        ref, place = (near_ref, q) if q < half else (far_ref, q - half)
        start = pl.multiple_of((me_ref[0] ^ offset) * rows, 8)
        for s in range(STREAMS):
            value = ref[place, s * rows : (s + 1) * rows].astype(F32)
            total_ref[pl.ds(start, rows), s * width : (s + 1) * width] = value
    cut = first_ref.shape[0]
    first_ref[...] = total_ref[:cut]
    second_ref[...] = total_ref[cut : cut + second_ref.shape[0]]


def params(axes=0):
    return pltpu.CompilerParams(
        vmem_limit_bytes=VMEM_LIMIT,
        dimension_semantics=("arbitrary",) * axes if axes else None,
    )


def cost(flops, moved):
    return pl.CostEstimate(flops=flops, bytes_accessed=moved, transcendentals=0)


def whole(array_shape):
    return pl.BlockSpec(array_shape, lambda *_: (0,) * len(array_shape))


def struct(shape, dtype):
    return jax.ShapeDtypeStruct(shape, dtype)


def on_device(
    node_state,
    edge_state,
    edge_source,
    contact_block,
    contact_host,
    contact_remote,
    w_edge_in,
    w_edge_out,
    w_node_in,
    w_node_out,
    w_contact_in,
    w_contact_out,
    node_cot,
    edge_cot,
):
    node_count, latent = node_state.shape
    edge_count = edge_state.shape[0]
    groups = lax.axis_size("dom")
    blocks = node_count // BLOCK
    row_count = contact_block.shape[0]
    width = latent // STREAMS
    orders = exchange_orders(groups)
    me = lax.axis_index("dom").astype(jnp.int32).reshape(1)
    host = contact_host[:, 0]
    smem = pl.BlockSpec(memory_space=pltpu.SMEM)
    anywhere = pl.BlockSpec(memory_space=pl.ANY)

    up = [(i, i + 1) for i in range(groups - 1)]
    down = [(j, i) for i, j in up]
    before = lax.ppermute(node_state[node_count - RIM :], "dom", up)
    after = lax.ppermute(node_state[:RIM], "dom", down)
    last = len(orders[0]) - 1
    far_bit = orders[0][-1]
    half = groups // 2
    rows_named = jnp.concatenate([host, contact_remote])
    arrived, before, after, *named = joined(
        [swap(node_state, far_bit), before, after]
        + [swap(rows_named, order[0]) for order in orders]
    )
    pair = jnp.stack([node_state, arrived])
    slabs = [pair[:, :, s * width : (s + 1) * width] for s in range(STREAMS)]
    for step in range(1, last):
        if step == last - 1:
            *slabs, before = joined([*slabs, before])
        arrived = gather_step(slabs, orders, step)
        if step < last - 1:
            slabs = both(slabs, joined(arrived))

    steps = edge_count // EDGE_ROWS
    sources = edge_source.reshape(steps, 1, EDGE_ROWS)
    edge_block = pl.BlockSpec((EDGE_ROWS, latent), lambda i: (i, 0))
    node_block = pl.BlockSpec((EDGE_ROWS // EPN, latent), lambda i: (i, 0))
    source_block = pl.BlockSpec((1, 1, EDGE_ROWS), lambda i: (i, 0, 0))
    rim_block = whole((RIM, latent))
    extended_rows = node_count + 2 * RIM
    edge_out, mesh_sum, e_pre, e_linear = pl.pallas_call(
        edge_forward,
        grid=(steps,),
        in_specs=[
            source_block,
            rim_block,
            whole(node_state.shape),
            rim_block,
            edge_block,
            whole(w_edge_in.shape),
            whole(w_edge_out.shape),
        ],
        out_specs=[edge_block, node_block, edge_block, edge_block],
        out_shape=[
            struct((edge_count, latent), BF16),
            struct((node_count, latent), BF16),
            struct((edge_count, latent), F32),
            struct((edge_count, latent), F32),
        ],
        scratch_shapes=[
            pltpu.VMEM((extended_rows, latent), BF16),
            pltpu.VMEM((EDGE_ROWS, 3 * latent), BF16),
            pltpu.VMEM((EDGE_ROWS, latent), BF16),
        ],
        compiler_params=params(1),
        cost_estimate=cost(2 * edge_count * latent * latent * 6, edge_count * latent * 16),
        name="edge_forward",
    )(sources, before, node_state, after, edge_state, w_edge_in, w_edge_out)

    *arrived, mesh_sum = joined([*arrived, mesh_sum])
    slabs = [
        slab.reshape(half * blocks, BLOCK, width) for slab in both(slabs, arrived)
    ]
    picked = pl.pallas_call(
        functools.partial(pick_blocks, orders, blocks, row_count),
        in_specs=[smem] * (1 + STREAMS) + [anywhere] * STREAMS,
        out_specs=[anywhere] * STREAMS,
        out_shape=[struct((row_count, BLOCK, width), BF16)] * STREAMS,
        scratch_shapes=[pltpu.SemaphoreType.DMA((STREAMS * row_count,))],
        compiler_params=params(),
        cost_estimate=cost(0, 2**20),
        name="pick_blocks",
    )(me, *named, *slabs)
    answered = [swap(value, order[0]) for value, order in zip(picked, orders)]

    def near_spec(row, s):
        def index(i, me_ref, host_ref, remote_ref, block_ref):
            spot = place_of(orders[s], host_ref[row] ^ me_ref[0])
            return (jnp.where(spot < half, spot * blocks + remote_ref[row], 0), 0, 0)

        return pl.BlockSpec((1, BLOCK, width), index)

    def answer_spec(row):
        return pl.BlockSpec((1, BLOCK, width), lambda *_: (row, 0, 0))

    far = []
    for row in range(row_count):
        for s in range(STREAMS):
            far += [(near_spec(row, s), slabs[s]), (answer_spec(row), answered[s])]
    far_specs, far_args = [spec for spec, _ in far], [arg for _, arg in far]
    matrices = [(w_edge_in, w_edge_out), (w_node_in, w_node_out), (w_contact_in, w_contact_out)]
    parts = [parts_of(first.shape[0], second.shape[0], groups) for first, second in matrices]
    pair_rows = [chunk_rows(part) for part in parts]
    halves = lambda rows: [struct((half, rows * STREAMS, width), BF16)] * 2
    labelled = [
        struct((row_count, BLOCK + LABEL, columns), BF16) for columns in (2 * width, latent - 2 * width)
    ]
    b_out = [
        struct((node_count, latent), BF16),
        struct((node_count, latent), F32),
        struct((node_count, latent), BF16),
        *halves(pair_rows[1]),
        *halves(pair_rows[2]),
        *labelled,
    ]
    b_args = [node_state, mesh_sum, node_cot, w_node_in, w_node_out, w_contact_in, w_contact_out]
    contact_rows = row_count * BLOCK
    chunk_length = min(4, row_count) * BLOCK
    (node_out, partial_h, d_mesh, n_kept, n_sent, c_kept, c_sent, *away) = pl.pallas_call(
        functools.partial(node_and_contact, orders, parts[1], parts[2], row_count),
        grid_spec=pltpu.PrefetchScalarGridSpec(
            num_scalar_prefetch=4,
            grid=(1,),
            in_specs=far_specs
            + [anywhere if 3 <= i <= 4 else whole(arg.shape) for i, arg in enumerate(b_args)],
            out_specs=[
                anywhere if 3 <= i <= 4 else whole(out.shape) for i, out in enumerate(b_out)
            ],
            scratch_shapes=[
                pltpu.VMEM((contact_rows, 2 * latent), BF16),
                pltpu.VMEM((contact_rows, latent), F32),
                pltpu.VMEM((contact_rows, latent), F32),
                pltpu.VMEM((node_count, latent), F32),
                pltpu.VMEM((max(total_rows(part, groups) for part in parts[1:]), latent), F32),
                pltpu.VMEM((node_count, 3 * latent), BF16),
                pltpu.VMEM((node_count, latent), F32),
                pltpu.VMEM((chunk_length, 2 * latent), F32),
                pltpu.VMEM(w_node_in.shape, BF16),
                pltpu.VMEM(w_node_out.shape, BF16),
                pltpu.VMEM(b_out[3].shape, BF16),
                pltpu.VMEM(b_out[4].shape, BF16),
                pltpu.SemaphoreType.DMA((4,)),
            ],
        ),
        out_shape=b_out,
        compiler_params=params(1),
        cost_estimate=cost(2 * (contact_rows * 9 + node_count * 12) * latent * latent, 12 * 2**20),
        name="node_and_contact",
    )(me, host, contact_remote, contact_block, *far_args, *b_args)

    back = return_orders(orders)
    away_arrived = [swap(value, order[0]) for value, order in zip(away, back[1:])]
    n_arrived, c_arrived = swap(n_sent, orders[1][0]), swap(c_sent, orders[2][0])

    edge_grad, near_h, low, high, e_kept, e_sent = pl.pallas_call(
        functools.partial(edge_backward, orders, parts[0]),
        grid=(steps,),
        in_specs=[
            smem,
            source_block,
            rim_block,
            whole(node_state.shape),
            rim_block,
            edge_block,
            edge_block,
            edge_block,
            edge_block,
            node_block,
            whole((node_count, latent)),
            whole(w_edge_in.shape),
            whole(w_edge_out.shape),
        ],
        out_specs=[
            edge_block,
            whole((node_count, latent)),
            rim_block,
            rim_block,
            *[whole((half, pair_rows[0] * STREAMS, width))] * 2,
        ],
        out_shape=[
            struct((edge_count, latent), BF16),
            struct((node_count, latent), F32),
            struct((RIM, latent), BF16),
            struct((RIM, latent), BF16),
            *halves(pair_rows[0]),
        ],
        scratch_shapes=[
            pltpu.VMEM((extended_rows, latent), BF16),
            pltpu.VMEM((extended_rows, latent), F32),
            pltpu.VMEM((node_count, latent), F32),
            pltpu.VMEM((total_rows(parts[0], groups), latent), F32),
        ],
        compiler_params=params(1),
        cost_estimate=cost(2 * edge_count * latent * latent * 8, edge_count * latent * 20),
        name="edge_backward",
    )(me, sources, before, node_state, after, edge_state, e_pre, e_linear, edge_cot, d_mesh,
      partial_h, w_edge_in, w_edge_out)

    *away_arrived, e_sent = joined([*away_arrived, e_sent])
    e_arrived = swap(e_sent, orders[0][0])
    slots = half * blocks // 2
    def places_call(half_index, dtype, own, arrived):
        return pl.pallas_call(
            functools.partial(add_to_places, back, blocks, half_index),
            in_specs=[smem] * 3 + [pl.BlockSpec(memory_space=pltpu.VMEM)] * 4,
            out_specs=[pl.BlockSpec(memory_space=pltpu.VMEM)] * STREAMS,
            out_shape=[struct((slots, BLOCK, width), dtype)] * STREAMS,
            compiler_params=params(),
            cost_estimate=cost(0, 3 * 2**20),
            name="add_to_places",
        )(me, host, contact_remote, *own, *arrived)

    away_sent = places_call(1, BF16, away, away_arrived)
    n_arrived, c_arrived, *away_sent = joined([n_arrived, c_arrived, *away_sent])
    arrived = [swap(sent, order[1]) for sent, order in zip(away_sent, back)]
    arrived[0], *blocks_in = joined([arrived[0], *away, *away_arrived])
    away_kept = places_call(0, F32, blocks_in[:2], blocks_in[2:])
    *arrived, e_arrived = joined([*arrived, e_arrived])
    away = list(zip(away_kept, away_sent))
    away = added(away, arrived)
    weights = added(
        [(e_kept, e_sent), (n_kept, n_sent), (c_kept, c_sent)], [e_arrived, n_arrived, c_arrived]
    )
    for step in range(1, last - 1):
        sent = [jnp.concatenate([a[1], w[1]], axis=1) for a, w in zip(away, weights)]
        arrived = joined([swap(value, order[step]) for value, order in zip(sent, orders)])
        away = added(away, [value[:, :BLOCK] for value in arrived])
        weights = added(weights, [value[:, BLOCK:] for value in arrived])
    arrived = joined([swap(w[1], order[last - 1]) for w, order in zip(weights, orders)])
    mine = jnp.concatenate(
        [(w[0] + value.astype(F32)).astype(BF16) for w, value in zip(weights, arrived)], axis=1
    )
    mine, low, high = joined([mine, low, high])
    theirs, low, high = joined(
        [swap(mine, far_bit), lax.ppermute(low, "dom", down), lax.ppermute(high, "dom", up)]
    )
    pair = (mine.astype(F32) + theirs[::-1].astype(F32)).astype(BF16)
    away_sent = jnp.concatenate([sent for _, sent in away], axis=2)
    pair, away_sent = joined([pair, away_sent])
    returned = swap(away_sent, far_bit)
    cuts = [sum(pair_rows[:s]) * STREAMS for s in range(STREAMS + 1)]
    sums = [pair[:, cuts[s] : cuts[s + 1]] for s in range(STREAMS)]
    for step in range(1, last):
        sums = both(sums, joined(gather_step(sums, orders, step)))
    gathered = list(zip(sums, gather_step(sums, orders, last)))
    kept = jnp.concatenate([kept for kept, _ in away], axis=2)
    returned = (kept + returned.astype(F32)).reshape(node_count, latent)
    vmem = pl.BlockSpec(memory_space=pltpu.VMEM)
    if all(len(part) == 2 for part in parts):
        summed = []
        for side in range(2):
            summed = pl.pallas_call(
                functools.partial(unpack, orders, parts, side),
                in_specs=[smem] + [vmem] * STREAMS + [anywhere] * len(summed),
                out_specs=[anywhere] * (2 * STREAMS),
                out_shape=[struct(w.shape, F32) for pair in matrices for w in pair],
                scratch_shapes=[
                    *[pltpu.VMEM((half, rows, latent), F32) for rows in pair_rows],
                    pltpu.SemaphoreType.DMA((2 * STREAMS * half,)),
                ],
                input_output_aliases={1 + STREAMS + i: i for i in range(len(summed))},
                compiler_params=params(),
                cost_estimate=cost(0, half * sum(pair_rows) * latent * 10),
                name="unpack",
            )(me, *[pair[side] for pair in gathered], *summed)
    else:
        summed = []
        for s, (first, second) in enumerate(matrices):
            summed += pl.pallas_call(
                functools.partial(unpack_whole, orders[s]),
                in_specs=[smem] + [vmem] * 2,
                out_specs=[vmem] * 2,
                out_shape=[struct(first.shape, F32), struct(second.shape, F32)],
                scratch_shapes=[pltpu.VMEM((pair_rows[s] * groups, latent), F32)],
                compiler_params=params(),
                name="unpack_whole",
            )(me, *gathered[s])

    rims = jnp.concatenate(
        [
            high.astype(F32),
            jnp.zeros((node_count - 2 * RIM, latent), F32),
            low.astype(F32),
        ],
        axis=0,
    )
    node_grad = (near_h + rims + returned).astype(BF16)
    return (node_out, edge_out, node_grad, edge_grad, *summed)


def solution(mesh):
    rows = P(("rep", "dom"), None)
    flat = P(("rep", "dom"))
    weight = P("rep", None)
    in_specs = (rows, rows, flat, flat, rows, flat) + (weight,) * 6 + (rows, rows)
    out_specs = (rows,) * 4 + (weight,) * 6
    return jax.shard_map(
        on_device, mesh=mesh, in_specs=in_specs, out_specs=out_specs, check_vma=False
    )
```

time: 511 us -> 159 us (0.31); the launches traced: 504 us -> 158 us
  waiting for transfers between devices: 275 us -> 58.6 us
  local copies, waits for them, and re-layouts: 82 us -> 2.27 us
  matrix products: 38.9 us -> 0 us
  other arithmetic: 38.6 us -> 6.65 us
  Pallas kernels: 0 us -> 30.5 us
  between operations: 15 us -> 1.43 us
    psum x1 -> x0, waiting for transfers between devices: 169 us -> none  [on_device(): lax.psum((grad_edge_in, grad_edge_out, grad_node_in, grad_node_out, grad_...]
    all_to_all x3 -> x0, waiting for transfers between devices: 106 us -> none  [the longest x1 67.8 us: on_device(): lax.all_to_all(payload.reshape(groups, CAP, BLOCK * latent), 'dom', split...]
    ppermute x4 -> x42, waiting for transfers between devices: 0.28 us -> 58.6 us  [the longest x38 56.9 us: swap(): return lax.ppermute(value, 'dom', [(i, i ^ 1 << bit) for i in range(peers)])]
    ppermute x4 -> x42, starting transfers between devices: 10.8 us -> 58.8 us  [the longest x38 46.6 us: swap(): return lax.ppermute(value, 'dom', [(i, i ^ 1 << bit) for i in range(peers)])]
    all_to_all x3 -> x0, starting transfers between devices: 43.7 us -> none  [the longest x1 30.8 us: on_device(): lax.all_to_all(payload.reshape(groups, CAP, BLOCK * latent), 'dom', split...]
    dot_general x23 -> x0, matrix products: 38.9 us -> none  [the longest x3 9.05 us: forward_mlp(): hidden_pre = jnp.dot(inputs, w_first, preferred_element_type=jnp.float32)]
    reshape x16 -> x0, local copies, waits for them, and re-layouts: 32.1 us -> none  [the longest x2 6.85 us: on_device(): arrived.reshape(slot_count, BLOCK * latent)[slot_index]]
    pallas_call x0 -> x8, Pallas kernels: none -> 30.5 us  [the longest x1 9.07 us: on_device(): pl.pallas_call(functools.partial(node_and_contact, orders, parts[1], part...]
  transfers between devices with their start and end apart: 8 -> 42, of which waited for: 5 -> 22; matrix products, arithmetic and copies ran while one was open for 12% -> 2% of each run, Pallas kernels for 0% -> 11%
where the time goes in v1:
time: 159 us; the launch traced here: 158 us
  starting transfers between devices  58.8 us (37%)
  waiting for transfers between devices  58.6 us (37%)
  Pallas kernels  30.5 us (19%)
  other arithmetic  6.65 us (4%)
  local copies, waits for them, and re-layouts  2.27 us (1%)
    ppermute x38, waiting for transfers between devices, swap(): return lax.ppermute(value, 'dom', [(i, i ^ 1 << bit) for i in range(peers)])  56.9 us
    ppermute x38, starting transfers between devices, swap(): return lax.ppermute(value, 'dom', [(i, i ^ 1 << bit) for i in range(peers)])  46.6 us
    pallas_call x1, Pallas kernels, on_device(): pl.pallas_call(functools.partial(node_and_contact, orders, parts[1], part...  9.07 us
    pallas_call x1, Pallas kernels, on_device(): pl.pallas_call(functools.partial(edge_backward, orders, parts[0]), grid=(...  7.92 us
    ppermute x1, starting transfers between devices, on_device(): lax.ppermute(high, 'dom', up)  5.01 us
    pallas_call x1, Pallas kernels, on_device(): pl.pallas_call(edge_forward, grid=(steps,), in_specs=[source_block, rim_b...  4.63 us
    ppermute x1, starting transfers between devices, on_device(): before = lax.ppermute(node_state[node_count - RIM:], 'dom', up)  4.55 us
    pallas_call x2, Pallas kernels, on_device(): pl.pallas_call(functools.partial(unpack, orders, parts, side), in_specs=[...  4.22 us
  transfers between devices with their start and end apart: 42, of which 22 were waited for; matrix products, arithmetic and copies ran while one was open for 2% of the time, Pallas kernels for 11%

profile of v1, /device:TPU:0, one launch (start us, length us, event | category | flops | bytes accessed | tf_op | source)
XLA Modules:
  0.0 158.2 jit_solution(3546694327033399183)
XLA Ops:
  0.6 4.1 %collective-permute-start = (bf16[256,384]{1,0:T(8,128)(2,1)}, bf16[256,384]{1,0:T(8,128)(2,1)S(1)}, u32[]{:S(2)}, u32[]{:S(2)}) collective-permute-start(bf16[256,384]{1,0:T(8,128)(2,1)} %node_ref.3), channel_id=1, source_target_pairs={{0,16},{2,18},{4,20},{6,22},{8,24},{10,26},{12,28},{14,30},{16,0},... | collective-permute-start | bytes 589832 | tf_op jit(solution)/shard_map/ppermute | solution.py:51
  6.9 4.5 %collective-permute-start.1 = (bf16[64,384]{1,0:T(8,128)(2,1)S(1)}, bf16[64,384]{1,0:T(8,128)(2,1)S(1)}, u32[]{:S(2)}, u32[]{:S(2)}) collective-permute-start(bf16[64,384]{1,0:T(8,128)(2,1)S(1)} %get-tuple-element.204), channel_id=1, source_target_pairs={{0,2},{2,4},{4,6},{6,8},{8,10},{10,12},{12,14},{14,16},{16,18},{18... | collective-permute-start | bytes 147464 | tf_op jit(solution)/shard_map/ppermute | solution.py:494
  15.7 2.9 %collective-permute-start.3 = (s32[8]{0:T(128)S(1)}, s32[8]{0:T(128)S(1)}, u32[]{:S(2)}, u32[]{:S(2)}) collective-permute-start(s32[8]{0:T(128)S(1)} %pad_add_fusion), channel_id=1, source_target_pairs={{0,2},{2,0},{4,6},{6,4},{8,10},{10,8},{12,14},{14,12},{16,18},{18,... | collective-permute-start | bytes 104 | tf_op jit(solution)/shard_map/ppermute | solution.py:51
  28.5 2.7 %collective-permute-done.7 = bf16[2,256,128]{2,1,0:T(8,128)(2,1)S(1)} collective-permute-done((bf16[2,256,128]{2,1,0:T(8,128)(2,1)S(1)}, bf16[2,256,128]{2,1,0:T(8,128)(2,1)S(1)}, u32[]{:S(2)}, u32[]{:S(2)}) %collective-permute-start.7) | collective-permute-done | bytes 131104 | tf_op jit(solution)/shard_map/ppermute | solution.py:51
  33.6 4.6 %edge_forward.1 = (bf16[1024,384]{1,0:T(8,128)(2,1)}, bf16[256,384]{1,0:T(8,128)(2,1)S(1)}, f32[1024,384]{1,0:T(8,128)S(1)}, f32[1024,384]{1,0:T(8,128)}) custom-call(s32[2,1,512]{2,1,0:T(1,128)S(1)} %bitcast.30, bf16[64,384]{1,0:T(8,128)(2,1)S(1)} %collective-permute-done.1.before_ref, bf16[256,384]{1,0:T(8,128)(2,1)S(1)} %copy-done.2, ...), custom_call_target="tpu_custom_call" | custom-call | flops 1811939328 | bytes 6291456 | tf_op jit(solution)/shard_map/edge_forward/pallas_call | solution.py:520
  43.9 2.6 %collective-permute-start.13 = (bf16[4,128,128]{2,1,0:T(8,128)(2,1)S(1)}, bf16[4,128,128]{2,1,0:T(8,128)(2,1)S(1)}, u32[]{:S(2)}, u32[]{:S(2)}) collective-permute-start(bf16[4,128,128]{2,1,0:T(8,128)(2,1)S(1)} %get-tuple-element.122), channel_id=1, source_target_pairs={{0,4},{2,6},{4,0},{6,2},{8,12},{10,14},{12,8},{14,10},{16,20},{18,... | collective-permute-start | bytes 393224 | tf_op jit(solution)/shard_map/ppermute | solution.py:51
  46.4 2.6 %collective-permute-start.14 = (bf16[4,128,128]{2,1,0:T(8,128)(2,1)S(1)}, bf16[4,128,128]{2,1,0:T(8,128)(2,1)S(1)}, u32[]{:S(2)}, u32[]{:S(2)}) collective-permute-start(bf16[4,128,128]{2,1,0:T(8,128)(2,1)S(1)} %get-tuple-element.123), channel_id=1, source_target_pairs={{0,8},{2,10},{4,12},{6,14},{8,0},{10,2},{12,4},{14,6},{16,24},{18,... | collective-permute-start | bytes 393224 | tf_op jit(solution)/shard_map/ppermute | solution.py:51
  49.4 2.6 %collective-permute-done.14.refs_5_.refs_11_.refs_17_.refs_23_ = bf16[4,128,128]{2,1,0:T(8,128)(2,1)S(1)} collective-permute-done((bf16[4,128,128]{2,1,0:T(8,128)(2,1)S(1)}, bf16[4,128,128]{2,1,0:T(8,128)(2,1)S(1)}, u32[]{:S(2)}, u32[]{:S(2)}) %collective-permute-start.14) | collective-permute-done | bytes 131104 | tf_op jit(solution)/shard_map/ppermute | solution.py:51
  52.0 9.1 %node_and_contact.1 = (bf16[256,384]{1,0:T(8,128)(2,1)}, f32[256,384]{1,0:T(8,128)S(1)}, bf16[256,384]{1,0:T(8,128)(2,1)S(1)}, bf16[8,288,128]{2,1,0:T(8,128)(2,...) custom-call(s32[1]{0:T(128)} %bitcast.me_ref, ...), custom_call_target="tpu_custom_call" | custom-call | flops 2264924160 | bytes 12582912 | tf_op jit(solution)/shard_map/node_and_contact/pallas_call | solution.py:598
  61.2 2.1 %collective-permute-start.16 = (bf16[8,240,128]{2,1,0:T(8,128)(2,1)S(1)}, bf16[8,240,128]{2,1,0:T(8,128)(2,1)S(1)}, u32[]{:S(2)}, u32[]{:S(2)}) collective-permute-start(bf16[8,240,128]{2,1,0:T(8,128)(2,1)S(1)} %get-tuple-element.134), channel_id=1, source_target_pairs={{0,8},{2,10},{4,12},{6,14},{8,0},{10,2},{12,4},{14,6},{16,24},{18,... | collective-permute-start | bytes 1474568 | tf_op jit(solution)/shard_map/ppermute | solution.py:51
  63.4 7.9 %edge_backward.1 = (bf16[1024,384]{1,0:T(8,128)(2,1)}, f32[256,384]{1,0:T(8,128)S(1)}, bf16[64,384]{1,0:T(8,128)(2,1)S(1)}, bf16[64,384]{1,0:T(8,128)(2,1)S(1)},...) custom-call(s32[1]{0:T(128)} %bitcast.me_ref, s32[2,1,512]{2,1,0:T(1,128)S(1)} %bitcast.31, ...), custom_call_target="tpu_custom_call" | custom-call | flops 2415919104 | bytes 7864320 | tf_op jit(solution)/shard_map/edge_backward/pallas_call | solution.py:634
  71.4 3.1 %collective-permute-done.18.refs_3_ = bf16[4,144,128]{2,1,0:T(8,128)(2,1)S(1)} collective-permute-done((bf16[4,144,128]{2,1,0:T(8,128)(2,1)S(1)}, bf16[4,144,128]{2,1,0:T(8,128)(2,1)S(1)}, u32[]{:S(2)}, u32[]{:S(2)}) %collective-permute-start.18) | collective-permute-done | bytes 147488 | tf_op jit(solution)/shard_map/ppermute | solution.py:51
  81.6 3.7 %collective-permute-done.19 = bf16[8,128,128]{2,1,0:T(8,128)(2,1)S(1)} collective-permute-done((bf16[8,128,128]{2,1,0:T(8,128)(2,1)S(1)}, bf16[8,128,128]{2,1,0:T(8,128)(2,1)S(1)}, u32[]{:S(2)}, u32[]{:S(2)}) %collective-permute-start.19) | collective-permute-done | bytes 262176 | tf_op jit(solution)/shard_map/ppermute | solution.py:51
  87.6 4.3 %collective-permute-done.21 = bf16[8,128,128]{2,1,0:T(8,128)(2,1)S(1)} collective-permute-done((bf16[8,128,128]{2,1,0:T(8,128)(2,1)S(1)}, bf16[8,128,128]{2,1,0:T(8,128)(2,1)S(1)}, u32[]{:S(2)}, u32[]{:S(2)}) %collective-permute-start.21) | collective-permute-done | bytes 262176 | tf_op jit(solution)/shard_map/ppermute | solution.py:51
  93.3 7.5 %collective-permute-done.25 = bf16[4,368,128]{2,1,0:T(8,128)(2,1)S(1)} collective-permute-done((bf16[4,368,128]{2,1,0:T(8,128)(2,1)S(1)}, bf16[4,368,128]{2,1,0:T(8,128)(2,1)S(1)}, u32[]{:S(2)}, u32[]{:S(2)}) %collective-permute-start.25) | collective-permute-done | bytes 376864 | tf_op jit(solution)/shard_map/ppermute | solution.py:51
  111.4 5.0 %collective-permute-start.31 = (bf16[64,384]{1,0:T(8,128)(2,1)S(1)}, bf16[64,384]{1,0:T(8,128)(2,1)S(1)}, u32[]{:S(2)}, u32[]{:S(2)}) collective-permute-start(bf16[64,384]{1,0:T(8,128)(2,1)S(1)} %get-tuple-element.173), channel_id=1, source_target_pairs={{0,2},{2,4},{4,6},{6,8},{8,10},{10,12},{12,14},{14,16},{16,18},{18... | collective-permute-start | bytes 147464 | tf_op jit(solution)/shard_map/ppermute | solution.py:714
  118.2 8.4 %collective-permute-done.29 = bf16[2,816,128]{2,1,0:T(8,128)(2,1)S(1)} collective-permute-done((bf16[2,816,128]{2,1,0:T(8,128)(2,1)S(1)}, bf16[2,816,128]{2,1,0:T(8,128)(2,1)S(1)}, u32[]{:S(2)}, u32[]{:S(2)}) %collective-permute-start.29) | collective-permute-done | bytes 417824 | tf_op jit(solution)/shard_map/ppermute | solution.py:51
  126.8 2.6 %collective-permute-start.34 = (bf16[2,288,128]{2,1,0:T(8,128)(2,1)S(1)}, bf16[2,288,128]{2,1,0:T(8,128)(2,1)S(1)}, u32[]{:S(2)}, u32[]{:S(2)}) collective-permute-start(bf16[2,288,128]{2,1,0:T(8,128)(2,1)S(1)} %get-tuple-element.198), channel_id=1, source_target_pairs={{0,2},{2,0},{4,6},{6,4},{8,10},{10,8},{12,14},{14,12},{16,18},{18,... | collective-permute-start | bytes 442376 | tf_op jit(solution)/shard_map/ppermute | solution.py:51
  129.4 2.2 %collective-permute-start.35 = (bf16[2,240,128]{2,1,0:T(8,128)(2,1)S(1)}, bf16[2,240,128]{2,1,0:T(8,128)(2,1)S(1)}, u32[]{:S(2)}, u32[]{:S(2)}) collective-permute-start(bf16[2,240,128]{2,1,0:T(8,128)(2,1)S(1)} %slice.163), channel_id=1, source_target_pairs={{0,4},{2,6},{4,0},{6,2},{8,12},{10,14},{12,8},{14,10},{16,20},{18,... | collective-permute-start | bytes 368648 | tf_op jit(solution)/shard_map/ppermute | solution.py:51
  131.6 4.2 %collective-permute-done.35 = bf16[2,240,128]{2,1,0:T(8,128)(2,1)S(1)} collective-permute-done((bf16[2,240,128]{2,1,0:T(8,128)(2,1)S(1)}, bf16[2,240,128]{2,1,0:T(8,128)(2,1)S(1)}, u32[]{:S(2)}, u32[]{:S(2)}) %collective-permute-start.35) | collective-permute-done | bytes 122912 | tf_op jit(solution)/shard_map/ppermute | solution.py:51
  140.0 4.9 %collective-permute-done.38 = bf16[4,240,128]{2,1,0:T(8,128)(2,1)S(1)} collective-permute-done((bf16[4,240,128]{2,1,0:T(8,128)(2,1)S(1)}, bf16[4,240,128]{2,1,0:T(8,128)(2,1)S(1)}, u32[]{:S(2)}, u32[]{:S(2)}) %collective-permute-start.38) | collective-permute-done | bytes 245792 | tf_op jit(solution)/shard_map/ppermute | solution.py:51
  149.0 2.1 %unpack.2 = (f32[1152,384]{1,0:T(8,128)}, f32[384,384]{1,0:T(8,128)}, f32[1152,384]{1,0:T(8,128)}, f32[384,384]{1,0:T(8,128)}, f32[768,384]{1,0:T(8,128)}, /*index=5*/f32[384,384]{1,0:T(8,128)}) custom-call(s32[1]{0:T(128)} %bitcast.me_ref, bf16[8,288,128]{2,1,0:T(8,128)(2,1)S(1)} %pad_maximum_fusion.refs_0_, ...), custom_call_target="tpu_custom_call" | custom-call | bytes 8355840 | tf_op jit(solution)/shard_map/unpack/pallas_call | solution.py:731
  151.1 4.8 %collective-permute-done.41.refs_2_ = bf16[8,240,128]{2,1,0:T(8,128)(2,1)S(1)} collective-permute-done((bf16[8,240,128]{2,1,0:T(8,128)(2,1)S(1)}, bf16[8,240,128]{2,1,0:T(8,128)(2,1)S(1)}, u32[]{:S(2)}, u32[]{:S(2)}) %collective-permute-start.41) | collective-permute-done | bytes 491552 | tf_op jit(solution)/shard_map/ppermute | solution.py:51
  155.9 2.1 %unpack.3 = (f32[1152,384]{1,0:T(8,128)}, f32[384,384]{1,0:T(8,128)}, f32[1152,384]{1,0:T(8,128)}, f32[384,384]{1,0:T(8,128)}, f32[768,384]{1,0:T(8,128)}, /*index=5*/f32[384,384]{1,0:T(8,128)}) custom-call(s32[1]{0:T(128)} %bitcast.me_ref, ...), custom_call_target="tpu_custom_call", output_to_operand_aliasing={{0}: (4, {}), {1}: (5, {}), {2}: (6, {}), {3}: (7, {}), {4}... | custom-call | bytes 8355840 | tf_op jit(solution)/shard_map/unpack/pallas_call | solution.py:731
  (156 shorter events, 55.9 us)
Async XLA Ops:
  0.6 19.5 %collective-permute-start = (bf16[256,384]{1,0:T(8,128)(2,1)}, bf16[256,384]{1,0:T(8,128)(2,1)S(1)}, u32[]{:S(2)}, u32[]{:S(2)}) collective-permute-start(bf16[256,384]{1,0:T(8,128)(2,1)} %node_ref.3), channel_id=1, source_target_pairs={{0,16},{2,18},{4,20},{6,22},{8,24},{10,26},{12,28},{14,30},{16,0},... | collective-permute-start | bytes 589832 | tf_op jit(solution)/shard_map/ppermute | solution.py:51
  5.6 14.5 %collective-permute-start.2 = (bf16[64,384]{1,0:T(8,128)(2,1)S(1)}, bf16[64,384]{1,0:T(8,128)(2,1)S(1)}, u32[]{:S(2)}, u32[]{:S(2)}) collective-permute-start(bf16[64,384]{1,0:T(8,128)(2,1)S(1)} %get-tuple-element.203), channel_id=1, source_target_pairs={{2,0},{4,2},{6,4},{8,6},{10,8},{12,10},{14,12},{16,14},{18,16},{20... | collective-permute-start | bytes 147464 | tf_op jit(solution)/shard_map/ppermute | solution.py:495
  6.9 13.2 %collective-permute-start.1 = (bf16[64,384]{1,0:T(8,128)(2,1)S(1)}, bf16[64,384]{1,0:T(8,128)(2,1)S(1)}, u32[]{:S(2)}, u32[]{:S(2)}) collective-permute-start(bf16[64,384]{1,0:T(8,128)(2,1)S(1)} %get-tuple-element.204), channel_id=1, source_target_pairs={{0,2},{2,4},{4,6},{6,8},{8,10},{10,12},{12,14},{14,16},{16,18},{18... | collective-permute-start | bytes 147464 | tf_op jit(solution)/shard_map/ppermute | solution.py:494
  31.3 6.9 %collective-permute-start.9 = (bf16[4,256,128]{2,1,0:T(8,128)(2,1)S(1)}, bf16[4,256,128]{2,1,0:T(8,128)(2,1)S(1)}, u32[]{:S(2)}, u32[]{:S(2)}) collective-permute-start(bf16[4,256,128]{2,1,0:T(8,128)(2,1)S(1)} %get-tuple-element.109), channel_id=1, source_target_pairs={{0,4},{2,6},{4,0},{6,2},{8,12},{10,14},{12,8},{14,10},{16,20},{18,... | collective-permute-start | bytes 786440 | tf_op jit(solution)/shard_map/ppermute | solution.py:51
  42.2 6.8 %collective-permute-start.12 = (bf16[4,128,128]{2,1,0:T(8,128)(2,1)S(1)}, bf16[4,128,128]{2,1,0:T(8,128)(2,1)S(1)}, u32[]{:S(2)}, u32[]{:S(2)}) collective-permute-start(bf16[4,128,128]{2,1,0:T(8,128)(2,1)S(1)} %get-tuple-element.121), channel_id=1, source_target_pairs={{0,2},{2,0},{4,6},{6,4},{8,10},{10,8},{12,14},{14,12},{16,18},{18,... | collective-permute-start | bytes 393224 | tf_op jit(solution)/shard_map/ppermute | solution.py:51
  61.1 15.2 %collective-permute-start.15 = (bf16[8,288,128]{2,1,0:T(8,128)(2,1)}, bf16[8,288,128]{2,1,0:T(8,128)(2,1)S(1)}, u32[]{:S(2)}, u32[]{:S(2)}) collective-permute-start(bf16[8,288,128]{2,1,0:T(8,128)(2,1)} %get-tuple-element.133), channel_id=1, source_target_pairs={{0,4},{2,6},{4,0},{6,2},{8,12},{10,14},{12,8},{14,10},{16,20},{18,... | collective-permute-start | bytes 1769480 | tf_op jit(solution)/shard_map/ppermute | solution.py:51
  61.2 15.1 %collective-permute-start.16 = (bf16[8,240,128]{2,1,0:T(8,128)(2,1)S(1)}, bf16[8,240,128]{2,1,0:T(8,128)(2,1)S(1)}, u32[]{:S(2)}, u32[]{:S(2)}) collective-permute-start(bf16[8,240,128]{2,1,0:T(8,128)(2,1)S(1)} %get-tuple-element.134), channel_id=1, source_target_pairs={{0,8},{2,10},{4,12},{6,14},{8,0},{10,2},{12,4},{14,6},{16,24},{18,... | collective-permute-start | bytes 1474568 | tf_op jit(solution)/shard_map/ppermute | solution.py:51
  63.3 11.2 %collective-permute-start.17 = (bf16[4,144,256]{2,1,0:T(8,128)(2,1)S(1)}, bf16[4,144,256]{2,1,0:T(8,128)(2,1)S(1)}, u32[]{:S(2)}, u32[]{:S(2)}) collective-permute-start(bf16[4,144,256]{2,1,0:T(8,128)(2,1)S(1)} %get-tuple-element.149.refs_0_), channel_id=1, source_target_pairs={{0,2},{2,0},{4,6},{6,4},{8,10},{10,8},{12,14},{14,12},{16,18},{18,... | collective-permute-start | bytes 884744 | tf_op jit(solution)/shard_map/ppermute | solution.py:51
  63.3 11.1 %collective-permute-start.18 = (bf16[4,144,128]{2,1,0:T(8,128)(2,1)S(1)}, bf16[4,144,128]{2,1,0:T(8,128)(2,1)S(1)}, u32[]{:S(2)}, u32[]{:S(2)}) collective-permute-start(bf16[4,144,128]{2,1,0:T(8,128)(2,1)S(1)} %get-tuple-element.150.refs_1_), channel_id=1, source_target_pairs={{0,8},{2,10},{4,12},{6,14},{8,0},{10,2},{12,4},{14,6},{16,24},{18,... | collective-permute-start | bytes 442376 | tf_op jit(solution)/shard_map/ppermute | solution.py:51
  74.5 17.4 %collective-permute-start.22 = (bf16[8,288,128]{2,1,0:T(8,128)(2,1)S(1)}, bf16[8,288,128]{2,1,0:T(8,128)(2,1)S(1)}, u32[]{:S(2)}, u32[]{:S(2)}) collective-permute-start(bf16[8,288,128]{2,1,0:T(8,128)(2,1)S(1)} %get-tuple-element.147), channel_id=1, source_target_pairs={{0,2},{2,0},{4,6},{6,4},{8,10},{10,8},{12,14},{14,12},{16,18},{18,... | collective-permute-start | bytes 1769480 | tf_op jit(solution)/shard_map/ppermute | solution.py:51
  76.3 9.0 %collective-permute-start.19 = (bf16[8,128,128]{2,1,0:T(8,128)(2,1)S(1)}, bf16[8,128,128]{2,1,0:T(8,128)(2,1)S(1)}, u32[]{:S(2)}, u32[]{:S(2)}) collective-permute-start(bf16[8,128,128]{2,1,0:T(8,128)(2,1)S(1)} %get-tuple-element.143), channel_id=1, source_target_pairs={{0,8},{2,10},{4,12},{6,14},{8,0},{10,2},{12,4},{14,6},{16,24},{18,... | collective-permute-start | bytes 786440 | tf_op jit(solution)/shard_map/ppermute | solution.py:51
  78.4 9.2 %collective-permute-start.20 = (bf16[8,128,128]{2,1,0:T(8,128)(2,1)S(1)}, bf16[8,128,128]{2,1,0:T(8,128)(2,1)S(1)}, u32[]{:S(2)}, u32[]{:S(2)}) collective-permute-start(bf16[8,128,128]{2,1,0:T(8,128)(2,1)S(1)} %get-tuple-element.145), channel_id=1, source_target_pairs={{0,4},{2,6},{4,0},{6,2},{8,12},{10,14},{12,8},{14,10},{16,20},{18,... | collective-permute-start | bytes 786440 | tf_op jit(solution)/shard_map/ppermute | solution.py:51
  80.3 11.6 %collective-permute-start.21 = (bf16[8,128,128]{2,1,0:T(8,128)(2,1)S(1)}, bf16[8,128,128]{2,1,0:T(8,128)(2,1)S(1)}, u32[]{:S(2)}, u32[]{:S(2)}) collective-permute-start(bf16[8,128,128]{2,1,0:T(8,128)(2,1)S(1)} %get-tuple-element.146), channel_id=1, source_target_pairs={{0,4},{2,6},{4,0},{6,2},{8,12},{10,14},{12,8},{14,10},{16,20},{18,... | collective-permute-start | bytes 786440 | tf_op jit(solution)/shard_map/ppermute | solution.py:51
  92.4 9.2 %collective-permute-start.24 = (bf16[4,416,128]{2,1,0:T(8,128)(2,1)S(1)}, bf16[4,416,128]{2,1,0:T(8,128)(2,1)S(1)}, u32[]{:S(2)}, u32[]{:S(2)}) collective-permute-start(bf16[4,416,128]{2,1,0:T(8,128)(2,1)S(1)} %pad_maximum_fusion.7), channel_id=1, source_target_pairs={{0,8},{2,10},{4,12},{6,14},{8,0},{10,2},{12,4},{14,6},{16,24},{18,... | collective-permute-start | bytes 1277960 | tf_op jit(solution)/shard_map/ppermute | solution.py:51
  92.8 8.8 %collective-permute-start.23 = (bf16[4,416,128]{2,1,0:T(8,128)(2,1)S(1)}, bf16[4,416,128]{2,1,0:T(8,128)(2,1)S(1)}, u32[]{:S(2)}, u32[]{:S(2)}) collective-permute-start(bf16[4,416,128]{2,1,0:T(8,128)(2,1)S(1)} %pad_maximum_fusion.6), channel_id=1, source_target_pairs={{0,4},{2,6},{4,0},{6,2},{8,12},{10,14},{12,8},{14,10},{16,20},{18,... | collective-permute-start | bytes 1277960 | tf_op jit(solution)/shard_map/ppermute | solution.py:51
  93.2 7.7 %collective-permute-start.25 = (bf16[4,368,128]{2,1,0:T(8,128)(2,1)S(1)}, bf16[4,368,128]{2,1,0:T(8,128)(2,1)S(1)}, u32[]{:S(2)}, u32[]{:S(2)}) collective-permute-start(bf16[4,368,128]{2,1,0:T(8,128)(2,1)S(1)} %pad_maximum_fusion.9), channel_id=1, source_target_pairs={{0,2},{2,0},{4,6},{6,4},{8,10},{10,8},{12,14},{14,12},{16,18},{18,... | collective-permute-start | bytes 1130504 | tf_op jit(solution)/shard_map/ppermute | solution.py:51
  109.9 16.7 %collective-permute-start.29 = (bf16[2,816,128]{2,1,0:T(8,128)(2,1)S(1)}, bf16[2,816,128]{2,1,0:T(8,128)(2,1)S(1)}, u32[]{:S(2)}, u32[]{:S(2)}) collective-permute-start(bf16[2,816,128]{2,1,0:T(8,128)(2,1)S(1)} %pad_maximum_fusion.8), channel_id=1, source_target_pairs={{0,16},{2,18},{4,20},{6,22},{8,24},{10,26},{12,28},{14,30},{16,0},... | collective-permute-start | bytes 1253384 | tf_op jit(solution)/shard_map/ppermute | solution.py:51
  126.8 9.0 %collective-permute-start.34 = (bf16[2,288,128]{2,1,0:T(8,128)(2,1)S(1)}, bf16[2,288,128]{2,1,0:T(8,128)(2,1)S(1)}, u32[]{:S(2)}, u32[]{:S(2)}) collective-permute-start(bf16[2,288,128]{2,1,0:T(8,128)(2,1)S(1)} %get-tuple-element.198), channel_id=1, source_target_pairs={{0,2},{2,0},{4,6},{6,4},{8,10},{10,8},{12,14},{14,12},{16,18},{18,... | collective-permute-start | bytes 442376 | tf_op jit(solution)/shard_map/ppermute | solution.py:51
  136.2 8.7 %collective-permute-start.37 = (bf16[4,288,128]{2,1,0:T(8,128)(2,1)S(1)}, bf16[4,288,128]{2,1,0:T(8,128)(2,1)S(1)}, u32[]{:S(2)}, u32[]{:S(2)}) collective-permute-start(bf16[4,288,128]{2,1,0:T(8,128)(2,1)S(1)} %pad_maximum_fusion.11), channel_id=1, source_target_pairs={{0,8},{2,10},{4,12},{6,14},{8,0},{10,2},{12,4},{14,6},{16,24},{18,... | collective-permute-start | bytes 884744 | tf_op jit(solution)/shard_map/ppermute | solution.py:51
  136.6 8.3 %collective-permute-start.36 = (bf16[4,288,128]{2,1,0:T(8,128)(2,1)S(1)}, bf16[4,288,128]{2,1,0:T(8,128)(2,1)S(1)}, u32[]{:S(2)}, u32[]{:S(2)}) collective-permute-start(bf16[4,288,128]{2,1,0:T(8,128)(2,1)S(1)} %pad_maximum_fusion.10), channel_id=1, source_target_pairs={{0,4},{2,6},{4,0},{6,2},{8,12},{10,14},{12,8},{14,10},{16,20},{18,... | collective-permute-start | bytes 884744 | tf_op jit(solution)/shard_map/ppermute | solution.py:51
  139.1 9.0 %collective-permute-start.32 = (bf16[2,128,384]{2,1,0:T(8,128)(2,1)S(1)}, bf16[2,128,384]{2,1,0:T(8,128)(2,1)S(1)}, u32[]{:S(2)}, u32[]{:S(2)}) collective-permute-start(bf16[2,128,384]{2,1,0:T(8,128)(2,1)S(1)} %pad_maximum_fusion.16), channel_id=1, source_target_pairs={{0,16},{2,18},{4,20},{6,22},{8,24},{10,26},{12,28},{14,30},{16,0},... | collective-permute-start | bytes 589832 | tf_op jit(solution)/shard_map/ppermute | solution.py:51
  145.0 10.9 %collective-permute-start.40 = (bf16[8,288,128]{2,1,0:T(8,128)(2,1)S(1)}, bf16[8,288,128]{2,1,0:T(8,128)(2,1)S(1)}, u32[]{:S(2)}, u32[]{:S(2)}) collective-permute-start(bf16[8,288,128]{2,1,0:T(8,128)(2,1)S(1)} %pad_maximum_fusion.1.refs_1_), channel_id=1, source_target_pairs={{0,4},{2,6},{4,0},{6,2},{8,12},{10,14},{12,8},{14,10},{16,20},{18,... | collective-permute-start | bytes 1769480 | tf_op jit(solution)/shard_map/ppermute | solution.py:51
  145.5 10.4 %collective-permute-start.39 = (bf16[8,288,128]{2,1,0:T(8,128)(2,1)S(1)}, bf16[8,288,128]{2,1,0:T(8,128)(2,1)S(1)}, u32[]{:S(2)}, u32[]{:S(2)}) collective-permute-start(bf16[8,288,128]{2,1,0:T(8,128)(2,1)S(1)} %pad_maximum_fusion.refs_0_), channel_id=1, source_target_pairs={{0,2},{2,0},{4,6},{6,4},{8,10},{10,8},{12,14},{14,12},{16,18},{18,... | collective-permute-start | bytes 1769480 | tf_op jit(solution)/shard_map/ppermute | solution.py:51
  147.0 8.9 %collective-permute-start.41 = (bf16[8,240,128]{2,1,0:T(8,128)(2,1)S(1)}, bf16[8,240,128]{2,1,0:T(8,128)(2,1)S(1)}, u32[]{:S(2)}, u32[]{:S(2)}) collective-permute-start(bf16[8,240,128]{2,1,0:T(8,128)(2,1)S(1)} %pad_maximum_fusion.5.refs_2_), channel_id=1, source_target_pairs={{0,8},{2,10},{4,12},{6,14},{8,0},{10,2},{12,4},{14,6},{16,24},{18,... | collective-permute-start | bytes 1474568 | tf_op jit(solution)/shard_map/ppermute | solution.py:51
  (33 other events, 263.2 us)

commit v2 on v1

--- a/solution.py
+++ b/solution.py
@@ -49,6 +49,21 @@
 def swap(value, bit):
     peers = lax.axis_size("dom")
     return lax.ppermute(value, "dom", [(i, i ^ (1 << bit)) for i in range(peers)])
+
+
+def swap_rims(first, last):
+    peers = lax.axis_size("dom")
+    odd = lax.axis_index("dom") % 2 == 1
+    pairs = [[(i, i + 1) for i in range(start, peers - 1, 2)] for start in range(2)]
+    both_ways = [pair + [(j, i) for i, j in pair] for pair in pairs]
+    inner = lax.ppermute(jnp.where(odd, first, last), "dom", both_ways[0])
+    outer = lax.ppermute(jnp.where(odd, last, first), "dom", both_ways[1])
+    return inner, outer
+
+
+def sorted_rims(inner, outer):
+    odd = lax.axis_index("dom") % 2 == 1
+    return jnp.where(odd, inner, outer), jnp.where(odd, outer, inner)
 
 
 def joined(values):
@@ -351,17 +366,26 @@
 
 
 def pick_blocks(orders, blocks, row_count, me_ref, *refs):
-    named, slabs, outs, sems = refs[:3], refs[3:6], refs[6:9], refs[9]
+    named, quarters, outs, sems = refs[:3], refs[3:9], refs[9:12], refs[12]
     copies = []
     for s, order in enumerate(orders):
+        near, away = quarters[2 * s], quarters[2 * s + 1]
+        count = near.shape[0]
         for i in range(row_count):
-            spot = place_of(order, named[s][i] ^ me_ref[0])
-            spot = jnp.where(spot < slabs[s].shape[0] // blocks, spot, 0)
-            block = spot * blocks + named[s][row_count + i]
-            copies.append(
-                pltpu.make_async_copy(slabs[s].at[block], outs[s].at[i], sems.at[len(copies)])
-            )
-            copies[-1].start()
+            spot = place_of(order, named[s][i] ^ me_ref[0]) * blocks + named[s][row_count + i]
+            spot = jnp.where(spot < 2 * count, spot, 0)
+            is_near = spot < count
+            sem = sems.at[len(copies)]
+
+            @pl.when(is_near)
+            def _():
+                pltpu.make_async_copy(near.at[spot], outs[s].at[i], sem).start()
+
+            @pl.when(jnp.logical_not(is_near))
+            def _():
+                pltpu.make_async_copy(away.at[spot - count], outs[s].at[i], sem).start()
+
+            copies.append(pltpu.make_async_copy(near.at[0], outs[s].at[i], sem))
     for copy in copies:
         copy.wait()
 
@@ -489,23 +513,22 @@
     smem = pl.BlockSpec(memory_space=pltpu.SMEM)
     anywhere = pl.BlockSpec(memory_space=pl.ANY)
 
-    up = [(i, i + 1) for i in range(groups - 1)]
-    down = [(j, i) for i, j in up]
-    before = lax.ppermute(node_state[node_count - RIM :], "dom", up)
-    after = lax.ppermute(node_state[:RIM], "dom", down)
+    inner, outer = swap_rims(node_state[:RIM], node_state[node_count - RIM :])
     last = len(orders[0]) - 1
     far_bit = orders[0][-1]
     half = groups // 2
     rows_named = jnp.concatenate([host, contact_remote])
-    arrived, before, after, *named = joined(
-        [swap(node_state, far_bit), before, after]
-        + [swap(rows_named, order[0]) for order in orders]
+    arrived, inner, outer, *named = joined(
+        [swap(node_state, far_bit), inner, outer]
+        + [swap(rows_named, order[0]) for order in orders[:2]]
     )
+    before, after = sorted_rims(inner, outer)
     pair = jnp.stack([node_state, arrived])
     slabs = [pair[:, :, s * width : (s + 1) * width] for s in range(STREAMS)]
     for step in range(1, last):
         if step == last - 1:
-            *slabs, before = joined([*slabs, before])
+            *slabs, before, rows_named = joined([*slabs, before, rows_named])
+            named.append(swap(rows_named, orders[2][0]))
         arrived = gather_step(slabs, orders, step)
         if step < last - 1:
             slabs = both(slabs, joined(arrived))
@@ -546,20 +569,25 @@
         name="edge_forward",
     )(sources, before, node_state, after, edge_state, w_edge_in, w_edge_out)
 
-    *arrived, mesh_sum = joined([*arrived, mesh_sum])
-    slabs = [
-        slab.reshape(half * blocks, BLOCK, width) for slab in both(slabs, arrived)
+    *arrived, named[2], mesh_sum = joined([*arrived, named[2], mesh_sum])
+    quarters = [
+        value.reshape(half * blocks // 2, BLOCK, width)
+        for pair in zip(slabs, arrived)
+        for value in pair
     ]
     picked = pl.pallas_call(
         functools.partial(pick_blocks, orders, blocks, row_count),
-        in_specs=[smem] * (1 + STREAMS) + [anywhere] * STREAMS,
+        in_specs=[smem] * (1 + STREAMS) + [anywhere] * (2 * STREAMS),
         out_specs=[anywhere] * STREAMS,
         out_shape=[struct((row_count, BLOCK, width), BF16)] * STREAMS,
         scratch_shapes=[pltpu.SemaphoreType.DMA((STREAMS * row_count,))],
         compiler_params=params(),
         cost_estimate=cost(0, 2**20),
         name="pick_blocks",
-    )(me, *named, *slabs)
+    )(me, *named, *quarters)
+    joined_now = joined([*picked, *quarters])
+    picked, quarters = joined_now[:STREAMS], joined_now[STREAMS:]
+    slabs = [jnp.concatenate(quarters[2 * s : 2 * s + 2], axis=0) for s in range(STREAMS)]
     answered = [swap(value, order[0]) for value, order in zip(picked, orders)]
 
     def near_spec(row, s):
@@ -710,9 +738,8 @@
         [(w[0] + value.astype(F32)).astype(BF16) for w, value in zip(weights, arrived)], axis=1
     )
     mine, low, high = joined([mine, low, high])
-    theirs, low, high = joined(
-        [swap(mine, far_bit), lax.ppermute(low, "dom", down), lax.ppermute(high, "dom", up)]
-    )
+    theirs, *rims = joined([swap(mine, far_bit), *swap_rims(low, high)])
+    high, low = sorted_rims(*rims)
     pair = (mine.astype(F32) + theirs[::-1].astype(F32)).astype(BF16)
     away_sent = jnp.concatenate([sent for _, sent in away], axis=2)
     pair, away_sent = joined([pair, away_sent])

time: 159 us -> 152 us (0.956)
  waiting for transfers between devices: 58.6 us -> 52.5 us
    ppermute x38, waiting for transfers between devices: 56.9 us -> 50.3 us  [swap(): return lax.ppermute(value, 'dom', [(i, i ^ 1 << bit) for i in range(peers)])]
    ppermute x4, starting transfers between devices: 12.1 us -> 9.3 us  [the longest x2 7.75 us: swap_rims(): inner = lax.ppermute(jnp.where(odd, first, last), 'dom', both_ways[0])]
    concatenate x11 -> x8, other arithmetic: 2.79 us -> 0.33 us  [both(): return [jnp.concatenate(pair, axis=0) for pair in zip(held, arrived)]]
    concatenate x0 -> x3, other arithmetic: none -> 1.73 us  [on_device(): jnp.concatenate(quarters[2 * s:2 * s + 2], axis=0)]
    ppermute x38, starting transfers between devices: 46.6 us -> 48.3 us  [swap(): return lax.ppermute(value, 'dom', [(i, i ^ 1 << bit) for i in range(peers)])]
  transfers between devices with their start and end apart: 42 -> 42, of which waited for: 22 -> 23; matrix products, arithmetic and copies ran while one was open for 2% -> 3% of each run, Pallas kernels for 11% -> 12%
where the time goes in v2:
time: 152 us; the launch traced here: 151 us
  starting transfers between devices  57.6 us (38%)
  waiting for transfers between devices  52.5 us (35%)
  Pallas kernels  30.6 us (20%)
  other arithmetic  6.82 us (4%)
  local copies, waits for them, and re-layouts  2.52 us (2%)
    ppermute x38, waiting for transfers between devices, swap(): return lax.ppermute(value, 'dom', [(i, i ^ 1 << bit) for i in range(peers)])  50.3 us
    ppermute x38, starting transfers between devices, swap(): return lax.ppermute(value, 'dom', [(i, i ^ 1 << bit) for i in range(peers)])  48.3 us
    pallas_call x1, Pallas kernels, on_device(): pl.pallas_call(functools.partial(node_and_contact, orders, parts[1], part...  9.08 us
    pallas_call x1, Pallas kernels, on_device(): pl.pallas_call(functools.partial(edge_backward, orders, parts[0]), grid=(...  7.93 us
    ppermute x2, starting transfers between devices, swap_rims(): inner = lax.ppermute(jnp.where(odd, first, last), 'dom', both_ways[0])  7.75 us
    pallas_call x1, Pallas kernels, on_device(): pl.pallas_call(edge_forward, grid=(steps,), in_specs=[source_block, rim_b...  4.64 us
    pallas_call x2, Pallas kernels, on_device(): pl.pallas_call(functools.partial(unpack, orders, parts, side), in_specs=[...  4.22 us
    pallas_call x2, Pallas kernels, places_call(): pl.pallas_call(functools.partial(add_to_places, back, blocks, half_index)...  3.32 us
  transfers between devices with their start and end apart: 42, of which 23 were waited for; matrix products, arithmetic and copies ran while one was open for 3% of the time, Pallas kernels for 12%

profile of v2, /device:TPU:0, one launch (start us, length us, event | category | flops | bytes accessed | tf_op | source)
XLA Modules:
  0.0 151.4 jit_solution(6662439132675137395)
XLA Ops:
  0.6 4.1 %collective-permute-start = (bf16[256,384]{1,0:T(8,128)(2,1)}, bf16[256,384]{1,0:T(8,128)(2,1)S(1)}, u32[]{:S(2)}, u32[]{:S(2)}) collective-permute-start(bf16[256,384]{1,0:T(8,128)(2,1)} %node_ref.3), channel_id=1, source_target_pairs={{0,16},{2,18},{4,20},{6,22},{8,24},{10,26},{12,28},{14,30},{16,0},... | collective-permute-start | bytes 589832 | tf_op jit(solution)/shard_map/ppermute | solution.py:51
  6.3 4.3 %collective-permute-start.1 = (bf16[64,384]{1,0:T(8,128)(2,1)S(1)}, bf16[64,384]{1,0:T(8,128)(2,1)S(1)}, u32[]{:S(2)}, u32[]{:S(2)}) collective-permute-start(bf16[64,384]{1,0:T(8,128)(2,1)S(1)} %get-tuple-element.224), channel_id=1, source_target_pairs={{0,2},{4,6},{8,10},{12,14},{16,18},{20,22},{24,26},{28,30},{2,0},{... | collective-permute-start | bytes 147464 | tf_op jit(solution)/shard_map/ppermute | solution.py:59
  28.9 4.6 %edge_forward.1 = (bf16[1024,384]{1,0:T(8,128)(2,1)}, bf16[256,384]{1,0:T(8,128)(2,1)S(1)}, f32[1024,384]{1,0:T(8,128)S(1)}, f32[1024,384]{1,0:T(8,128)}) custom-call(s32[2,1,512]{2,1,0:T(1,128)S(1)} %bitcast.30, bf16[64,384]{1,0:T(8,128)(2,1)S(1)} %get-tuple-element.126.before_ref, bf16[256,384]{1,0:T(8,128)(2,1)S(1)} %copy-done, ...), custom_call_target="tpu_custom_call" | custom-call | flops 1811939328 | bytes 6291456 | tf_op jit(solution)/shard_map/edge_forward/pallas_call | solution.py:543
  36.2 1.9 %collective-permute-start.13 = (bf16[4,128,128]{2,1,0:T(8,128)(2,1)S(1)}, bf16[4,128,128]{2,1,0:T(8,128)(2,1)S(1)}, u32[]{:S(2)}, u32[]{:S(2)}) collective-permute-start(bf16[4,128,128]{2,1,0:T(8,128)(2,1)S(1)} %get-tuple-element.140), channel_id=1, source_target_pairs={{0,4},{2,6},{4,0},{6,2},{8,12},{10,14},{12,8},{14,10},{16,20},{18,... | collective-permute-start | bytes 393224 | tf_op jit(solution)/shard_map/ppermute | solution.py:51
  43.2 9.1 %node_and_contact.1 = (bf16[256,384]{1,0:T(8,128)(2,1)}, f32[256,384]{1,0:T(8,128)S(1)}, bf16[256,384]{1,0:T(8,128)(2,1)S(1)}, bf16[8,288,128]{2,1,0:T(8,128)(2,...) custom-call(s32[1]{0:T(128)} %bitcast.me_ref, ...), custom_call_target="tpu_custom_call" | custom-call | flops 2264924160 | bytes 12582912 | tf_op jit(solution)/shard_map/node_and_contact/pallas_call | solution.py:626
  56.4 7.9 %edge_backward.1 = (bf16[1024,384]{1,0:T(8,128)(2,1)}, f32[256,384]{1,0:T(8,128)S(1)}, bf16[64,384]{1,0:T(8,128)(2,1)S(1)}, bf16[64,384]{1,0:T(8,128)(2,1)S(1)},...) custom-call(s32[1]{0:T(128)} %bitcast.me_ref, s32[2,1,512]{2,1,0:T(1,128)S(1)} %bitcast.31, ...), custom_call_target="tpu_custom_call" | custom-call | flops 2415919104 | bytes 7864320 | tf_op jit(solution)/shard_map/edge_backward/pallas_call | solution.py:662
  72.0 2.5 %collective-permute-done.19 = bf16[8,128,128]{2,1,0:T(8,128)(2,1)S(1)} collective-permute-done((bf16[8,128,128]{2,1,0:T(8,128)(2,1)S(1)}, bf16[8,128,128]{2,1,0:T(8,128)(2,1)S(1)}, u32[]{:S(2)}, u32[]{:S(2)}) %collective-permute-start.19) | collective-permute-done | bytes 262176 | tf_op jit(solution)/shard_map/ppermute | solution.py:51
  76.7 5.6 %collective-permute-done.21 = bf16[8,128,128]{2,1,0:T(8,128)(2,1)S(1)} collective-permute-done((bf16[8,128,128]{2,1,0:T(8,128)(2,1)S(1)}, bf16[8,128,128]{2,1,0:T(8,128)(2,1)S(1)}, u32[]{:S(2)}, u32[]{:S(2)}) %collective-permute-start.21) | collective-permute-done | bytes 262176 | tf_op jit(solution)/shard_map/ppermute | solution.py:51
  85.0 7.6 %collective-permute-done.25 = bf16[4,368,128]{2,1,0:T(8,128)(2,1)S(1)} collective-permute-done((bf16[4,368,128]{2,1,0:T(8,128)(2,1)S(1)}, bf16[4,368,128]{2,1,0:T(8,128)(2,1)S(1)}, u32[]{:S(2)}, u32[]{:S(2)}) %collective-permute-start.25) | collective-permute-done | bytes 376864 | tf_op jit(solution)/shard_map/ppermute | solution.py:51
  95.4 2.4 %collective-permute-done.28 = bf16[2,240,128]{2,1,0:T(8,128)(2,1)S(1)} collective-permute-done((bf16[2,240,128]{2,1,0:T(8,128)(2,1)S(1)}, bf16[2,240,128]{2,1,0:T(8,128)(2,1)S(1)}, u32[]{:S(2)}, u32[]{:S(2)}) %collective-permute-start.28) | collective-permute-done | bytes 122912 | tf_op jit(solution)/shard_map/ppermute | solution.py:51
  99.9 5.1 %collective-permute-start.29 = (bf16[2,816,128]{2,1,0:T(8,128)(2,1)S(1)}, bf16[2,816,128]{2,1,0:T(8,128)(2,1)S(1)}, u32[]{:S(2)}, u32[]{:S(2)}) collective-permute-start(bf16[2,816,128]{2,1,0:T(8,128)(2,1)S(1)} %pad_maximum_fusion.8), channel_id=1, source_target_pairs={{0,16},{2,18},{4,20},{6,22},{8,24},{10,26},{12,28},{14,30},{16,0},... | collective-permute-start | bytes 1253384 | tf_op jit(solution)/shard_map/ppermute | solution.py:51
  105.9 3.5 %collective-permute-start.30 = (bf16[64,384]{1,0:T(8,128)(2,1)S(1)}, bf16[64,384]{1,0:T(8,128)(2,1)S(1)}, u32[]{:S(2)}, u32[]{:S(2)}) collective-permute-start(bf16[64,384]{1,0:T(8,128)(2,1)S(1)} %get-tuple-element.228), channel_id=1, source_target_pairs={{0,2},{4,6},{8,10},{12,14},{16,18},{20,22},{24,26},{28,30},{2,0},{... | collective-permute-start | bytes 147464 | tf_op jit(solution)/shard_map/ppermute | solution.py:59
  109.4 2.2 %collective-permute-done.30 = bf16[64,384]{1,0:T(8,128)(2,1)S(1)} collective-permute-done((bf16[64,384]{1,0:T(8,128)(2,1)S(1)}, bf16[64,384]{1,0:T(8,128)(2,1)S(1)}, u32[]{:S(2)}, u32[]{:S(2)}) %collective-permute-start.30) | collective-permute-done | bytes 49184 | tf_op jit(solution)/shard_map/ppermute | solution.py:59
  111.7 3.8 %collective-permute-done.29 = bf16[2,816,128]{2,1,0:T(8,128)(2,1)S(1)} collective-permute-done((bf16[2,816,128]{2,1,0:T(8,128)(2,1)S(1)}, bf16[2,816,128]{2,1,0:T(8,128)(2,1)S(1)}, u32[]{:S(2)}, u32[]{:S(2)}) %collective-permute-start.29) | collective-permute-done | bytes 417824 | tf_op jit(solution)/shard_map/ppermute | solution.py:51
  115.7 3.0 %collective-permute-start.34 = (bf16[2,288,128]{2,1,0:T(8,128)(2,1)S(1)}, bf16[2,288,128]{2,1,0:T(8,128)(2,1)S(1)}, u32[]{:S(2)}, u32[]{:S(2)}) collective-permute-start(bf16[2,288,128]{2,1,0:T(8,128)(2,1)S(1)} %get-tuple-element.218), channel_id=1, source_target_pairs={{0,2},{2,0},{4,6},{6,4},{8,10},{10,8},{12,14},{14,12},{16,18},{18,... | collective-permute-start | bytes 442376 | tf_op jit(solution)/shard_map/ppermute | solution.py:51
  118.7 2.5 %collective-permute-start.33 = (bf16[2,288,128]{2,1,0:T(8,128)(2,1)S(1)}, bf16[2,288,128]{2,1,0:T(8,128)(2,1)S(1)}, u32[]{:S(2)}, u32[]{:S(2)}) collective-permute-start(bf16[2,288,128]{2,1,0:T(8,128)(2,1)S(1)} %get-tuple-element.219), channel_id=1, source_target_pairs={{0,8},{2,10},{4,12},{6,14},{8,0},{10,2},{12,4},{14,6},{16,24},{18,... | collective-permute-start | bytes 442376 | tf_op jit(solution)/shard_map/ppermute | solution.py:51
  121.2 2.2 %collective-permute-start.35 = (bf16[2,240,128]{2,1,0:T(8,128)(2,1)S(1)}, bf16[2,240,128]{2,1,0:T(8,128)(2,1)S(1)}, u32[]{:S(2)}, u32[]{:S(2)}) collective-permute-start(bf16[2,240,128]{2,1,0:T(8,128)(2,1)S(1)} %slice.163), channel_id=1, source_target_pairs={{0,4},{2,6},{4,0},{6,2},{8,12},{10,14},{12,8},{14,10},{16,20},{18,... | collective-permute-start | bytes 368648 | tf_op jit(solution)/shard_map/ppermute | solution.py:51
  123.5 4.1 %collective-permute-done.35 = bf16[2,240,128]{2,1,0:T(8,128)(2,1)S(1)} collective-permute-done((bf16[2,240,128]{2,1,0:T(8,128)(2,1)S(1)}, bf16[2,240,128]{2,1,0:T(8,128)(2,1)S(1)}, u32[]{:S(2)}, u32[]{:S(2)}) %collective-permute-start.35) | collective-permute-done | bytes 122912 | tf_op jit(solution)/shard_map/ppermute | solution.py:51
  127.7 2.1 %collective-permute-start.37 = (bf16[4,288,128]{2,1,0:T(8,128)(2,1)S(1)}, bf16[4,288,128]{2,1,0:T(8,128)(2,1)S(1)}, u32[]{:S(2)}, u32[]{:S(2)}) collective-permute-start(bf16[4,288,128]{2,1,0:T(8,128)(2,1)S(1)} %pad_maximum_fusion.11), channel_id=1, source_target_pairs={{0,8},{2,10},{4,12},{6,14},{8,0},{10,2},{12,4},{14,6},{16,24},{18,... | collective-permute-start | bytes 884744 | tf_op jit(solution)/shard_map/ppermute | solution.py:51
  129.8 2.1 %collective-permute-start.36 = (bf16[4,288,128]{2,1,0:T(8,128)(2,1)S(1)}, bf16[4,288,128]{2,1,0:T(8,128)(2,1)S(1)}, u32[]{:S(2)}, u32[]{:S(2)}) collective-permute-start(bf16[4,288,128]{2,1,0:T(8,128)(2,1)S(1)} %pad_maximum_fusion.10), channel_id=1, source_target_pairs={{0,4},{2,6},{4,0},{6,2},{8,12},{10,14},{12,8},{14,10},{16,20},{18,... | collective-permute-start | bytes 884744 | tf_op jit(solution)/shard_map/ppermute | solution.py:51
  132.4 5.8 %collective-permute-done.38 = bf16[4,240,128]{2,1,0:T(8,128)(2,1)S(1)} collective-permute-done((bf16[4,240,128]{2,1,0:T(8,128)(2,1)S(1)}, bf16[4,240,128]{2,1,0:T(8,128)(2,1)S(1)}, u32[]{:S(2)}, u32[]{:S(2)}) %collective-permute-start.38) | collective-permute-done | bytes 245792 | tf_op jit(solution)/shard_map/ppermute | solution.py:51
  141.9 2.1 %unpack.2 = (f32[1152,384]{1,0:T(8,128)}, f32[384,384]{1,0:T(8,128)}, f32[1152,384]{1,0:T(8,128)}, f32[384,384]{1,0:T(8,128)}, f32[768,384]{1,0:T(8,128)}, /*index=5*/f32[384,384]{1,0:T(8,128)}) custom-call(s32[1]{0:T(128)} %bitcast.me_ref, bf16[8,288,128]{2,1,0:T(8,128)(2,1)S(1)} %pad_maximum_fusion.refs_0_, ...), custom_call_target="tpu_custom_call" | custom-call | bytes 8355840 | tf_op jit(solution)/shard_map/unpack/pallas_call | solution.py:758
  144.0 3.3 %collective-permute-done.41.refs_2_ = bf16[8,240,128]{2,1,0:T(8,128)(2,1)S(1)} collective-permute-done((bf16[8,240,128]{2,1,0:T(8,128)(2,1)S(1)}, bf16[8,240,128]{2,1,0:T(8,128)(2,1)S(1)}, u32[]{:S(2)}, u32[]{:S(2)}) %collective-permute-start.41) | collective-permute-done | bytes 491552 | tf_op jit(solution)/shard_map/ppermute | solution.py:51
  149.2 2.1 %unpack.3 = (f32[1152,384]{1,0:T(8,128)}, f32[384,384]{1,0:T(8,128)}, f32[1152,384]{1,0:T(8,128)}, f32[384,384]{1,0:T(8,128)}, f32[768,384]{1,0:T(8,128)}, /*index=5*/f32[384,384]{1,0:T(8,128)}) custom-call(s32[1]{0:T(128)} %bitcast.me_ref, ...), custom_call_target="tpu_custom_call", output_to_operand_aliasing={{0}: (4, {}), {1}: (5, {}), {2}: (6, {}), {3}: (7, {}), {4}... | custom-call | bytes 8355840 | tf_op jit(solution)/shard_map/unpack/pallas_call | solution.py:758
  (162 shorter events, 56.1 us)
Async XLA Ops:
  0.6 15.7 %collective-permute-start = (bf16[256,384]{1,0:T(8,128)(2,1)}, bf16[256,384]{1,0:T(8,128)(2,1)S(1)}, u32[]{:S(2)}, u32[]{:S(2)}) collective-permute-start(bf16[256,384]{1,0:T(8,128)(2,1)} %node_ref.3), channel_id=1, source_target_pairs={{0,16},{2,18},{4,20},{6,22},{8,24},{10,26},{12,28},{14,30},{16,0},... | collective-permute-start | bytes 589832 | tf_op jit(solution)/shard_map/ppermute | solution.py:51
  5.6 10.8 %collective-permute-start.2 = (bf16[64,384]{1,0:T(8,128)(2,1)S(1)}, bf16[64,384]{1,0:T(8,128)(2,1)S(1)}, u32[]{:S(2)}, u32[]{:S(2)}) collective-permute-start(bf16[64,384]{1,0:T(8,128)(2,1)S(1)} %get-tuple-element.223), channel_id=1, source_target_pairs={{2,4},{6,8},{10,12},{14,16},{18,20},{22,24},{26,28},{4,2},{8,6},{1... | collective-permute-start | bytes 147464 | tf_op jit(solution)/shard_map/ppermute | solution.py:60
  6.3 10.1 %collective-permute-start.1 = (bf16[64,384]{1,0:T(8,128)(2,1)S(1)}, bf16[64,384]{1,0:T(8,128)(2,1)S(1)}, u32[]{:S(2)}, u32[]{:S(2)}) collective-permute-start(bf16[64,384]{1,0:T(8,128)(2,1)S(1)} %get-tuple-element.224), channel_id=1, source_target_pairs={{0,2},{4,6},{8,10},{12,14},{16,18},{20,22},{24,26},{28,30},{2,0},{... | collective-permute-start | bytes 147464 | tf_op jit(solution)/shard_map/ppermute | solution.py:59
  24.7 9.9 %collective-permute-start.8 = (bf16[4,256,128]{2,1,0:T(8,128)(2,1)S(1)}, bf16[4,256,128]{2,1,0:T(8,128)(2,1)S(1)}, u32[]{:S(2)}, u32[]{:S(2)}) collective-permute-start(bf16[4,256,128]{2,1,0:T(8,128)(2,1)S(1)} %get-tuple-element.122), channel_id=1, source_target_pairs={{0,4},{2,6},{4,0},{6,2},{8,12},{10,14},{12,8},{14,10},{16,20},{18,... | collective-permute-start | bytes 786440 | tf_op jit(solution)/shard_map/ppermute | solution.py:51
  24.9 9.8 %collective-permute-start.9 = (bf16[4,256,128]{2,1,0:T(8,128)(2,1)S(1)}, bf16[4,256,128]{2,1,0:T(8,128)(2,1)S(1)}, u32[]{:S(2)}, u32[]{:S(2)}) collective-permute-start(bf16[4,256,128]{2,1,0:T(8,128)(2,1)S(1)} %get-tuple-element.123), channel_id=1, source_target_pairs={{0,8},{2,10},{4,12},{6,14},{8,0},{10,2},{12,4},{14,6},{16,24},{18,... | collective-permute-start | bytes 786440 | tf_op jit(solution)/shard_map/ppermute | solution.py:51
  26.8 7.9 %collective-permute-start.10 = (bf16[4,256,128]{2,1,0:T(8,128)(2,1)S(1)}, bf16[4,256,128]{2,1,0:T(8,128)(2,1)S(1)}, u32[]{:S(2)}, u32[]{:S(2)}) collective-permute-start(bf16[4,256,128]{2,1,0:T(8,128)(2,1)S(1)} %pad_maximum_fusion.14), channel_id=1, source_target_pairs={{0,2},{2,0},{4,6},{6,4},{8,10},{10,8},{12,14},{14,12},{16,18},{18,... | collective-permute-start | bytes 786440 | tf_op jit(solution)/shard_map/ppermute | solution.py:51
  52.3 15.2 %collective-permute-start.15 = (bf16[8,288,128]{2,1,0:T(8,128)(2,1)}, bf16[8,288,128]{2,1,0:T(8,128)(2,1)S(1)}, u32[]{:S(2)}, u32[]{:S(2)}) collective-permute-start(bf16[8,288,128]{2,1,0:T(8,128)(2,1)} %get-tuple-element.153), channel_id=1, source_target_pairs={{0,4},{2,6},{4,0},{6,2},{8,12},{10,14},{12,8},{14,10},{16,20},{18,... | collective-permute-start | bytes 1769480 | tf_op jit(solution)/shard_map/ppermute | solution.py:51
  52.4 15.0 %collective-permute-start.16 = (bf16[8,240,128]{2,1,0:T(8,128)(2,1)S(1)}, bf16[8,240,128]{2,1,0:T(8,128)(2,1)S(1)}, u32[]{:S(2)}, u32[]{:S(2)}) collective-permute-start(bf16[8,240,128]{2,1,0:T(8,128)(2,1)S(1)} %get-tuple-element.154), channel_id=1, source_target_pairs={{0,8},{2,10},{4,12},{6,14},{8,0},{10,2},{12,4},{14,6},{16,24},{18,... | collective-permute-start | bytes 1474568 | tf_op jit(solution)/shard_map/ppermute | solution.py:51
  54.3 10.0 %collective-permute-start.17 = (bf16[4,144,256]{2,1,0:T(8,128)(2,1)S(1)}, bf16[4,144,256]{2,1,0:T(8,128)(2,1)S(1)}, u32[]{:S(2)}, u32[]{:S(2)}) collective-permute-start(bf16[4,144,256]{2,1,0:T(8,128)(2,1)S(1)} %get-tuple-element.169.refs_0_), channel_id=1, source_target_pairs={{0,2},{2,0},{4,6},{6,4},{8,10},{10,8},{12,14},{14,12},{16,18},{18,... | collective-permute-start | bytes 884744 | tf_op jit(solution)/shard_map/ppermute | solution.py:51
  54.8 9.5 %collective-permute-start.18 = (bf16[4,144,128]{2,1,0:T(8,128)(2,1)S(1)}, bf16[4,144,128]{2,1,0:T(8,128)(2,1)S(1)}, u32[]{:S(2)}, u32[]{:S(2)}) collective-permute-start(bf16[4,144,128]{2,1,0:T(8,128)(2,1)S(1)} %get-tuple-element.170.refs_1_), channel_id=1, source_target_pairs={{0,8},{2,10},{4,12},{6,14},{8,0},{10,2},{12,4},{14,6},{16,24},{18,... | collective-permute-start | bytes 442376 | tf_op jit(solution)/shard_map/ppermute | solution.py:51
  64.3 18.1 %collective-permute-start.22 = (bf16[8,288,128]{2,1,0:T(8,128)(2,1)S(1)}, bf16[8,288,128]{2,1,0:T(8,128)(2,1)S(1)}, u32[]{:S(2)}, u32[]{:S(2)}) collective-permute-start(bf16[8,288,128]{2,1,0:T(8,128)(2,1)S(1)} %get-tuple-element.167), channel_id=1, source_target_pairs={{0,2},{2,0},{4,6},{6,4},{8,10},{10,8},{12,14},{14,12},{16,18},{18,... | collective-permute-start | bytes 1769480 | tf_op jit(solution)/shard_map/ppermute | solution.py:51
  68.8 8.0 %collective-permute-start.20 = (bf16[8,128,128]{2,1,0:T(8,128)(2,1)S(1)}, bf16[8,128,128]{2,1,0:T(8,128)(2,1)S(1)}, u32[]{:S(2)}, u32[]{:S(2)}) collective-permute-start(bf16[8,128,128]{2,1,0:T(8,128)(2,1)S(1)} %get-tuple-element.165), channel_id=1, source_target_pairs={{0,4},{2,6},{4,0},{6,2},{8,12},{10,14},{12,8},{14,10},{16,20},{18,... | collective-permute-start | bytes 786440 | tf_op jit(solution)/shard_map/ppermute | solution.py:51
  70.5 11.9 %collective-permute-start.21 = (bf16[8,128,128]{2,1,0:T(8,128)(2,1)S(1)}, bf16[8,128,128]{2,1,0:T(8,128)(2,1)S(1)}, u32[]{:S(2)}, u32[]{:S(2)}) collective-permute-start(bf16[8,128,128]{2,1,0:T(8,128)(2,1)S(1)} %get-tuple-element.166), channel_id=1, source_target_pairs={{0,4},{2,6},{4,0},{6,2},{8,12},{10,14},{12,8},{14,10},{16,20},{18,... | collective-permute-start | bytes 786440 | tf_op jit(solution)/shard_map/ppermute | solution.py:51
  82.8 9.8 %collective-permute-start.24 = (bf16[4,416,128]{2,1,0:T(8,128)(2,1)S(1)}, bf16[4,416,128]{2,1,0:T(8,128)(2,1)S(1)}, u32[]{:S(2)}, u32[]{:S(2)}) collective-permute-start(bf16[4,416,128]{2,1,0:T(8,128)(2,1)S(1)} %pad_maximum_fusion.7), channel_id=1, source_target_pairs={{0,8},{2,10},{4,12},{6,14},{8,0},{10,2},{12,4},{14,6},{16,24},{18,... | collective-permute-start | bytes 1277960 | tf_op jit(solution)/shard_map/ppermute | solution.py:51
  83.0 9.7 %collective-permute-start.23 = (bf16[4,416,128]{2,1,0:T(8,128)(2,1)S(1)}, bf16[4,416,128]{2,1,0:T(8,128)(2,1)S(1)}, u32[]{:S(2)}, u32[]{:S(2)}) collective-permute-start(bf16[4,416,128]{2,1,0:T(8,128)(2,1)S(1)} %pad_maximum_fusion.6), channel_id=1, source_target_pairs={{0,4},{2,6},{4,0},{6,2},{8,12},{10,14},{12,8},{14,10},{16,20},{18,... | collective-permute-start | bytes 1277960 | tf_op jit(solution)/shard_map/ppermute | solution.py:51
  99.9 15.7 %collective-permute-start.29 = (bf16[2,816,128]{2,1,0:T(8,128)(2,1)S(1)}, bf16[2,816,128]{2,1,0:T(8,128)(2,1)S(1)}, u32[]{:S(2)}, u32[]{:S(2)}) collective-permute-start(bf16[2,816,128]{2,1,0:T(8,128)(2,1)S(1)} %pad_maximum_fusion.8), channel_id=1, source_target_pairs={{0,16},{2,18},{4,20},{6,22},{8,24},{10,26},{12,28},{14,30},{16,0},... | collective-permute-start | bytes 1253384 | tf_op jit(solution)/shard_map/ppermute | solution.py:51
  115.7 11.9 %collective-permute-start.34 = (bf16[2,288,128]{2,1,0:T(8,128)(2,1)S(1)}, bf16[2,288,128]{2,1,0:T(8,128)(2,1)S(1)}, u32[]{:S(2)}, u32[]{:S(2)}) collective-permute-start(bf16[2,288,128]{2,1,0:T(8,128)(2,1)S(1)} %get-tuple-element.218), channel_id=1, source_target_pairs={{0,2},{2,0},{4,6},{6,4},{8,10},{10,8},{12,14},{14,12},{16,18},{18,... | collective-permute-start | bytes 442376 | tf_op jit(solution)/shard_map/ppermute | solution.py:51
  118.7 8.9 %collective-permute-start.33 = (bf16[2,288,128]{2,1,0:T(8,128)(2,1)S(1)}, bf16[2,288,128]{2,1,0:T(8,128)(2,1)S(1)}, u32[]{:S(2)}, u32[]{:S(2)}) collective-permute-start(bf16[2,288,128]{2,1,0:T(8,128)(2,1)S(1)} %get-tuple-element.219), channel_id=1, source_target_pairs={{0,8},{2,10},{4,12},{6,14},{8,0},{10,2},{12,4},{14,6},{16,24},{18,... | collective-permute-start | bytes 442376 | tf_op jit(solution)/shard_map/ppermute | solution.py:51
  127.7 10.5 %collective-permute-start.37 = (bf16[4,288,128]{2,1,0:T(8,128)(2,1)S(1)}, bf16[4,288,128]{2,1,0:T(8,128)(2,1)S(1)}, u32[]{:S(2)}, u32[]{:S(2)}) collective-permute-start(bf16[4,288,128]{2,1,0:T(8,128)(2,1)S(1)} %pad_maximum_fusion.11), channel_id=1, source_target_pairs={{0,8},{2,10},{4,12},{6,14},{8,0},{10,2},{12,4},{14,6},{16,24},{18,... | collective-permute-start | bytes 884744 | tf_op jit(solution)/shard_map/ppermute | solution.py:51
  129.8 8.4 %collective-permute-start.36 = (bf16[4,288,128]{2,1,0:T(8,128)(2,1)S(1)}, bf16[4,288,128]{2,1,0:T(8,128)(2,1)S(1)}, u32[]{:S(2)}, u32[]{:S(2)}) collective-permute-start(bf16[4,288,128]{2,1,0:T(8,128)(2,1)S(1)} %pad_maximum_fusion.10), channel_id=1, source_target_pairs={{0,4},{2,6},{4,0},{6,2},{8,12},{10,14},{12,8},{14,10},{16,20},{18,... | collective-permute-start | bytes 884744 | tf_op jit(solution)/shard_map/ppermute | solution.py:51
  132.3 8.7 %collective-permute-start.32 = (bf16[2,128,384]{2,1,0:T(8,128)(2,1)S(1)}, bf16[2,128,384]{2,1,0:T(8,128)(2,1)S(1)}, u32[]{:S(2)}, u32[]{:S(2)}) collective-permute-start(bf16[2,128,384]{2,1,0:T(8,128)(2,1)S(1)} %pad_maximum_fusion.16), channel_id=1, source_target_pairs={{0,16},{2,18},{4,20},{6,22},{8,24},{10,26},{12,28},{14,30},{16,0},... | collective-permute-start | bytes 589832 | tf_op jit(solution)/shard_map/ppermute | solution.py:51
  138.4 8.9 %collective-permute-start.41 = (bf16[8,240,128]{2,1,0:T(8,128)(2,1)S(1)}, bf16[8,240,128]{2,1,0:T(8,128)(2,1)S(1)}, u32[]{:S(2)}, u32[]{:S(2)}) collective-permute-start(bf16[8,240,128]{2,1,0:T(8,128)(2,1)S(1)} %pad_maximum_fusion.5.refs_2_), channel_id=1, source_target_pairs={{0,8},{2,10},{4,12},{6,14},{8,0},{10,2},{12,4},{14,6},{16,24},{18,... | collective-permute-start | bytes 1474568 | tf_op jit(solution)/shard_map/ppermute | solution.py:51
  138.8 9.9 %collective-permute-start.40 = (bf16[8,288,128]{2,1,0:T(8,128)(2,1)S(1)}, bf16[8,288,128]{2,1,0:T(8,128)(2,1)S(1)}, u32[]{:S(2)}, u32[]{:S(2)}) collective-permute-start(bf16[8,288,128]{2,1,0:T(8,128)(2,1)S(1)} %pad_maximum_fusion.1.refs_1_), channel_id=1, source_target_pairs={{0,4},{2,6},{4,0},{6,2},{8,12},{10,14},{12,8},{14,10},{16,20},{18,... | collective-permute-start | bytes 1769480 | tf_op jit(solution)/shard_map/ppermute | solution.py:51
  139.3 9.9 %collective-permute-start.39 = (bf16[8,288,128]{2,1,0:T(8,128)(2,1)S(1)}, bf16[8,288,128]{2,1,0:T(8,128)(2,1)S(1)}, u32[]{:S(2)}, u32[]{:S(2)}) collective-permute-start(bf16[8,288,128]{2,1,0:T(8,128)(2,1)S(1)} %pad_maximum_fusion.refs_0_), channel_id=1, source_target_pairs={{0,2},{2,0},{4,6},{6,4},{8,10},{10,8},{12,14},{14,12},{16,18},{18,... | collective-permute-start | bytes 1769480 | tf_op jit(solution)/shard_map/ppermute | solution.py:51
  (37 other events, 301.8 us)

commit v3 on v2

--- a/solution.py
+++ b/solution.py
@@ -11,7 +11,6 @@
 EPN = 4
 RIM = 64
 EDGE_ROWS = 512
-LABEL = 16
 TILE = 32
 STREAMS = 3
 VMEM_LIMIT = 50 * 2**20
@@ -30,7 +29,7 @@
 
 
 def return_orders(orders):
-    heads = [(o[0], o[-2]) if s % 2 == 0 else (o[-2], o[0]) for s, o in enumerate(orders)]
+    heads = [(o[0], o[-2]) if s == 0 else (o[-2], o[0]) for s, o in enumerate(orders)]
     return [[*head, *o[1:-2], o[-1]] for head, o in zip(heads, orders)]
 
 
@@ -353,12 +352,10 @@
         for row in range(first, first + chunk):
             part = slice((row - first) * BLOCK, (row - first + 1) * BLOCK)
             h_ref[own_rows(row), :] += g_ref[part, :latent]
-            label = (host_ref[row] * blocks + remote_ref[row]).astype(F32)
             cut = latent
             for ref in slab_refs:
                 columns = ref.shape[2]
-                ref[row, :BLOCK] = g_ref[part, cut : cut + columns].astype(BF16)
-                ref[row, BLOCK:] = jnp.full((LABEL, columns), label, F32).astype(BF16)
+                ref[row] = g_ref[part, cut : cut + columns].astype(BF16)
                 cut += columns
     deal(total_ref, ckept_ref, csent_ref, orders[2], contact_parts, me)
     for copy in stores:
@@ -391,38 +388,28 @@
 
 
 def add_to_places(orders, blocks, half, me_ref, host_ref, remote_ref, *refs):
-    own, arrived, outs = refs[:2], refs[2:4], refs[4:]
+    named, own, arrived, outs = refs[:2], refs[2:4], refs[4:6], refs[6:]
     row_count = own[0].shape[0]
     width = outs[0].shape[2]
     views = [(0, slice(0, width)), (0, slice(width, 2 * width)), (1, slice(0, width))]
     me = me_ref[0]
     for s, order in enumerate(orders):
-        bits = len(order)
         out = outs[s]
         slots = out.shape[0]
-        first = half * slots
         array, columns = views[s]
-        marks = [arrived[array][i, BLOCK:, columns].astype(F32)[:1] for i in range(row_count)]
-
-        def step(slot, carry):
-            place = (first + slot) // blocks
-            offset = sum(((place >> (bits - 1 - i)) & 1) << b for i, b in enumerate(order))
-            label = ((me ^ offset) * blocks + slot % blocks).astype(F32)
-            value = jnp.zeros((BLOCK, out.shape[2]), F32)
-            for i, mark in enumerate(marks):
-                hit = jnp.where(mark == label, 1.0, 0.0)
-                value = value + arrived[array][i, :BLOCK, columns].astype(F32) * hit
-            out[slot] = value.astype(out.dtype)
-            return carry
-
-        lax.fori_loop(0, slots, step, 0)
-        for i in range(row_count):
-            spot = place_of(order, host_ref[i] ^ me) * blocks + remote_ref[i] - first
+        out[...] = jnp.zeros_like(out)
+
+        def place(source, i, host, remote):
+            spot = place_of(order, host ^ me) * blocks + remote - half * slots
 
             @pl.when(jnp.logical_and(spot >= 0, spot < slots))
             def _():
-                total = out[spot].astype(F32) + own[array][i, :BLOCK, columns].astype(F32)
+                total = out[spot].astype(F32) + source[array][i, :, columns].astype(F32)
                 out[spot] = total.astype(out.dtype)
+
+        for i in range(row_count):
+            place(own, i, host_ref[i], remote_ref[i])
+            place(arrived, i, named[array][i], named[array][row_count + i])
 
 
 def unpack(orders, parts, half_index, me_ref, *refs):
@@ -609,8 +596,8 @@
     parts = [parts_of(first.shape[0], second.shape[0], groups) for first, second in matrices]
     pair_rows = [chunk_rows(part) for part in parts]
     halves = lambda rows: [struct((half, rows * STREAMS, width), BF16)] * 2
-    labelled = [
-        struct((row_count, BLOCK + LABEL, columns), BF16) for columns in (2 * width, latent - 2 * width)
+    remote_parts = [
+        struct((row_count, BLOCK, columns), BF16) for columns in (2 * width, latent - 2 * width)
     ]
     b_out = [
         struct((node_count, latent), BF16),
@@ -618,7 +605,7 @@
         struct((node_count, latent), BF16),
         *halves(pair_rows[1]),
         *halves(pair_rows[2]),
-        *labelled,
+        *remote_parts,
     ]
     b_args = [node_state, mesh_sum, node_cot, w_node_in, w_node_out, w_contact_in, w_contact_out]
     contact_rows = row_count * BLOCK
@@ -709,13 +696,13 @@
     def places_call(half_index, dtype, own, arrived):
         return pl.pallas_call(
             functools.partial(add_to_places, back, blocks, half_index),
-            in_specs=[smem] * 3 + [pl.BlockSpec(memory_space=pltpu.VMEM)] * 4,
+            in_specs=[smem] * 5 + [pl.BlockSpec(memory_space=pltpu.VMEM)] * 4,
             out_specs=[pl.BlockSpec(memory_space=pltpu.VMEM)] * STREAMS,
             out_shape=[struct((slots, BLOCK, width), dtype)] * STREAMS,
             compiler_params=params(),
             cost_estimate=cost(0, 3 * 2**20),
             name="add_to_places",
-        )(me, host, contact_remote, *own, *arrived)
+        )(me, host, contact_remote, *named[:2], *own, *arrived)
 
     away_sent = places_call(1, BF16, away, away_arrived)
     n_arrived, c_arrived, *away_sent = joined([n_arrived, c_arrived, *away_sent])

time: 152 us -> 152 us (level)
  waiting for transfers between devices: 52.5 us -> 60 us
  starting transfers between devices: 57.6 us -> 53.7 us
    ppermute x38, waiting for transfers between devices: 50.3 us -> 57.8 us  [swap(): return lax.ppermute(value, 'dom', [(i, i ^ 1 << bit) for i in range(peers)])]
    ppermute x38, starting transfers between devices: 48.3 us -> 43.4 us  [swap(): return lax.ppermute(value, 'dom', [(i, i ^ 1 << bit) for i in range(peers)])]
  transfers between devices with their start and end apart: 42 -> 42, of which waited for: 23 -> 25; matrix products, arithmetic and copies ran while one was open for 3% -> 3% of each run, Pallas kernels for 12% -> 10%
where the time goes in v3:
time: 152 us; the launch traced here: 153 us
  waiting for transfers between devices  60 us (39%)
  starting transfers between devices  53.7 us (35%)
  Pallas kernels  29.2 us (19%)
  other arithmetic  6.8 us (4%)
    ppermute x38, waiting for transfers between devices, swap(): return lax.ppermute(value, 'dom', [(i, i ^ 1 << bit) for i in range(peers)])  57.8 us
    ppermute x38, starting transfers between devices, swap(): return lax.ppermute(value, 'dom', [(i, i ^ 1 << bit) for i in range(peers)])  43.4 us
    pallas_call x1, Pallas kernels, on_device(): pl.pallas_call(functools.partial(node_and_contact, orders, parts[1], part...  9.07 us
    ppermute x2, starting transfers between devices, swap_rims(): inner = lax.ppermute(jnp.where(odd, first, last), 'dom', both_ways[0])  8.77 us
    pallas_call x1, Pallas kernels, on_device(): pl.pallas_call(functools.partial(edge_backward, orders, parts[0]), grid=(...  7.93 us
    pallas_call x1, Pallas kernels, on_device(): pl.pallas_call(edge_forward, grid=(steps,), in_specs=[source_block, rim_b...  4.63 us
    pallas_call x2, Pallas kernels, on_device(): pl.pallas_call(functools.partial(unpack, orders, parts, side), in_specs=[...  4.22 us
  transfers between devices with their start and end apart: 42, of which 25 were waited for; matrix products, arithmetic and copies ran while one was open for 3% of the time, Pallas kernels for 10%

profile of v3, /device:TPU:0, one launch (start us, length us, event | category | flops | bytes accessed | tf_op | source)
XLA Modules:
  0.0 152.6 jit_solution(17599167903640251197)
XLA Ops:
  0.6 4.1 %collective-permute-start = (bf16[256,384]{1,0:T(8,128)(2,1)}, bf16[256,384]{1,0:T(8,128)(2,1)S(1)}, u32[]{:S(2)}, u32[]{:S(2)}) collective-permute-start(bf16[256,384]{1,0:T(8,128)(2,1)} %node_ref.3), channel_id=1, source_target_pairs={{0,16},{2,18},{4,20},{6,22},{8,24},{10,26},{12,28},{14,30},{16,0},... | collective-permute-start | bytes 589832 | tf_op jit(solution)/shard_map/ppermute | solution.py:50
  6.3 4.3 %collective-permute-start.1 = (bf16[64,384]{1,0:T(8,128)(2,1)S(1)}, bf16[64,384]{1,0:T(8,128)(2,1)S(1)}, u32[]{:S(2)}, u32[]{:S(2)}) collective-permute-start(bf16[64,384]{1,0:T(8,128)(2,1)S(1)} %get-tuple-element.224), channel_id=1, source_target_pairs={{0,2},{4,6},{8,10},{12,14},{16,18},{20,22},{24,26},{28,30},{2,0},{... | collective-permute-start | bytes 147464 | tf_op jit(solution)/shard_map/ppermute | solution.py:58
  28.9 4.6 %edge_forward.1 = (bf16[1024,384]{1,0:T(8,128)(2,1)}, bf16[256,384]{1,0:T(8,128)(2,1)S(1)}, f32[1024,384]{1,0:T(8,128)S(1)}, f32[1024,384]{1,0:T(8,128)}) custom-call(s32[2,1,512]{2,1,0:T(1,128)S(1)} %bitcast.30, bf16[64,384]{1,0:T(8,128)(2,1)S(1)} %get-tuple-element.126.before_ref, bf16[256,384]{1,0:T(8,128)(2,1)S(1)} %copy-done, ...), custom_call_target="tpu_custom_call" | custom-call | flops 1811939328 | bytes 6291456 | tf_op jit(solution)/shard_map/edge_forward/pallas_call | solution.py:530
  42.1 9.1 %node_and_contact.1 = (bf16[256,384]{1,0:T(8,128)(2,1)}, f32[256,384]{1,0:T(8,128)S(1)}, bf16[256,384]{1,0:T(8,128)(2,1)S(1)}, bf16[8,288,128]{2,1,0:T(8,128)(2,...) custom-call(s32[1]{0:T(128)} %bitcast.me_ref, ...), custom_call_target="tpu_custom_call" | custom-call | flops 2264924160 | bytes 12582912 | tf_op jit(solution)/shard_map/node_and_contact/pallas_call | solution.py:613
  54.9 7.9 %edge_backward.1 = (bf16[1024,384]{1,0:T(8,128)(2,1)}, f32[256,384]{1,0:T(8,128)S(1)}, bf16[64,384]{1,0:T(8,128)(2,1)S(1)}, bf16[64,384]{1,0:T(8,128)(2,1)S(1)},...) custom-call(s32[1]{0:T(128)} %bitcast.me_ref, s32[2,1,512]{2,1,0:T(1,128)S(1)} %bitcast.31, ...), custom_call_target="tpu_custom_call" | custom-call | flops 2415919104 | bytes 7864320 | tf_op jit(solution)/shard_map/edge_backward/pallas_call | solution.py:649
  67.1 2.1 %collective-permute-start.19 = (bf16[8,128,128]{2,1,0:T(8,128)(2,1)S(1)}, bf16[8,128,128]{2,1,0:T(8,128)(2,1)S(1)}, u32[]{:S(2)}, u32[]{:S(2)}) collective-permute-start(bf16[8,128,128]{2,1,0:T(8,128)(2,1)S(1)} %get-tuple-element.163), channel_id=1, source_target_pairs={{0,8},{2,10},{4,12},{6,14},{8,0},{10,2},{12,4},{14,6},{16,24},{18,... | collective-permute-start | bytes 786440 | tf_op jit(solution)/shard_map/ppermute | solution.py:50
  70.9 3.1 %collective-permute-done.19 = bf16[8,128,128]{2,1,0:T(8,128)(2,1)S(1)} collective-permute-done((bf16[8,128,128]{2,1,0:T(8,128)(2,1)S(1)}, bf16[8,128,128]{2,1,0:T(8,128)(2,1)S(1)}, u32[]{:S(2)}, u32[]{:S(2)}) %collective-permute-start.19) | collective-permute-done | bytes 262176 | tf_op jit(solution)/shard_map/ppermute | solution.py:50
  74.3 2.2 %collective-permute-done.20 = bf16[8,128,128]{2,1,0:T(8,128)(2,1)S(1)} collective-permute-done((bf16[8,128,128]{2,1,0:T(8,128)(2,1)S(1)}, bf16[8,128,128]{2,1,0:T(8,128)(2,1)S(1)}, u32[]{:S(2)}, u32[]{:S(2)}) %collective-permute-start.20) | collective-permute-done | bytes 262176 | tf_op jit(solution)/shard_map/ppermute | solution.py:50
  76.5 3.1 %collective-permute-done.21 = bf16[8,128,128]{2,1,0:T(8,128)(2,1)S(1)} collective-permute-done((bf16[8,128,128]{2,1,0:T(8,128)(2,1)S(1)}, bf16[8,128,128]{2,1,0:T(8,128)(2,1)S(1)}, u32[]{:S(2)}, u32[]{:S(2)}) %collective-permute-start.21) | collective-permute-done | bytes 262176 | tf_op jit(solution)/shard_map/ppermute | solution.py:50
  81.1 2.4 %collective-permute-start.24 = (bf16[4,416,128]{2,1,0:T(8,128)(2,1)S(1)}, bf16[4,416,128]{2,1,0:T(8,128)(2,1)S(1)}, u32[]{:S(2)}, u32[]{:S(2)}) collective-permute-start(bf16[4,416,128]{2,1,0:T(8,128)(2,1)S(1)} %pad_maximum_fusion.7), channel_id=1, source_target_pairs={{0,8},{2,10},{4,12},{6,14},{8,0},{10,2},{12,4},{14,6},{16,24},{18,... | collective-permute-start | bytes 1277960 | tf_op jit(solution)/shard_map/ppermute | solution.py:50
  84.5 7.5 %collective-permute-done.25 = bf16[4,368,128]{2,1,0:T(8,128)(2,1)S(1)} collective-permute-done((bf16[4,368,128]{2,1,0:T(8,128)(2,1)S(1)}, bf16[4,368,128]{2,1,0:T(8,128)(2,1)S(1)}, u32[]{:S(2)}, u32[]{:S(2)}) %collective-permute-start.25) | collective-permute-done | bytes 376864 | tf_op jit(solution)/shard_map/ppermute | solution.py:50
  94.5 2.7 %collective-permute-done.28 = bf16[2,240,128]{2,1,0:T(8,128)(2,1)S(1)} collective-permute-done((bf16[2,240,128]{2,1,0:T(8,128)(2,1)S(1)}, bf16[2,240,128]{2,1,0:T(8,128)(2,1)S(1)}, u32[]{:S(2)}, u32[]{:S(2)}) %collective-permute-start.28) | collective-permute-done | bytes 122912 | tf_op jit(solution)/shard_map/ppermute | solution.py:50
  97.2 2.5 %collective-permute-done.27 = bf16[2,288,128]{2,1,0:T(8,128)(2,1)S(1)} collective-permute-done((bf16[2,288,128]{2,1,0:T(8,128)(2,1)S(1)}, bf16[2,288,128]{2,1,0:T(8,128)(2,1)S(1)}, u32[]{:S(2)}, u32[]{:S(2)}) %collective-permute-start.27) | collective-permute-done | bytes 147488 | tf_op jit(solution)/shard_map/ppermute | solution.py:50
  99.7 3.3 %collective-permute-done.26 = bf16[2,288,128]{2,1,0:T(8,128)(2,1)S(1)} collective-permute-done((bf16[2,288,128]{2,1,0:T(8,128)(2,1)S(1)}, bf16[2,288,128]{2,1,0:T(8,128)(2,1)S(1)}, u32[]{:S(2)}, u32[]{:S(2)}) %collective-permute-start.26) | collective-permute-done | bytes 147488 | tf_op jit(solution)/shard_map/ppermute | solution.py:50
  105.3 4.5 %collective-permute-start.30 = (bf16[64,384]{1,0:T(8,128)(2,1)S(1)}, bf16[64,384]{1,0:T(8,128)(2,1)S(1)}, u32[]{:S(2)}, u32[]{:S(2)}) collective-permute-start(bf16[64,384]{1,0:T(8,128)(2,1)S(1)} %get-tuple-element.228), channel_id=1, source_target_pairs={{0,2},{4,6},{8,10},{12,14},{16,18},{20,22},{24,26},{28,30},{2,0},{... | collective-permute-start | bytes 147464 | tf_op jit(solution)/shard_map/ppermute | solution.py:58
  109.9 2.2 %collective-permute-done.30 = bf16[64,384]{1,0:T(8,128)(2,1)S(1)} collective-permute-done((bf16[64,384]{1,0:T(8,128)(2,1)S(1)}, bf16[64,384]{1,0:T(8,128)(2,1)S(1)}, u32[]{:S(2)}, u32[]{:S(2)}) %collective-permute-start.30) | collective-permute-done | bytes 49184 | tf_op jit(solution)/shard_map/ppermute | solution.py:58
  112.1 8.1 %collective-permute-done.29 = bf16[2,816,128]{2,1,0:T(8,128)(2,1)S(1)} collective-permute-done((bf16[2,816,128]{2,1,0:T(8,128)(2,1)S(1)}, bf16[2,816,128]{2,1,0:T(8,128)(2,1)S(1)}, u32[]{:S(2)}, u32[]{:S(2)}) %collective-permute-start.29) | collective-permute-done | bytes 417824 | tf_op jit(solution)/shard_map/ppermute | solution.py:50
  121.9 3.1 %collective-permute-start.35 = (bf16[2,240,128]{2,1,0:T(8,128)(2,1)S(1)}, bf16[2,240,128]{2,1,0:T(8,128)(2,1)S(1)}, u32[]{:S(2)}, u32[]{:S(2)}) collective-permute-start(bf16[2,240,128]{2,1,0:T(8,128)(2,1)S(1)} %slice.163), channel_id=1, source_target_pairs={{0,4},{2,6},{4,0},{6,2},{8,12},{10,14},{12,8},{14,10},{16,20},{18,... | collective-permute-start | bytes 368648 | tf_op jit(solution)/shard_map/ppermute | solution.py:50
  125.0 4.2 %collective-permute-done.35 = bf16[2,240,128]{2,1,0:T(8,128)(2,1)S(1)} collective-permute-done((bf16[2,240,128]{2,1,0:T(8,128)(2,1)S(1)}, bf16[2,240,128]{2,1,0:T(8,128)(2,1)S(1)}, u32[]{:S(2)}, u32[]{:S(2)}) %collective-permute-start.35) | collective-permute-done | bytes 122912 | tf_op jit(solution)/shard_map/ppermute | solution.py:50
  134.2 3.6 %collective-permute-done.38 = bf16[4,240,128]{2,1,0:T(8,128)(2,1)S(1)} collective-permute-done((bf16[4,240,128]{2,1,0:T(8,128)(2,1)S(1)}, bf16[4,240,128]{2,1,0:T(8,128)(2,1)S(1)}, u32[]{:S(2)}, u32[]{:S(2)}) %collective-permute-start.38) | collective-permute-done | bytes 245792 | tf_op jit(solution)/shard_map/ppermute | solution.py:50
  141.6 2.1 %unpack.2 = (f32[1152,384]{1,0:T(8,128)}, f32[384,384]{1,0:T(8,128)}, f32[1152,384]{1,0:T(8,128)}, f32[384,384]{1,0:T(8,128)}, f32[768,384]{1,0:T(8,128)}, /*index=5*/f32[384,384]{1,0:T(8,128)}) custom-call(s32[1]{0:T(128)} %bitcast.me_ref, bf16[8,288,128]{2,1,0:T(8,128)(2,1)S(1)} %pad_maximum_fusion.refs_0_, ...), custom_call_target="tpu_custom_call" | custom-call | bytes 8355840 | tf_op jit(solution)/shard_map/unpack/pallas_call | solution.py:745
  143.8 3.2 %collective-permute-done.41.refs_2_ = bf16[8,240,128]{2,1,0:T(8,128)(2,1)S(1)} collective-permute-done((bf16[8,240,128]{2,1,0:T(8,128)(2,1)S(1)}, bf16[8,240,128]{2,1,0:T(8,128)(2,1)S(1)}, u32[]{:S(2)}, u32[]{:S(2)}) %collective-permute-start.41) | collective-permute-done | bytes 491552 | tf_op jit(solution)/shard_map/ppermute | solution.py:50
  146.9 3.0 %collective-permute-done.40.refs_1_ = bf16[8,288,128]{2,1,0:T(8,128)(2,1)S(1)} collective-permute-done((bf16[8,288,128]{2,1,0:T(8,128)(2,1)S(1)}, bf16[8,288,128]{2,1,0:T(8,128)(2,1)S(1)}, u32[]{:S(2)}, u32[]{:S(2)}) %collective-permute-start.40) | collective-permute-done | bytes 589856 | tf_op jit(solution)/shard_map/ppermute | solution.py:50
  150.4 2.1 %unpack.3 = (f32[1152,384]{1,0:T(8,128)}, f32[384,384]{1,0:T(8,128)}, f32[1152,384]{1,0:T(8,128)}, f32[384,384]{1,0:T(8,128)}, f32[768,384]{1,0:T(8,128)}, /*index=5*/f32[384,384]{1,0:T(8,128)}) custom-call(s32[1]{0:T(128)} %bitcast.me_ref, ...), custom_call_target="tpu_custom_call", output_to_operand_aliasing={{0}: (4, {}), {1}: (5, {}), {2}: (6, {}), {3}: (7, {}), {4}... | custom-call | bytes 8355840 | tf_op jit(solution)/shard_map/unpack/pallas_call | solution.py:745
  (162 shorter events, 55.9 us)
Async XLA Ops:
  0.6 15.7 %collective-permute-start = (bf16[256,384]{1,0:T(8,128)(2,1)}, bf16[256,384]{1,0:T(8,128)(2,1)S(1)}, u32[]{:S(2)}, u32[]{:S(2)}) collective-permute-start(bf16[256,384]{1,0:T(8,128)(2,1)} %node_ref.3), channel_id=1, source_target_pairs={{0,16},{2,18},{4,20},{6,22},{8,24},{10,26},{12,28},{14,30},{16,0},... | collective-permute-start | bytes 589832 | tf_op jit(solution)/shard_map/ppermute | solution.py:50
  5.6 10.8 %collective-permute-start.2 = (bf16[64,384]{1,0:T(8,128)(2,1)S(1)}, bf16[64,384]{1,0:T(8,128)(2,1)S(1)}, u32[]{:S(2)}, u32[]{:S(2)}) collective-permute-start(bf16[64,384]{1,0:T(8,128)(2,1)S(1)} %get-tuple-element.223), channel_id=1, source_target_pairs={{2,4},{6,8},{10,12},{14,16},{18,20},{22,24},{26,28},{4,2},{8,6},{1... | collective-permute-start | bytes 147464 | tf_op jit(solution)/shard_map/ppermute | solution.py:59
  6.3 10.1 %collective-permute-start.1 = (bf16[64,384]{1,0:T(8,128)(2,1)S(1)}, bf16[64,384]{1,0:T(8,128)(2,1)S(1)}, u32[]{:S(2)}, u32[]{:S(2)}) collective-permute-start(bf16[64,384]{1,0:T(8,128)(2,1)S(1)} %get-tuple-element.224), channel_id=1, source_target_pairs={{0,2},{4,6},{8,10},{12,14},{16,18},{20,22},{24,26},{28,30},{2,0},{... | collective-permute-start | bytes 147464 | tf_op jit(solution)/shard_map/ppermute | solution.py:58
  24.7 8.8 %collective-permute-start.8 = (bf16[4,256,128]{2,1,0:T(8,128)(2,1)S(1)}, bf16[4,256,128]{2,1,0:T(8,128)(2,1)S(1)}, u32[]{:S(2)}, u32[]{:S(2)}) collective-permute-start(bf16[4,256,128]{2,1,0:T(8,128)(2,1)S(1)} %get-tuple-element.122), channel_id=1, source_target_pairs={{0,4},{2,6},{4,0},{6,2},{8,12},{10,14},{12,8},{14,10},{16,20},{18,... | collective-permute-start | bytes 786440 | tf_op jit(solution)/shard_map/ppermute | solution.py:50
  24.9 8.6 %collective-permute-start.9 = (bf16[4,256,128]{2,1,0:T(8,128)(2,1)S(1)}, bf16[4,256,128]{2,1,0:T(8,128)(2,1)S(1)}, u32[]{:S(2)}, u32[]{:S(2)}) collective-permute-start(bf16[4,256,128]{2,1,0:T(8,128)(2,1)S(1)} %get-tuple-element.123), channel_id=1, source_target_pairs={{0,8},{2,10},{4,12},{6,14},{8,0},{10,2},{12,4},{14,6},{16,24},{18,... | collective-permute-start | bytes 786440 | tf_op jit(solution)/shard_map/ppermute | solution.py:50
  51.1 16.0 %collective-permute-start.15 = (bf16[8,288,128]{2,1,0:T(8,128)(2,1)}, bf16[8,288,128]{2,1,0:T(8,128)(2,1)S(1)}, u32[]{:S(2)}, u32[]{:S(2)}) collective-permute-start(bf16[8,288,128]{2,1,0:T(8,128)(2,1)} %get-tuple-element.153), channel_id=1, source_target_pairs={{0,4},{2,6},{4,0},{6,2},{8,12},{10,14},{12,8},{14,10},{16,20},{18,... | collective-permute-start | bytes 1769480 | tf_op jit(solution)/shard_map/ppermute | solution.py:50
  51.3 15.9 %collective-permute-start.16 = (bf16[8,240,128]{2,1,0:T(8,128)(2,1)S(1)}, bf16[8,240,128]{2,1,0:T(8,128)(2,1)S(1)}, u32[]{:S(2)}, u32[]{:S(2)}) collective-permute-start(bf16[8,240,128]{2,1,0:T(8,128)(2,1)S(1)} %get-tuple-element.154), channel_id=1, source_target_pairs={{0,8},{2,10},{4,12},{6,14},{8,0},{10,2},{12,4},{14,6},{16,24},{18,... | collective-permute-start | bytes 1474568 | tf_op jit(solution)/shard_map/ppermute | solution.py:50
  53.2 11.0 %collective-permute-start.17 = (bf16[4,128,256]{2,1,0:T(8,128)(2,1)S(1)}, bf16[4,128,256]{2,1,0:T(8,128)(2,1)S(1)}, u32[]{:S(2)}, u32[]{:S(2)}) collective-permute-start(bf16[4,128,256]{2,1,0:T(8,128)(2,1)S(1)} %get-tuple-element.169.refs_2_), channel_id=1, source_target_pairs={{0,2},{2,0},{4,6},{6,4},{8,10},{10,8},{12,14},{14,12},{16,18},{18,... | collective-permute-start | bytes 786440 | tf_op jit(solution)/shard_map/ppermute | solution.py:50
  53.6 10.5 %collective-permute-start.18 = (bf16[4,128,128]{2,1,0:T(8,128)(2,1)S(1)}, bf16[4,128,128]{2,1,0:T(8,128)(2,1)S(1)}, u32[]{:S(2)}, u32[]{:S(2)}) collective-permute-start(bf16[4,128,128]{2,1,0:T(8,128)(2,1)S(1)} %get-tuple-element.170.refs_3_), channel_id=1, source_target_pairs={{0,4},{2,6},{4,0},{6,2},{8,12},{10,14},{12,8},{14,10},{16,20},{18,... | collective-permute-start | bytes 393224 | tf_op jit(solution)/shard_map/ppermute | solution.py:50
  64.2 10.1 %collective-permute-start.22 = (bf16[8,288,128]{2,1,0:T(8,128)(2,1)S(1)}, bf16[8,288,128]{2,1,0:T(8,128)(2,1)S(1)}, u32[]{:S(2)}, u32[]{:S(2)}) collective-permute-start(bf16[8,288,128]{2,1,0:T(8,128)(2,1)S(1)} %get-tuple-element.167), channel_id=1, source_target_pairs={{0,2},{2,0},{4,6},{6,4},{8,10},{10,8},{12,14},{14,12},{16,18},{18,... | collective-permute-start | bytes 1769480 | tf_op jit(solution)/shard_map/ppermute | solution.py:50
  69.6 10.0 %collective-permute-start.21 = (bf16[8,128,128]{2,1,0:T(8,128)(2,1)S(1)}, bf16[8,128,128]{2,1,0:T(8,128)(2,1)S(1)}, u32[]{:S(2)}, u32[]{:S(2)}) collective-permute-start(bf16[8,128,128]{2,1,0:T(8,128)(2,1)S(1)} %get-tuple-element.166), channel_id=1, source_target_pairs={{0,8},{2,10},{4,12},{6,14},{8,0},{10,2},{12,4},{14,6},{16,24},{18,... | collective-permute-start | bytes 786440 | tf_op jit(solution)/shard_map/ppermute | solution.py:50
  81.1 10.9 %collective-permute-start.24 = (bf16[4,416,128]{2,1,0:T(8,128)(2,1)S(1)}, bf16[4,416,128]{2,1,0:T(8,128)(2,1)S(1)}, u32[]{:S(2)}, u32[]{:S(2)}) collective-permute-start(bf16[4,416,128]{2,1,0:T(8,128)(2,1)S(1)} %pad_maximum_fusion.7), channel_id=1, source_target_pairs={{0,8},{2,10},{4,12},{6,14},{8,0},{10,2},{12,4},{14,6},{16,24},{18,... | collective-permute-start | bytes 1277960 | tf_op jit(solution)/shard_map/ppermute | solution.py:50
  83.5 8.4 %collective-permute-start.23 = (bf16[4,416,128]{2,1,0:T(8,128)(2,1)S(1)}, bf16[4,416,128]{2,1,0:T(8,128)(2,1)S(1)}, u32[]{:S(2)}, u32[]{:S(2)}) collective-permute-start(bf16[4,416,128]{2,1,0:T(8,128)(2,1)S(1)} %pad_maximum_fusion.6), channel_id=1, source_target_pairs={{0,4},{2,6},{4,0},{6,2},{8,12},{10,14},{12,8},{14,10},{16,20},{18,... | collective-permute-start | bytes 1277960 | tf_op jit(solution)/shard_map/ppermute | solution.py:50
  84.3 7.7 %collective-permute-start.25 = (bf16[4,368,128]{2,1,0:T(8,128)(2,1)S(1)}, bf16[4,368,128]{2,1,0:T(8,128)(2,1)S(1)}, u32[]{:S(2)}, u32[]{:S(2)}) collective-permute-start(bf16[4,368,128]{2,1,0:T(8,128)(2,1)S(1)} %pad_maximum_fusion.9), channel_id=1, source_target_pairs={{0,2},{2,0},{4,6},{6,4},{8,10},{10,8},{12,14},{14,12},{16,18},{18,... | collective-permute-start | bytes 1130504 | tf_op jit(solution)/shard_map/ppermute | solution.py:50
  93.9 9.2 %collective-permute-start.26 = (bf16[2,288,128]{2,1,0:T(8,128)(2,1)S(1)}, bf16[2,288,128]{2,1,0:T(8,128)(2,1)S(1)}, u32[]{:S(2)}, u32[]{:S(2)}) collective-permute-start(bf16[2,288,128]{2,1,0:T(8,128)(2,1)S(1)} %slice.245), channel_id=1, source_target_pairs={{0,8},{2,10},{4,12},{6,14},{8,0},{10,2},{12,4},{14,6},{16,24},{18,... | collective-permute-start | bytes 442376 | tf_op jit(solution)/shard_map/ppermute | solution.py:50
  103.2 17.0 %collective-permute-start.29 = (bf16[2,816,128]{2,1,0:T(8,128)(2,1)S(1)}, bf16[2,816,128]{2,1,0:T(8,128)(2,1)S(1)}, u32[]{:S(2)}, u32[]{:S(2)}) collective-permute-start(bf16[2,816,128]{2,1,0:T(8,128)(2,1)S(1)} %pad_maximum_fusion.8), channel_id=1, source_target_pairs={{0,16},{2,18},{4,20},{6,22},{8,24},{10,26},{12,28},{14,30},{16,0},... | collective-permute-start | bytes 1253384 | tf_op jit(solution)/shard_map/ppermute | solution.py:50
  120.3 8.9 %collective-permute-start.34 = (bf16[2,288,128]{2,1,0:T(8,128)(2,1)S(1)}, bf16[2,288,128]{2,1,0:T(8,128)(2,1)S(1)}, u32[]{:S(2)}, u32[]{:S(2)}) collective-permute-start(bf16[2,288,128]{2,1,0:T(8,128)(2,1)S(1)} %get-tuple-element.218), channel_id=1, source_target_pairs={{0,2},{2,0},{4,6},{6,4},{8,10},{10,8},{12,14},{14,12},{16,18},{18,... | collective-permute-start | bytes 442376 | tf_op jit(solution)/shard_map/ppermute | solution.py:50
  120.9 8.4 %collective-permute-start.33 = (bf16[2,288,128]{2,1,0:T(8,128)(2,1)S(1)}, bf16[2,288,128]{2,1,0:T(8,128)(2,1)S(1)}, u32[]{:S(2)}, u32[]{:S(2)}) collective-permute-start(bf16[2,288,128]{2,1,0:T(8,128)(2,1)S(1)} %get-tuple-element.219), channel_id=1, source_target_pairs={{0,8},{2,10},{4,12},{6,14},{8,0},{10,2},{12,4},{14,6},{16,24},{18,... | collective-permute-start | bytes 442376 | tf_op jit(solution)/shard_map/ppermute | solution.py:50
  129.3 8.5 %collective-permute-start.37 = (bf16[4,288,128]{2,1,0:T(8,128)(2,1)S(1)}, bf16[4,288,128]{2,1,0:T(8,128)(2,1)S(1)}, u32[]{:S(2)}, u32[]{:S(2)}) collective-permute-start(bf16[4,288,128]{2,1,0:T(8,128)(2,1)S(1)} %pad_maximum_fusion.11), channel_id=1, source_target_pairs={{0,8},{2,10},{4,12},{6,14},{8,0},{10,2},{12,4},{14,6},{16,24},{18,... | collective-permute-start | bytes 884744 | tf_op jit(solution)/shard_map/ppermute | solution.py:50
  129.4 8.4 %collective-permute-start.36 = (bf16[4,288,128]{2,1,0:T(8,128)(2,1)S(1)}, bf16[4,288,128]{2,1,0:T(8,128)(2,1)S(1)}, u32[]{:S(2)}, u32[]{:S(2)}) collective-permute-start(bf16[4,288,128]{2,1,0:T(8,128)(2,1)S(1)} %pad_maximum_fusion.10), channel_id=1, source_target_pairs={{0,4},{2,6},{4,0},{6,2},{8,12},{10,14},{12,8},{14,10},{16,20},{18,... | collective-permute-start | bytes 884744 | tf_op jit(solution)/shard_map/ppermute | solution.py:50
  132.1 8.7 %collective-permute-start.32 = (bf16[2,128,384]{2,1,0:T(8,128)(2,1)S(1)}, bf16[2,128,384]{2,1,0:T(8,128)(2,1)S(1)}, u32[]{:S(2)}, u32[]{:S(2)}) collective-permute-start(bf16[2,128,384]{2,1,0:T(8,128)(2,1)S(1)} %pad_maximum_fusion.16), channel_id=1, source_target_pairs={{0,16},{2,18},{4,20},{6,22},{8,24},{10,26},{12,28},{14,30},{16,0},... | collective-permute-start | bytes 589832 | tf_op jit(solution)/shard_map/ppermute | solution.py:50
  138.0 8.9 %collective-permute-start.41 = (bf16[8,240,128]{2,1,0:T(8,128)(2,1)S(1)}, bf16[8,240,128]{2,1,0:T(8,128)(2,1)S(1)}, u32[]{:S(2)}, u32[]{:S(2)}) collective-permute-start(bf16[8,240,128]{2,1,0:T(8,128)(2,1)S(1)} %pad_maximum_fusion.5.refs_2_), channel_id=1, source_target_pairs={{0,8},{2,10},{4,12},{6,14},{8,0},{10,2},{12,4},{14,6},{16,24},{18,... | collective-permute-start | bytes 1474568 | tf_op jit(solution)/shard_map/ppermute | solution.py:50
  140.0 9.9 %collective-permute-start.40 = (bf16[8,288,128]{2,1,0:T(8,128)(2,1)S(1)}, bf16[8,288,128]{2,1,0:T(8,128)(2,1)S(1)}, u32[]{:S(2)}, u32[]{:S(2)}) collective-permute-start(bf16[8,288,128]{2,1,0:T(8,128)(2,1)S(1)} %pad_maximum_fusion.1.refs_1_), channel_id=1, source_target_pairs={{0,4},{2,6},{4,0},{6,2},{8,12},{10,14},{12,8},{14,10},{16,20},{18,... | collective-permute-start | bytes 1769480 | tf_op jit(solution)/shard_map/ppermute | solution.py:50
  140.5 9.9 %collective-permute-start.39 = (bf16[8,288,128]{2,1,0:T(8,128)(2,1)S(1)}, bf16[8,288,128]{2,1,0:T(8,128)(2,1)S(1)}, u32[]{:S(2)}, u32[]{:S(2)}) collective-permute-start(bf16[8,288,128]{2,1,0:T(8,128)(2,1)S(1)} %pad_maximum_fusion.refs_0_), channel_id=1, source_target_pairs={{0,2},{2,0},{4,6},{6,4},{8,10},{10,8},{12,14},{14,12},{16,18},{18,... | collective-permute-start | bytes 1769480 | tf_op jit(solution)/shard_map/ppermute | solution.py:50
  (37 other events, 305.9 us)

commit v4 on v3

--- a/solution.py
+++ b/solution.py
@@ -387,25 +387,28 @@
         copy.wait()
 
 
-def add_to_places(orders, blocks, half, me_ref, host_ref, remote_ref, *refs):
+def add_to_places(orders, blocks, me_ref, host_ref, remote_ref, *refs):
     named, own, arrived, outs = refs[:2], refs[2:4], refs[4:6], refs[6:]
     row_count = own[0].shape[0]
     width = outs[0].shape[2]
     views = [(0, slice(0, width)), (0, slice(width, 2 * width)), (1, slice(0, width))]
     me = me_ref[0]
+    for out in outs:
+        out[...] = jnp.zeros_like(out)
     for s, order in enumerate(orders):
-        out = outs[s]
-        slots = out.shape[0]
         array, columns = views[s]
-        out[...] = jnp.zeros_like(out)
 
         def place(source, i, host, remote):
-            spot = place_of(order, host ^ me) * blocks + remote - half * slots
-
-            @pl.when(jnp.logical_and(spot >= 0, spot < slots))
-            def _():
-                total = out[spot].astype(F32) + source[array][i, :, columns].astype(F32)
-                out[spot] = total.astype(out.dtype)
+            spot = place_of(order, host ^ me) * blocks + remote
+            for half in range(2):
+                out = outs[half * STREAMS + s]
+                slots = out.shape[0]
+                here = spot - half * slots
+
+                @pl.when(jnp.logical_and(here >= 0, here < slots))
+                def _():
+                    total = out[here].astype(F32) + source[array][i, :, columns].astype(F32)
+                    out[here] = total.astype(out.dtype)
 
         for i in range(row_count):
             place(own, i, host_ref[i], remote_ref[i])
@@ -693,22 +696,20 @@
     *away_arrived, e_sent = joined([*away_arrived, e_sent])
     e_arrived = swap(e_sent, orders[0][0])
     slots = half * blocks // 2
-    def places_call(half_index, dtype, own, arrived):
-        return pl.pallas_call(
-            functools.partial(add_to_places, back, blocks, half_index),
-            in_specs=[smem] * 5 + [pl.BlockSpec(memory_space=pltpu.VMEM)] * 4,
-            out_specs=[pl.BlockSpec(memory_space=pltpu.VMEM)] * STREAMS,
-            out_shape=[struct((slots, BLOCK, width), dtype)] * STREAMS,
-            compiler_params=params(),
-            cost_estimate=cost(0, 3 * 2**20),
-            name="add_to_places",
-        )(me, host, contact_remote, *named[:2], *own, *arrived)
-
-    away_sent = places_call(1, BF16, away, away_arrived)
-    n_arrived, c_arrived, *away_sent = joined([n_arrived, c_arrived, *away_sent])
+    placed = pl.pallas_call(
+        functools.partial(add_to_places, back, blocks),
+        in_specs=[smem] * 5 + [pl.BlockSpec(memory_space=pltpu.VMEM)] * 4,
+        out_specs=[pl.BlockSpec(memory_space=pltpu.VMEM)] * (2 * STREAMS),
+        out_shape=[
+            struct((slots, BLOCK, width), dtype) for dtype in (F32, BF16) for _ in range(STREAMS)
+        ],
+        compiler_params=params(),
+        cost_estimate=cost(0, 6 * 2**20),
+        name="add_to_places",
+    )(me, host, contact_remote, *named[:2], *away, *away_arrived)
+    away_kept = placed[:STREAMS]
+    n_arrived, c_arrived, *away_sent = joined([n_arrived, c_arrived, *placed[STREAMS:]])
     arrived = [swap(sent, order[1]) for sent, order in zip(away_sent, back)]
-    arrived[0], *blocks_in = joined([arrived[0], *away, *away_arrived])
-    away_kept = places_call(0, F32, blocks_in[:2], blocks_in[2:])
     *arrived, e_arrived = joined([*arrived, e_arrived])
     away = list(zip(away_kept, away_sent))
     away = added(away, arrived)
@@ -728,14 +729,14 @@
     theirs, *rims = joined([swap(mine, far_bit), *swap_rims(low, high)])
     high, low = sorted_rims(*rims)
     pair = (mine.astype(F32) + theirs[::-1].astype(F32)).astype(BF16)
-    away_sent = jnp.concatenate([sent for _, sent in away], axis=2)
-    pair, away_sent = joined([pair, away_sent])
-    returned = swap(away_sent, far_bit)
     cuts = [sum(pair_rows[:s]) * STREAMS for s in range(STREAMS + 1)]
     sums = [pair[:, cuts[s] : cuts[s + 1]] for s in range(STREAMS)]
     for step in range(1, last):
         sums = both(sums, joined(gather_step(sums, orders, step)))
+    away_sent = jnp.concatenate([sent for _, sent in away], axis=2)
+    *sums, away_sent = joined([*sums, away_sent])
     gathered = list(zip(sums, gather_step(sums, orders, last)))
+    returned = swap(away_sent, far_bit)
     kept = jnp.concatenate([kept for kept, _ in away], axis=2)
     returned = (kept + returned.astype(F32)).reshape(node_count, latent)
     vmem = pl.BlockSpec(memory_space=pltpu.VMEM)

time: 152 us -> 149 us (0.980)
  waiting for transfers between devices: 60 us -> 57.8 us
    ppermute x38, waiting for transfers between devices: 57.8 us -> 55.6 us  [swap(): return lax.ppermute(value, 'dom', [(i, i ^ 1 << bit) for i in range(peers)])]
  transfers between devices with their start and end apart: 42 -> 42, of which waited for: 25 -> 26; matrix products, arithmetic and copies ran while one was open for 3% -> 3% of each run, Pallas kernels for 10% -> 11%
where the time goes in v4:
time: 149 us
  waiting for transfers between devices  57.8 us (39%)
  starting transfers between devices  53.1 us (36%)
  Pallas kernels  28.5 us (19%)
  other arithmetic  6.84 us (5%)
    ppermute x38, waiting for transfers between devices, swap(): return lax.ppermute(value, 'dom', [(i, i ^ 1 << bit) for i in range(peers)])  55.6 us
    ppermute x38, starting transfers between devices, swap(): return lax.ppermute(value, 'dom', [(i, i ^ 1 << bit) for i in range(peers)])  43.3 us
    pallas_call x1, Pallas kernels, on_device(): pl.pallas_call(functools.partial(node_and_contact, orders, parts[1], part...  9.07 us
    ppermute x2, starting transfers between devices, swap_rims(): inner = lax.ppermute(jnp.where(odd, first, last), 'dom', both_ways[0])  8.25 us
    pallas_call x1, Pallas kernels, on_device(): pl.pallas_call(functools.partial(edge_backward, orders, parts[0]), grid=(...  7.93 us
    pallas_call x1, Pallas kernels, on_device(): pl.pallas_call(edge_forward, grid=(steps,), in_specs=[source_block, rim_b...  4.64 us
    pallas_call x2, Pallas kernels, on_device(): pl.pallas_call(functools.partial(unpack, orders, parts, side), in_specs=[...  4.22 us
  transfers between devices with their start and end apart: 42, of which 26 were waited for; matrix products, arithmetic and copies ran while one was open for 3% of the time, Pallas kernels for 11%

profile of v4, /device:TPU:0, one launch (start us, length us, event | category | flops | bytes accessed | tf_op | source)
XLA Modules:
  0.0 149.1 jit_solution(305020407765300325)
XLA Ops:
  0.6 4.1 %collective-permute-start = (bf16[256,384]{1,0:T(8,128)(2,1)}, bf16[256,384]{1,0:T(8,128)(2,1)S(1)}, u32[]{:S(2)}, u32[]{:S(2)}) collective-permute-start(bf16[256,384]{1,0:T(8,128)(2,1)} %node_ref.3), channel_id=1, source_target_pairs={{0,16},{2,18},{4,20},{6,22},{8,24},{10,26},{12,28},{14,30},{16,0},... | collective-permute-start | bytes 589832 | tf_op jit(solution)/shard_map/ppermute | solution.py:50
  6.3 4.3 %collective-permute-start.1 = (bf16[64,384]{1,0:T(8,128)(2,1)S(1)}, bf16[64,384]{1,0:T(8,128)(2,1)S(1)}, u32[]{:S(2)}, u32[]{:S(2)}) collective-permute-start(bf16[64,384]{1,0:T(8,128)(2,1)S(1)} %get-tuple-element.218), channel_id=1, source_target_pairs={{0,2},{4,6},{8,10},{12,14},{16,18},{20,22},{24,26},{28,30},{2,0},{... | collective-permute-start | bytes 147464 | tf_op jit(solution)/shard_map/ppermute | solution.py:58
  28.9 4.6 %edge_forward.1 = (bf16[1024,384]{1,0:T(8,128)(2,1)}, bf16[256,384]{1,0:T(8,128)(2,1)S(1)}, f32[1024,384]{1,0:T(8,128)S(1)}, f32[1024,384]{1,0:T(8,128)}) custom-call(s32[2,1,512]{2,1,0:T(1,128)S(1)} %bitcast.29, bf16[64,384]{1,0:T(8,128)(2,1)S(1)} %get-tuple-element.123.before_ref, bf16[256,384]{1,0:T(8,128)(2,1)S(1)} %copy-done, ...), custom_call_target="tpu_custom_call" | custom-call | flops 1811939328 | bytes 6291456 | tf_op jit(solution)/shard_map/edge_forward/pallas_call | solution.py:533
  42.1 9.1 %node_and_contact.1 = (bf16[256,384]{1,0:T(8,128)(2,1)}, f32[256,384]{1,0:T(8,128)S(1)}, bf16[256,384]{1,0:T(8,128)(2,1)S(1)}, bf16[8,288,128]{2,1,0:T(8,128)(2,...) custom-call(s32[1]{0:T(128)} %bitcast.me_ref, ...), custom_call_target="tpu_custom_call" | custom-call | flops 2264924160 | bytes 12582912 | tf_op jit(solution)/shard_map/node_and_contact/pallas_call | solution.py:616
  54.9 7.9 %edge_backward.1 = (bf16[1024,384]{1,0:T(8,128)(2,1)}, f32[256,384]{1,0:T(8,128)S(1)}, bf16[64,384]{1,0:T(8,128)(2,1)S(1)}, bf16[64,384]{1,0:T(8,128)(2,1)S(1)},...) custom-call(s32[1]{0:T(128)} %bitcast.me_ref, s32[2,1,512]{2,1,0:T(1,128)S(1)} %bitcast.30, ...), custom_call_target="tpu_custom_call" | custom-call | flops 2415919104 | bytes 7864320 | tf_op jit(solution)/shard_map/edge_backward/pallas_call | solution.py:652
  67.1 2.1 %collective-permute-start.19 = (bf16[8,128,128]{2,1,0:T(8,128)(2,1)S(1)}, bf16[8,128,128]{2,1,0:T(8,128)(2,1)S(1)}, u32[]{:S(2)}, u32[]{:S(2)}) collective-permute-start(bf16[8,128,128]{2,1,0:T(8,128)(2,1)S(1)} %get-tuple-element.160), channel_id=1, source_target_pairs={{0,8},{2,10},{4,12},{6,14},{8,0},{10,2},{12,4},{14,6},{16,24},{18,... | collective-permute-start | bytes 786440 | tf_op jit(solution)/shard_map/ppermute | solution.py:50
  71.0 3.5 %collective-permute-done.22 = bf16[8,288,128]{2,1,0:T(8,128)(2,1)S(1)} collective-permute-done((bf16[8,288,128]{2,1,0:T(8,128)(2,1)S(1)}, bf16[8,288,128]{2,1,0:T(8,128)(2,1)S(1)}, u32[]{:S(2)}, u32[]{:S(2)}) %collective-permute-start.22) | collective-permute-done | bytes 589856 | tf_op jit(solution)/shard_map/ppermute | solution.py:50
  74.5 3.9 %collective-permute-done.20 = bf16[8,128,128]{2,1,0:T(8,128)(2,1)S(1)} collective-permute-done((bf16[8,128,128]{2,1,0:T(8,128)(2,1)S(1)}, bf16[8,128,128]{2,1,0:T(8,128)(2,1)S(1)}, u32[]{:S(2)}, u32[]{:S(2)}) %collective-permute-start.20) | collective-permute-done | bytes 262176 | tf_op jit(solution)/shard_map/ppermute | solution.py:50
  81.0 2.2 %collective-permute-start.24 = (bf16[4,416,128]{2,1,0:T(8,128)(2,1)S(1)}, bf16[4,416,128]{2,1,0:T(8,128)(2,1)S(1)}, u32[]{:S(2)}, u32[]{:S(2)}) collective-permute-start(bf16[4,416,128]{2,1,0:T(8,128)(2,1)S(1)} %pad_maximum_fusion.7), channel_id=1, source_target_pairs={{0,8},{2,10},{4,12},{6,14},{8,0},{10,2},{12,4},{14,6},{16,24},{18,... | collective-permute-start | bytes 1277960 | tf_op jit(solution)/shard_map/ppermute | solution.py:50
  83.4 7.5 %collective-permute-done.25 = bf16[4,368,128]{2,1,0:T(8,128)(2,1)S(1)} collective-permute-done((bf16[4,368,128]{2,1,0:T(8,128)(2,1)S(1)}, bf16[4,368,128]{2,1,0:T(8,128)(2,1)S(1)}, u32[]{:S(2)}, u32[]{:S(2)}) %collective-permute-start.25) | collective-permute-done | bytes 376864 | tf_op jit(solution)/shard_map/ppermute | solution.py:50
  91.3 2.0 %collective-permute-start.26 = (bf16[2,288,128]{2,1,0:T(8,128)(2,1)S(1)}, bf16[2,288,128]{2,1,0:T(8,128)(2,1)S(1)}, u32[]{:S(2)}, u32[]{:S(2)}) collective-permute-start(bf16[2,288,128]{2,1,0:T(8,128)(2,1)S(1)} %slice.248), channel_id=1, source_target_pairs={{0,8},{2,10},{4,12},{6,14},{8,0},{10,2},{12,4},{14,6},{16,24},{18,... | collective-permute-start | bytes 442376 | tf_op jit(solution)/shard_map/ppermute | solution.py:50
  94.4 3.9 %collective-permute-done.28 = bf16[2,240,128]{2,1,0:T(8,128)(2,1)S(1)} collective-permute-done((bf16[2,240,128]{2,1,0:T(8,128)(2,1)S(1)}, bf16[2,240,128]{2,1,0:T(8,128)(2,1)S(1)}, u32[]{:S(2)}, u32[]{:S(2)}) %collective-permute-start.28) | collective-permute-done | bytes 122912 | tf_op jit(solution)/shard_map/ppermute | solution.py:50
  98.4 3.4 %collective-permute-start.29 = (bf16[2,816,128]{2,1,0:T(8,128)(2,1)S(1)}, bf16[2,816,128]{2,1,0:T(8,128)(2,1)S(1)}, u32[]{:S(2)}, u32[]{:S(2)}) collective-permute-start(bf16[2,816,128]{2,1,0:T(8,128)(2,1)S(1)} %pad_maximum_fusion.8), channel_id=1, source_target_pairs={{0,16},{2,18},{4,20},{6,22},{8,24},{10,26},{12,28},{14,30},{16,0},... | collective-permute-start | bytes 1253384 | tf_op jit(solution)/shard_map/ppermute | solution.py:50
  102.8 4.0 %collective-permute-start.30 = (bf16[64,384]{1,0:T(8,128)(2,1)S(1)}, bf16[64,384]{1,0:T(8,128)(2,1)S(1)}, u32[]{:S(2)}, u32[]{:S(2)}) collective-permute-start(bf16[64,384]{1,0:T(8,128)(2,1)S(1)} %get-tuple-element.222), channel_id=1, source_target_pairs={{0,2},{4,6},{8,10},{12,14},{16,18},{20,22},{24,26},{28,30},{2,0},{... | collective-permute-start | bytes 147464 | tf_op jit(solution)/shard_map/ppermute | solution.py:58
  106.8 2.2 %collective-permute-done.30 = bf16[64,384]{1,0:T(8,128)(2,1)S(1)} collective-permute-done((bf16[64,384]{1,0:T(8,128)(2,1)S(1)}, bf16[64,384]{1,0:T(8,128)(2,1)S(1)}, u32[]{:S(2)}, u32[]{:S(2)}) %collective-permute-start.30) | collective-permute-done | bytes 49184 | tf_op jit(solution)/shard_map/ppermute | solution.py:58
  109.0 3.3 %collective-permute-done.29 = bf16[2,816,128]{2,1,0:T(8,128)(2,1)S(1)} collective-permute-done((bf16[2,816,128]{2,1,0:T(8,128)(2,1)S(1)}, bf16[2,816,128]{2,1,0:T(8,128)(2,1)S(1)}, u32[]{:S(2)}, u32[]{:S(2)}) %collective-permute-start.29) | collective-permute-done | bytes 417824 | tf_op jit(solution)/shard_map/ppermute | solution.py:50
  113.9 3.6 %collective-permute-start.33 = (bf16[2,288,128]{2,1,0:T(8,128)(2,1)S(1)}, bf16[2,288,128]{2,1,0:T(8,128)(2,1)S(1)}, u32[]{:S(2)}, u32[]{:S(2)}) collective-permute-start(bf16[2,288,128]{2,1,0:T(8,128)(2,1)S(1)} %get-tuple-element.212), channel_id=1, source_target_pairs={{0,2},{2,0},{4,6},{6,4},{8,10},{10,8},{12,14},{14,12},{16,18},{18,... | collective-permute-start | bytes 442376 | tf_op jit(solution)/shard_map/ppermute | solution.py:50
  118.4 2.2 %collective-permute-done.33 = bf16[2,288,128]{2,1,0:T(8,128)(2,1)S(1)} collective-permute-done((bf16[2,288,128]{2,1,0:T(8,128)(2,1)S(1)}, bf16[2,288,128]{2,1,0:T(8,128)(2,1)S(1)}, u32[]{:S(2)}, u32[]{:S(2)}) %collective-permute-start.33) | collective-permute-done | bytes 147488 | tf_op jit(solution)/shard_map/ppermute | solution.py:50
  120.6 3.0 %collective-permute-done.32 = bf16[2,288,128]{2,1,0:T(8,128)(2,1)S(1)} collective-permute-done((bf16[2,288,128]{2,1,0:T(8,128)(2,1)S(1)}, bf16[2,288,128]{2,1,0:T(8,128)(2,1)S(1)}, u32[]{:S(2)}, u32[]{:S(2)}) %collective-permute-start.32) | collective-permute-done | bytes 147488 | tf_op jit(solution)/shard_map/ppermute | solution.py:50
  124.0 7.3 %collective-permute-done.37 = bf16[4,240,128]{2,1,0:T(8,128)(2,1)S(1)} collective-permute-done((bf16[4,240,128]{2,1,0:T(8,128)(2,1)S(1)}, bf16[4,240,128]{2,1,0:T(8,128)(2,1)S(1)}, u32[]{:S(2)}, u32[]{:S(2)}) %collective-permute-start.37) | collective-permute-done | bytes 245792 | tf_op jit(solution)/shard_map/ppermute | solution.py:50
  137.5 2.1 %unpack.2 = (f32[1152,384]{1,0:T(8,128)}, f32[384,384]{1,0:T(8,128)}, f32[1152,384]{1,0:T(8,128)}, f32[384,384]{1,0:T(8,128)}, f32[768,384]{1,0:T(8,128)}, /*index=5*/f32[384,384]{1,0:T(8,128)}) custom-call(s32[1]{0:T(128)} %bitcast.me_ref, bf16[8,288,128]{2,1,0:T(8,128)(2,1)S(1)} %pad_maximum_fusion.refs_0_, ...), custom_call_target="tpu_custom_call" | custom-call | bytes 8355840 | tf_op jit(solution)/shard_map/unpack/pallas_call | solution.py:746
  139.6 2.6 %collective-permute-done.38 = bf16[2,128,384]{2,1,0:T(8,128)(2,1)S(1)} collective-permute-done((bf16[2,128,384]{2,1,0:T(8,128)(2,1)S(1)}, bf16[2,128,384]{2,1,0:T(8,128)(2,1)S(1)}, u32[]{:S(2)}, u32[]{:S(2)}) %collective-permute-start.38) | collective-permute-done | bytes 196640 | tf_op jit(solution)/shard_map/ppermute | solution.py:50
  143.1 2.2 %collective-permute-done.41.refs_2_ = bf16[8,240,128]{2,1,0:T(8,128)(2,1)S(1)} collective-permute-done((bf16[8,240,128]{2,1,0:T(8,128)(2,1)S(1)}, bf16[8,240,128]{2,1,0:T(8,128)(2,1)S(1)}, u32[]{:S(2)}, u32[]{:S(2)}) %collective-permute-start.41) | collective-permute-done | bytes 491552 | tf_op jit(solution)/shard_map/ppermute | solution.py:50
  146.8 2.1 %unpack.3 = (f32[1152,384]{1,0:T(8,128)}, f32[384,384]{1,0:T(8,128)}, f32[1152,384]{1,0:T(8,128)}, f32[384,384]{1,0:T(8,128)}, f32[768,384]{1,0:T(8,128)}, /*index=5*/f32[384,384]{1,0:T(8,128)}) custom-call(s32[1]{0:T(128)} %bitcast.me_ref, ...), custom_call_target="tpu_custom_call", output_to_operand_aliasing={{0}: (4, {}), {1}: (5, {}), {2}: (6, {}), {3}: (7, {}), {4}... | custom-call | bytes 8355840 | tf_op jit(solution)/shard_map/unpack/pallas_call | solution.py:746
  (161 shorter events, 54.5 us)
Async XLA Ops:
  0.6 15.7 %collective-permute-start = (bf16[256,384]{1,0:T(8,128)(2,1)}, bf16[256,384]{1,0:T(8,128)(2,1)S(1)}, u32[]{:S(2)}, u32[]{:S(2)}) collective-permute-start(bf16[256,384]{1,0:T(8,128)(2,1)} %node_ref.3), channel_id=1, source_target_pairs={{0,16},{2,18},{4,20},{6,22},{8,24},{10,26},{12,28},{14,30},{16,0},... | collective-permute-start | bytes 589832 | tf_op jit(solution)/shard_map/ppermute | solution.py:50
  5.6 10.8 %collective-permute-start.2 = (bf16[64,384]{1,0:T(8,128)(2,1)S(1)}, bf16[64,384]{1,0:T(8,128)(2,1)S(1)}, u32[]{:S(2)}, u32[]{:S(2)}) collective-permute-start(bf16[64,384]{1,0:T(8,128)(2,1)S(1)} %get-tuple-element.217), channel_id=1, source_target_pairs={{2,4},{6,8},{10,12},{14,16},{18,20},{22,24},{26,28},{4,2},{8,6},{1... | collective-permute-start | bytes 147464 | tf_op jit(solution)/shard_map/ppermute | solution.py:59
  6.3 10.1 %collective-permute-start.1 = (bf16[64,384]{1,0:T(8,128)(2,1)S(1)}, bf16[64,384]{1,0:T(8,128)(2,1)S(1)}, u32[]{:S(2)}, u32[]{:S(2)}) collective-permute-start(bf16[64,384]{1,0:T(8,128)(2,1)S(1)} %get-tuple-element.218), channel_id=1, source_target_pairs={{0,2},{4,6},{8,10},{12,14},{16,18},{20,22},{24,26},{28,30},{2,0},{... | collective-permute-start | bytes 147464 | tf_op jit(solution)/shard_map/ppermute | solution.py:58
  24.7 8.8 %collective-permute-start.8 = (bf16[4,256,128]{2,1,0:T(8,128)(2,1)S(1)}, bf16[4,256,128]{2,1,0:T(8,128)(2,1)S(1)}, u32[]{:S(2)}, u32[]{:S(2)}) collective-permute-start(bf16[4,256,128]{2,1,0:T(8,128)(2,1)S(1)} %get-tuple-element.119), channel_id=1, source_target_pairs={{0,4},{2,6},{4,0},{6,2},{8,12},{10,14},{12,8},{14,10},{16,20},{18,... | collective-permute-start | bytes 786440 | tf_op jit(solution)/shard_map/ppermute | solution.py:50
  24.9 8.6 %collective-permute-start.9 = (bf16[4,256,128]{2,1,0:T(8,128)(2,1)S(1)}, bf16[4,256,128]{2,1,0:T(8,128)(2,1)S(1)}, u32[]{:S(2)}, u32[]{:S(2)}) collective-permute-start(bf16[4,256,128]{2,1,0:T(8,128)(2,1)S(1)} %get-tuple-element.120), channel_id=1, source_target_pairs={{0,8},{2,10},{4,12},{6,14},{8,0},{10,2},{12,4},{14,6},{16,24},{18,... | collective-permute-start | bytes 786440 | tf_op jit(solution)/shard_map/ppermute | solution.py:50
  51.1 16.0 %collective-permute-start.15 = (bf16[8,288,128]{2,1,0:T(8,128)(2,1)}, bf16[8,288,128]{2,1,0:T(8,128)(2,1)S(1)}, u32[]{:S(2)}, u32[]{:S(2)}) collective-permute-start(bf16[8,288,128]{2,1,0:T(8,128)(2,1)} %get-tuple-element.150), channel_id=1, source_target_pairs={{0,4},{2,6},{4,0},{6,2},{8,12},{10,14},{12,8},{14,10},{16,20},{18,... | collective-permute-start | bytes 1769480 | tf_op jit(solution)/shard_map/ppermute | solution.py:50
  51.3 15.8 %collective-permute-start.16 = (bf16[8,240,128]{2,1,0:T(8,128)(2,1)S(1)}, bf16[8,240,128]{2,1,0:T(8,128)(2,1)S(1)}, u32[]{:S(2)}, u32[]{:S(2)}) collective-permute-start(bf16[8,240,128]{2,1,0:T(8,128)(2,1)S(1)} %get-tuple-element.151), channel_id=1, source_target_pairs={{0,8},{2,10},{4,12},{6,14},{8,0},{10,2},{12,4},{14,6},{16,24},{18,... | collective-permute-start | bytes 1474568 | tf_op jit(solution)/shard_map/ppermute | solution.py:50
  53.2 11.0 %collective-permute-start.17 = (bf16[4,128,256]{2,1,0:T(8,128)(2,1)S(1)}, bf16[4,128,256]{2,1,0:T(8,128)(2,1)S(1)}, u32[]{:S(2)}, u32[]{:S(2)}) collective-permute-start(bf16[4,128,256]{2,1,0:T(8,128)(2,1)S(1)} %get-tuple-element.152.refs_2_), channel_id=1, source_target_pairs={{0,2},{2,0},{4,6},{6,4},{8,10},{10,8},{12,14},{14,12},{16,18},{18,... | collective-permute-start | bytes 786440 | tf_op jit(solution)/shard_map/ppermute | solution.py:50
  53.6 10.5 %collective-permute-start.18 = (bf16[4,128,128]{2,1,0:T(8,128)(2,1)S(1)}, bf16[4,128,128]{2,1,0:T(8,128)(2,1)S(1)}, u32[]{:S(2)}, u32[]{:S(2)}) collective-permute-start(bf16[4,128,128]{2,1,0:T(8,128)(2,1)S(1)} %get-tuple-element.153.refs_3_), channel_id=1, source_target_pairs={{0,4},{2,6},{4,0},{6,2},{8,12},{10,14},{12,8},{14,10},{16,20},{18,... | collective-permute-start | bytes 393224 | tf_op jit(solution)/shard_map/ppermute | solution.py:50
  64.2 10.2 %collective-permute-start.22 = (bf16[8,288,128]{2,1,0:T(8,128)(2,1)S(1)}, bf16[8,288,128]{2,1,0:T(8,128)(2,1)S(1)}, u32[]{:S(2)}, u32[]{:S(2)}) collective-permute-start(bf16[8,288,128]{2,1,0:T(8,128)(2,1)S(1)} %get-tuple-element.163), channel_id=1, source_target_pairs={{0,2},{2,0},{4,6},{6,4},{8,10},{10,8},{12,14},{14,12},{16,18},{18,... | collective-permute-start | bytes 1769480 | tf_op jit(solution)/shard_map/ppermute | solution.py:50
  67.1 7.3 %collective-permute-start.19 = (bf16[8,128,128]{2,1,0:T(8,128)(2,1)S(1)}, bf16[8,128,128]{2,1,0:T(8,128)(2,1)S(1)}, u32[]{:S(2)}, u32[]{:S(2)}) collective-permute-start(bf16[8,128,128]{2,1,0:T(8,128)(2,1)S(1)} %get-tuple-element.160), channel_id=1, source_target_pairs={{0,8},{2,10},{4,12},{6,14},{8,0},{10,2},{12,4},{14,6},{16,24},{18,... | collective-permute-start | bytes 786440 | tf_op jit(solution)/shard_map/ppermute | solution.py:50
  69.3 9.1 %collective-permute-start.20 = (bf16[8,128,128]{2,1,0:T(8,128)(2,1)S(1)}, bf16[8,128,128]{2,1,0:T(8,128)(2,1)S(1)}, u32[]{:S(2)}, u32[]{:S(2)}) collective-permute-start(bf16[8,128,128]{2,1,0:T(8,128)(2,1)S(1)} %get-tuple-element.161), channel_id=1, source_target_pairs={{0,4},{2,6},{4,0},{6,2},{8,12},{10,14},{12,8},{14,10},{16,20},{18,... | collective-permute-start | bytes 786440 | tf_op jit(solution)/shard_map/ppermute | solution.py:50
  69.6 10.5 %collective-permute-start.21 = (bf16[8,128,128]{2,1,0:T(8,128)(2,1)S(1)}, bf16[8,128,128]{2,1,0:T(8,128)(2,1)S(1)}, u32[]{:S(2)}, u32[]{:S(2)}) collective-permute-start(bf16[8,128,128]{2,1,0:T(8,128)(2,1)S(1)} %get-tuple-element.162), channel_id=1, source_target_pairs={{0,8},{2,10},{4,12},{6,14},{8,0},{10,2},{12,4},{14,6},{16,24},{18,... | collective-permute-start | bytes 786440 | tf_op jit(solution)/shard_map/ppermute | solution.py:50
  80.6 10.3 %collective-permute-start.23 = (bf16[4,416,128]{2,1,0:T(8,128)(2,1)S(1)}, bf16[4,416,128]{2,1,0:T(8,128)(2,1)S(1)}, u32[]{:S(2)}, u32[]{:S(2)}) collective-permute-start(bf16[4,416,128]{2,1,0:T(8,128)(2,1)S(1)} %pad_maximum_fusion.6), channel_id=1, source_target_pairs={{0,4},{2,6},{4,0},{6,2},{8,12},{10,14},{12,8},{14,10},{16,20},{18,... | collective-permute-start | bytes 1277960 | tf_op jit(solution)/shard_map/ppermute | solution.py:50
  81.0 9.9 %collective-permute-start.24 = (bf16[4,416,128]{2,1,0:T(8,128)(2,1)S(1)}, bf16[4,416,128]{2,1,0:T(8,128)(2,1)S(1)}, u32[]{:S(2)}, u32[]{:S(2)}) collective-permute-start(bf16[4,416,128]{2,1,0:T(8,128)(2,1)S(1)} %pad_maximum_fusion.7), channel_id=1, source_target_pairs={{0,8},{2,10},{4,12},{6,14},{8,0},{10,2},{12,4},{14,6},{16,24},{18,... | collective-permute-start | bytes 1277960 | tf_op jit(solution)/shard_map/ppermute | solution.py:50
  83.2 7.7 %collective-permute-start.25 = (bf16[4,368,128]{2,1,0:T(8,128)(2,1)S(1)}, bf16[4,368,128]{2,1,0:T(8,128)(2,1)S(1)}, u32[]{:S(2)}, u32[]{:S(2)}) collective-permute-start(bf16[4,368,128]{2,1,0:T(8,128)(2,1)S(1)} %pad_maximum_fusion.9), channel_id=1, source_target_pairs={{0,2},{2,0},{4,6},{6,4},{8,10},{10,8},{12,14},{14,12},{16,18},{18,... | collective-permute-start | bytes 1130504 | tf_op jit(solution)/shard_map/ppermute | solution.py:50
  98.4 13.9 %collective-permute-start.29 = (bf16[2,816,128]{2,1,0:T(8,128)(2,1)S(1)}, bf16[2,816,128]{2,1,0:T(8,128)(2,1)S(1)}, u32[]{:S(2)}, u32[]{:S(2)}) collective-permute-start(bf16[2,816,128]{2,1,0:T(8,128)(2,1)S(1)} %pad_maximum_fusion.8), channel_id=1, source_target_pairs={{0,16},{2,18},{4,20},{6,22},{8,24},{10,26},{12,28},{14,30},{16,0},... | collective-permute-start | bytes 1253384 | tf_op jit(solution)/shard_map/ppermute | solution.py:50
  123.6 7.7 %collective-permute-start.37 = (bf16[4,240,128]{2,1,0:T(8,128)(2,1)S(1)}, bf16[4,240,128]{2,1,0:T(8,128)(2,1)S(1)}, u32[]{:S(2)}, u32[]{:S(2)}) collective-permute-start(bf16[4,240,128]{2,1,0:T(8,128)(2,1)S(1)} %pad_maximum_fusion.15), channel_id=1, source_target_pairs={{0,2},{2,0},{4,6},{6,4},{8,10},{10,8},{12,14},{14,12},{16,18},{18,... | collective-permute-start | bytes 737288 | tf_op jit(solution)/shard_map/ppermute | solution.py:50
  123.8 9.4 %collective-permute-start.36 = (bf16[4,288,128]{2,1,0:T(8,128)(2,1)S(1)}, bf16[4,288,128]{2,1,0:T(8,128)(2,1)S(1)}, u32[]{:S(2)}, u32[]{:S(2)}) collective-permute-start(bf16[4,288,128]{2,1,0:T(8,128)(2,1)S(1)} %pad_maximum_fusion.11), channel_id=1, source_target_pairs={{0,8},{2,10},{4,12},{6,14},{8,0},{10,2},{12,4},{14,6},{16,24},{18,... | collective-permute-start | bytes 884744 | tf_op jit(solution)/shard_map/ppermute | solution.py:50
  123.8 9.4 %collective-permute-start.35 = (bf16[4,288,128]{2,1,0:T(8,128)(2,1)S(1)}, bf16[4,288,128]{2,1,0:T(8,128)(2,1)S(1)}, u32[]{:S(2)}, u32[]{:S(2)}) collective-permute-start(bf16[4,288,128]{2,1,0:T(8,128)(2,1)S(1)} %pad_maximum_fusion.10), channel_id=1, source_target_pairs={{0,4},{2,6},{4,0},{6,2},{8,12},{10,14},{12,8},{14,10},{16,20},{18,... | collective-permute-start | bytes 884744 | tf_op jit(solution)/shard_map/ppermute | solution.py:50
  133.4 8.8 %collective-permute-start.38 = (bf16[2,128,384]{2,1,0:T(8,128)(2,1)S(1)}, bf16[2,128,384]{2,1,0:T(8,128)(2,1)S(1)}, u32[]{:S(2)}, u32[]{:S(2)}) collective-permute-start(bf16[2,128,384]{2,1,0:T(8,128)(2,1)S(1)} %pad_maximum_fusion.16), channel_id=1, source_target_pairs={{0,16},{2,18},{4,20},{6,22},{8,24},{10,26},{12,28},{14,30},{16,0},... | collective-permute-start | bytes 589832 | tf_op jit(solution)/shard_map/ppermute | solution.py:50
  134.9 10.4 %collective-permute-start.41 = (bf16[8,240,128]{2,1,0:T(8,128)(2,1)S(1)}, bf16[8,240,128]{2,1,0:T(8,128)(2,1)S(1)}, u32[]{:S(2)}, u32[]{:S(2)}) collective-permute-start(bf16[8,240,128]{2,1,0:T(8,128)(2,1)S(1)} %pad_maximum_fusion.5.refs_2_), channel_id=1, source_target_pairs={{0,8},{2,10},{4,12},{6,14},{8,0},{10,2},{12,4},{14,6},{16,24},{18,... | collective-permute-start | bytes 1474568 | tf_op jit(solution)/shard_map/ppermute | solution.py:50
  135.6 9.9 %collective-permute-start.39 = (bf16[8,288,128]{2,1,0:T(8,128)(2,1)S(1)}, bf16[8,288,128]{2,1,0:T(8,128)(2,1)S(1)}, u32[]{:S(2)}, u32[]{:S(2)}) collective-permute-start(bf16[8,288,128]{2,1,0:T(8,128)(2,1)S(1)} %pad_maximum_fusion.refs_0_), channel_id=1, source_target_pairs={{0,2},{2,0},{4,6},{6,4},{8,10},{10,8},{12,14},{14,12},{16,18},{18,... | collective-permute-start | bytes 1769480 | tf_op jit(solution)/shard_map/ppermute | solution.py:50
  136.9 9.9 %collective-permute-start.40 = (bf16[8,288,128]{2,1,0:T(8,128)(2,1)S(1)}, bf16[8,288,128]{2,1,0:T(8,128)(2,1)S(1)}, u32[]{:S(2)}, u32[]{:S(2)}) collective-permute-start(bf16[8,288,128]{2,1,0:T(8,128)(2,1)S(1)} %pad_maximum_fusion.1.refs_1_), channel_id=1, source_target_pairs={{0,4},{2,6},{4,0},{6,2},{8,12},{10,14},{12,8},{14,10},{16,20},{18,... | collective-permute-start | bytes 1769480 | tf_op jit(solution)/shard_map/ppermute | solution.py:50
  (37 other events, 238.4 us)

commit v5 on v4

--- a/solution.py
+++ b/solution.py
@@ -693,7 +693,7 @@
     )(me, sources, before, node_state, after, edge_state, e_pre, e_linear, edge_cot, d_mesh,
       partial_h, w_edge_in, w_edge_out)
 
-    *away_arrived, e_sent = joined([*away_arrived, e_sent])
+    away_arrived[0], e_sent = joined([away_arrived[0], e_sent])
     e_arrived = swap(e_sent, orders[0][0])
     slots = half * blocks // 2
     placed = pl.pallas_call(

time: 149 us -> 148 us (level)
  waiting for transfers between devices: 57.8 us -> 52.3 us
  starting transfers between devices: 53.1 us -> 57.5 us
    ppermute x38, waiting for transfers between devices: 55.6 us -> 50.1 us  [swap(): return lax.ppermute(value, 'dom', [(i, i ^ 1 << bit) for i in range(peers)])]
    ppermute x38, starting transfers between devices: 43.3 us -> 46.9 us  [swap(): return lax.ppermute(value, 'dom', [(i, i ^ 1 << bit) for i in range(peers)])]
where the time goes in v5:
time: 148 us
  starting transfers between devices  57.5 us (39%)
  waiting for transfers between devices  52.3 us (35%)
  Pallas kernels  28.5 us (19%)
  other arithmetic  6.84 us (5%)
    ppermute x38, waiting for transfers between devices, swap(): return lax.ppermute(value, 'dom', [(i, i ^ 1 << bit) for i in range(peers)])  50.1 us
    ppermute x38, starting transfers between devices, swap(): return lax.ppermute(value, 'dom', [(i, i ^ 1 << bit) for i in range(peers)])  46.9 us
    pallas_call x1, Pallas kernels, on_device(): pl.pallas_call(functools.partial(node_and_contact, orders, parts[1], part...  9.07 us
    ppermute x2, starting transfers between devices, swap_rims(): inner = lax.ppermute(jnp.where(odd, first, last), 'dom', both_ways[0])  9.06 us
    pallas_call x1, Pallas kernels, on_device(): pl.pallas_call(functools.partial(edge_backward, orders, parts[0]), grid=(...  7.93 us
    pallas_call x1, Pallas kernels, on_device(): pl.pallas_call(edge_forward, grid=(steps,), in_specs=[source_block, rim_b...  4.64 us
    pallas_call x2, Pallas kernels, on_device(): pl.pallas_call(functools.partial(unpack, orders, parts, side), in_specs=[...  4.22 us
  transfers between devices with their start and end apart: 42, of which 26 were waited for; matrix products, arithmetic and copies ran while one was open for 3% of the time, Pallas kernels for 11%

profile of v5, /device:TPU:0, one launch (start us, length us, event | category | flops | bytes accessed | tf_op | source)
XLA Modules:
  0.0 148.0 jit_solution(8322000542814714012)
XLA Ops:
  0.6 4.1 %collective-permute-start = (bf16[256,384]{1,0:T(8,128)(2,1)}, bf16[256,384]{1,0:T(8,128)(2,1)S(1)}, u32[]{:S(2)}, u32[]{:S(2)}) collective-permute-start(bf16[256,384]{1,0:T(8,128)(2,1)} %node_ref.3), channel_id=1, source_target_pairs={{0,16},{2,18},{4,20},{6,22},{8,24},{10,26},{12,28},{14,30},{16,0},... | collective-permute-start | bytes 589832 | tf_op jit(solution)/shard_map/ppermute | solution.py:50
  6.3 4.3 %collective-permute-start.1 = (bf16[64,384]{1,0:T(8,128)(2,1)S(1)}, bf16[64,384]{1,0:T(8,128)(2,1)S(1)}, u32[]{:S(2)}, u32[]{:S(2)}) collective-permute-start(bf16[64,384]{1,0:T(8,128)(2,1)S(1)} %get-tuple-element.216), channel_id=1, source_target_pairs={{0,2},{4,6},{8,10},{12,14},{16,18},{20,22},{24,26},{28,30},{2,0},{... | collective-permute-start | bytes 147464 | tf_op jit(solution)/shard_map/ppermute | solution.py:58
  24.9 1.9 %collective-permute-start.9 = (bf16[4,256,128]{2,1,0:T(8,128)(2,1)S(1)}, bf16[4,256,128]{2,1,0:T(8,128)(2,1)S(1)}, u32[]{:S(2)}, u32[]{:S(2)}) collective-permute-start(bf16[4,256,128]{2,1,0:T(8,128)(2,1)S(1)} %get-tuple-element.119), channel_id=1, source_target_pairs={{0,8},{2,10},{4,12},{6,14},{8,0},{10,2},{12,4},{14,6},{16,24},{18,... | collective-permute-start | bytes 786440 | tf_op jit(solution)/shard_map/ppermute | solution.py:50
  28.9 4.6 %edge_forward.1 = (bf16[1024,384]{1,0:T(8,128)(2,1)}, bf16[256,384]{1,0:T(8,128)(2,1)S(1)}, f32[1024,384]{1,0:T(8,128)S(1)}, f32[1024,384]{1,0:T(8,128)}) custom-call(s32[2,1,512]{2,1,0:T(1,128)S(1)} %bitcast.29, bf16[64,384]{1,0:T(8,128)(2,1)S(1)} %get-tuple-element.122.before_ref, bf16[256,384]{1,0:T(8,128)(2,1)S(1)} %copy-done, ...), custom_call_target="tpu_custom_call" | custom-call | flops 1811939328 | bytes 6291456 | tf_op jit(solution)/shard_map/edge_forward/pallas_call | solution.py:533
  35.1 1.9 %collective-permute-start.13 = (bf16[4,128,128]{2,1,0:T(8,128)(2,1)S(1)}, bf16[4,128,128]{2,1,0:T(8,128)(2,1)S(1)}, u32[]{:S(2)}, u32[]{:S(2)}) collective-permute-start(bf16[4,128,128]{2,1,0:T(8,128)(2,1)S(1)} %get-tuple-element.136), channel_id=1, source_target_pairs={{0,4},{2,6},{4,0},{6,2},{8,12},{10,14},{12,8},{14,10},{16,20},{18,... | collective-permute-start | bytes 393224 | tf_op jit(solution)/shard_map/ppermute | solution.py:50
  40.1 1.9 %collective-permute-done.14.refs_5_.refs_11_.refs_17_.refs_23_ = bf16[4,128,128]{2,1,0:T(8,128)(2,1)S(1)} collective-permute-done((bf16[4,128,128]{2,1,0:T(8,128)(2,1)S(1)}, bf16[4,128,128]{2,1,0:T(8,128)(2,1)S(1)}, u32[]{:S(2)}, u32[]{:S(2)}) %collective-permute-start.14) | collective-permute-done | bytes 131104 | tf_op jit(solution)/shard_map/ppermute | solution.py:50
  42.1 9.1 %node_and_contact.1 = (bf16[256,384]{1,0:T(8,128)(2,1)}, f32[256,384]{1,0:T(8,128)S(1)}, bf16[256,384]{1,0:T(8,128)(2,1)S(1)}, bf16[8,288,128]{2,1,0:T(8,128)(2,...) custom-call(s32[1]{0:T(128)} %bitcast.me_ref, ...), custom_call_target="tpu_custom_call" | custom-call | flops 2264924160 | bytes 12582912 | tf_op jit(solution)/shard_map/node_and_contact/pallas_call | solution.py:616
  51.3 1.9 %collective-permute-start.16 = (bf16[8,240,128]{2,1,0:T(8,128)(2,1)S(1)}, bf16[8,240,128]{2,1,0:T(8,128)(2,1)S(1)}, u32[]{:S(2)}, u32[]{:S(2)}) collective-permute-start(bf16[8,240,128]{2,1,0:T(8,128)(2,1)S(1)} %get-tuple-element.150), channel_id=1, source_target_pairs={{0,8},{2,10},{4,12},{6,14},{8,0},{10,2},{12,4},{14,6},{16,24},{18,... | collective-permute-start | bytes 1474568 | tf_op jit(solution)/shard_map/ppermute | solution.py:50
  54.9 7.9 %edge_backward.1 = (bf16[1024,384]{1,0:T(8,128)(2,1)}, f32[256,384]{1,0:T(8,128)S(1)}, bf16[64,384]{1,0:T(8,128)(2,1)S(1)}, bf16[64,384]{1,0:T(8,128)(2,1)S(1)},...) custom-call(s32[1]{0:T(128)} %bitcast.me_ref, s32[2,1,512]{2,1,0:T(1,128)S(1)} %bitcast.30, ...), custom_call_target="tpu_custom_call" | custom-call | flops 2415919104 | bytes 7864320 | tf_op jit(solution)/shard_map/edge_backward/pallas_call | solution.py:652
  70.8 1.9 %collective-permute-done.22 = bf16[8,288,128]{2,1,0:T(8,128)(2,1)S(1)} collective-permute-done((bf16[8,288,128]{2,1,0:T(8,128)(2,1)S(1)}, bf16[8,288,128]{2,1,0:T(8,128)(2,1)S(1)}, u32[]{:S(2)}, u32[]{:S(2)}) %collective-permute-start.22) | collective-permute-done | bytes 589856 | tf_op jit(solution)/shard_map/ppermute | solution.py:50
  72.7 2.8 %collective-permute-done.19 = bf16[8,128,128]{2,1,0:T(8,128)(2,1)S(1)} collective-permute-done((bf16[8,128,128]{2,1,0:T(8,128)(2,1)S(1)}, bf16[8,128,128]{2,1,0:T(8,128)(2,1)S(1)}, u32[]{:S(2)}, u32[]{:S(2)}) %collective-permute-start.19) | collective-permute-done | bytes 262176 | tf_op jit(solution)/shard_map/ppermute | solution.py:50
  77.1 3.6 %collective-permute-done.21 = bf16[8,128,128]{2,1,0:T(8,128)(2,1)S(1)} collective-permute-done((bf16[8,128,128]{2,1,0:T(8,128)(2,1)S(1)}, bf16[8,128,128]{2,1,0:T(8,128)(2,1)S(1)}, u32[]{:S(2)}, u32[]{:S(2)}) %collective-permute-start.21) | collective-permute-done | bytes 262176 | tf_op jit(solution)/shard_map/ppermute | solution.py:50
  83.0 7.1 %collective-permute-done.25 = bf16[4,368,128]{2,1,0:T(8,128)(2,1)S(1)} collective-permute-done((bf16[4,368,128]{2,1,0:T(8,128)(2,1)S(1)}, bf16[4,368,128]{2,1,0:T(8,128)(2,1)S(1)}, u32[]{:S(2)}, u32[]{:S(2)}) %collective-permute-start.25) | collective-permute-done | bytes 376864 | tf_op jit(solution)/shard_map/ppermute | solution.py:50
  93.7 3.8 %collective-permute-done.28 = bf16[2,240,128]{2,1,0:T(8,128)(2,1)S(1)} collective-permute-done((bf16[2,240,128]{2,1,0:T(8,128)(2,1)S(1)}, bf16[2,240,128]{2,1,0:T(8,128)(2,1)S(1)}, u32[]{:S(2)}, u32[]{:S(2)}) %collective-permute-start.28) | collective-permute-done | bytes 122912 | tf_op jit(solution)/shard_map/ppermute | solution.py:50
  97.7 2.8 %collective-permute-start.29 = (bf16[2,816,128]{2,1,0:T(8,128)(2,1)S(1)}, bf16[2,816,128]{2,1,0:T(8,128)(2,1)S(1)}, u32[]{:S(2)}, u32[]{:S(2)}) collective-permute-start(bf16[2,816,128]{2,1,0:T(8,128)(2,1)S(1)} %pad_maximum_fusion.8), channel_id=1, source_target_pairs={{0,16},{2,18},{4,20},{6,22},{8,24},{10,26},{12,28},{14,30},{16,0},... | collective-permute-start | bytes 1253384 | tf_op jit(solution)/shard_map/ppermute | solution.py:50
  101.4 4.8 %collective-permute-start.30 = (bf16[64,384]{1,0:T(8,128)(2,1)S(1)}, bf16[64,384]{1,0:T(8,128)(2,1)S(1)}, u32[]{:S(2)}, u32[]{:S(2)}) collective-permute-start(bf16[64,384]{1,0:T(8,128)(2,1)S(1)} %get-tuple-element.220), channel_id=1, source_target_pairs={{0,2},{4,6},{8,10},{12,14},{16,18},{20,22},{24,26},{28,30},{2,0},{... | collective-permute-start | bytes 147464 | tf_op jit(solution)/shard_map/ppermute | solution.py:58
  106.3 2.2 %collective-permute-done.30 = bf16[64,384]{1,0:T(8,128)(2,1)S(1)} collective-permute-done((bf16[64,384]{1,0:T(8,128)(2,1)S(1)}, bf16[64,384]{1,0:T(8,128)(2,1)S(1)}, u32[]{:S(2)}, u32[]{:S(2)}) %collective-permute-start.30) | collective-permute-done | bytes 49184 | tf_op jit(solution)/shard_map/ppermute | solution.py:58
  110.2 3.5 %collective-permute-start.34 = (bf16[2,240,128]{2,1,0:T(8,128)(2,1)S(1)}, bf16[2,240,128]{2,1,0:T(8,128)(2,1)S(1)}, u32[]{:S(2)}, u32[]{:S(2)}) collective-permute-start(bf16[2,240,128]{2,1,0:T(8,128)(2,1)S(1)} %slice.191), channel_id=1, source_target_pairs={{0,4},{2,6},{4,0},{6,2},{8,12},{10,14},{12,8},{14,10},{16,20},{18,... | collective-permute-start | bytes 368648 | tf_op jit(solution)/shard_map/ppermute | solution.py:50
  123.7 5.3 %collective-permute-done.37 = bf16[4,240,128]{2,1,0:T(8,128)(2,1)S(1)} collective-permute-done((bf16[4,240,128]{2,1,0:T(8,128)(2,1)S(1)}, bf16[4,240,128]{2,1,0:T(8,128)(2,1)S(1)}, u32[]{:S(2)}, u32[]{:S(2)}) %collective-permute-start.37) | collective-permute-done | bytes 245792 | tf_op jit(solution)/shard_map/ppermute | solution.py:50
  129.0 1.9 %collective-permute-done.36 = bf16[4,288,128]{2,1,0:T(8,128)(2,1)S(1)} collective-permute-done((bf16[4,288,128]{2,1,0:T(8,128)(2,1)S(1)}, bf16[4,288,128]{2,1,0:T(8,128)(2,1)S(1)}, u32[]{:S(2)}, u32[]{:S(2)}) %collective-permute-start.36) | collective-permute-done | bytes 294944 | tf_op jit(solution)/shard_map/ppermute | solution.py:50
  132.0 3.5 %collective-permute-start.38 = (bf16[2,128,384]{2,1,0:T(8,128)(2,1)S(1)}, bf16[2,128,384]{2,1,0:T(8,128)(2,1)S(1)}, u32[]{:S(2)}, u32[]{:S(2)}) collective-permute-start(bf16[2,128,384]{2,1,0:T(8,128)(2,1)S(1)} %pad_maximum_fusion.16), channel_id=1, source_target_pairs={{0,16},{2,18},{4,20},{6,22},{8,24},{10,26},{12,28},{14,30},{16,0},... | collective-permute-start | bytes 589832 | tf_op jit(solution)/shard_map/ppermute | solution.py:50
  137.6 2.1 %unpack.2 = (f32[1152,384]{1,0:T(8,128)}, f32[384,384]{1,0:T(8,128)}, f32[1152,384]{1,0:T(8,128)}, f32[384,384]{1,0:T(8,128)}, f32[768,384]{1,0:T(8,128)}, /*index=5*/f32[384,384]{1,0:T(8,128)}) custom-call(s32[1]{0:T(128)} %bitcast.me_ref, bf16[8,288,128]{2,1,0:T(8,128)(2,1)S(1)} %pad_maximum_fusion.refs_0_, ...), custom_call_target="tpu_custom_call" | custom-call | bytes 8355840 | tf_op jit(solution)/shard_map/unpack/pallas_call | solution.py:746
  142.2 3.5 %collective-permute-done.41.refs_2_ = bf16[8,240,128]{2,1,0:T(8,128)(2,1)S(1)} collective-permute-done((bf16[8,240,128]{2,1,0:T(8,128)(2,1)S(1)}, bf16[8,240,128]{2,1,0:T(8,128)(2,1)S(1)}, u32[]{:S(2)}, u32[]{:S(2)}) %collective-permute-start.41) | collective-permute-done | bytes 491552 | tf_op jit(solution)/shard_map/ppermute | solution.py:50
  145.7 2.1 %unpack.3 = (f32[1152,384]{1,0:T(8,128)}, f32[384,384]{1,0:T(8,128)}, f32[1152,384]{1,0:T(8,128)}, f32[384,384]{1,0:T(8,128)}, f32[768,384]{1,0:T(8,128)}, /*index=5*/f32[384,384]{1,0:T(8,128)}) custom-call(s32[1]{0:T(128)} %bitcast.me_ref, ...), custom_call_target="tpu_custom_call", output_to_operand_aliasing={{0}: (4, {}), {1}: (5, {}), {2}: (6, {}), {3}: (7, {}), {4}... | custom-call | bytes 8355840 | tf_op jit(solution)/shard_map/unpack/pallas_call | solution.py:746
  (161 shorter events, 57.9 us)
Async XLA Ops:
  0.6 15.7 %collective-permute-start = (bf16[256,384]{1,0:T(8,128)(2,1)}, bf16[256,384]{1,0:T(8,128)(2,1)S(1)}, u32[]{:S(2)}, u32[]{:S(2)}) collective-permute-start(bf16[256,384]{1,0:T(8,128)(2,1)} %node_ref.3), channel_id=1, source_target_pairs={{0,16},{2,18},{4,20},{6,22},{8,24},{10,26},{12,28},{14,30},{16,0},... | collective-permute-start | bytes 589832 | tf_op jit(solution)/shard_map/ppermute | solution.py:50
  5.6 10.8 %collective-permute-start.2 = (bf16[64,384]{1,0:T(8,128)(2,1)S(1)}, bf16[64,384]{1,0:T(8,128)(2,1)S(1)}, u32[]{:S(2)}, u32[]{:S(2)}) collective-permute-start(bf16[64,384]{1,0:T(8,128)(2,1)S(1)} %get-tuple-element.215), channel_id=1, source_target_pairs={{2,4},{6,8},{10,12},{14,16},{18,20},{22,24},{26,28},{4,2},{8,6},{1... | collective-permute-start | bytes 147464 | tf_op jit(solution)/shard_map/ppermute | solution.py:59
  6.3 10.1 %collective-permute-start.1 = (bf16[64,384]{1,0:T(8,128)(2,1)S(1)}, bf16[64,384]{1,0:T(8,128)(2,1)S(1)}, u32[]{:S(2)}, u32[]{:S(2)}) collective-permute-start(bf16[64,384]{1,0:T(8,128)(2,1)S(1)} %get-tuple-element.216), channel_id=1, source_target_pairs={{0,2},{4,6},{8,10},{12,14},{16,18},{20,22},{24,26},{28,30},{2,0},{... | collective-permute-start | bytes 147464 | tf_op jit(solution)/shard_map/ppermute | solution.py:58
  24.7 8.8 %collective-permute-start.8 = (bf16[4,256,128]{2,1,0:T(8,128)(2,1)S(1)}, bf16[4,256,128]{2,1,0:T(8,128)(2,1)S(1)}, u32[]{:S(2)}, u32[]{:S(2)}) collective-permute-start(bf16[4,256,128]{2,1,0:T(8,128)(2,1)S(1)} %get-tuple-element.118), channel_id=1, source_target_pairs={{0,4},{2,6},{4,0},{6,2},{8,12},{10,14},{12,8},{14,10},{16,20},{18,... | collective-permute-start | bytes 786440 | tf_op jit(solution)/shard_map/ppermute | solution.py:50
  24.9 8.6 %collective-permute-start.9 = (bf16[4,256,128]{2,1,0:T(8,128)(2,1)S(1)}, bf16[4,256,128]{2,1,0:T(8,128)(2,1)S(1)}, u32[]{:S(2)}, u32[]{:S(2)}) collective-permute-start(bf16[4,256,128]{2,1,0:T(8,128)(2,1)S(1)} %get-tuple-element.119), channel_id=1, source_target_pairs={{0,8},{2,10},{4,12},{6,14},{8,0},{10,2},{12,4},{14,6},{16,24},{18,... | collective-permute-start | bytes 786440 | tf_op jit(solution)/shard_map/ppermute | solution.py:50
  51.1 15.8 %collective-permute-start.15 = (bf16[8,288,128]{2,1,0:T(8,128)(2,1)}, bf16[8,288,128]{2,1,0:T(8,128)(2,1)S(1)}, u32[]{:S(2)}, u32[]{:S(2)}) collective-permute-start(bf16[8,288,128]{2,1,0:T(8,128)(2,1)} %get-tuple-element.149), channel_id=1, source_target_pairs={{0,4},{2,6},{4,0},{6,2},{8,12},{10,14},{12,8},{14,10},{16,20},{18,... | collective-permute-start | bytes 1769480 | tf_op jit(solution)/shard_map/ppermute | solution.py:50
  51.3 15.7 %collective-permute-start.16 = (bf16[8,240,128]{2,1,0:T(8,128)(2,1)S(1)}, bf16[8,240,128]{2,1,0:T(8,128)(2,1)S(1)}, u32[]{:S(2)}, u32[]{:S(2)}) collective-permute-start(bf16[8,240,128]{2,1,0:T(8,128)(2,1)S(1)} %get-tuple-element.150), channel_id=1, source_target_pairs={{0,8},{2,10},{4,12},{6,14},{8,0},{10,2},{12,4},{14,6},{16,24},{18,... | collective-permute-start | bytes 1474568 | tf_op jit(solution)/shard_map/ppermute | solution.py:50
  53.2 9.7 %collective-permute-start.17 = (bf16[4,128,256]{2,1,0:T(8,128)(2,1)S(1)}, bf16[4,128,256]{2,1,0:T(8,128)(2,1)S(1)}, u32[]{:S(2)}, u32[]{:S(2)}) collective-permute-start(bf16[4,128,256]{2,1,0:T(8,128)(2,1)S(1)} %get-tuple-element.151.refs_2_), channel_id=1, source_target_pairs={{0,2},{2,0},{4,6},{6,4},{8,10},{10,8},{12,14},{14,12},{16,18},{18,... | collective-permute-start | bytes 786440 | tf_op jit(solution)/shard_map/ppermute | solution.py:50
  53.6 12.0 %collective-permute-start.18 = (bf16[4,128,128]{2,1,0:T(8,128)(2,1)S(1)}, bf16[4,128,128]{2,1,0:T(8,128)(2,1)S(1)}, u32[]{:S(2)}, u32[]{:S(2)}) collective-permute-start(bf16[4,128,128]{2,1,0:T(8,128)(2,1)S(1)} %get-tuple-element.152.refs_3_), channel_id=1, source_target_pairs={{0,4},{2,6},{4,0},{6,2},{8,12},{10,14},{12,8},{14,10},{16,20},{18,... | collective-permute-start | bytes 393224 | tf_op jit(solution)/shard_map/ppermute | solution.py:50
  62.8 9.9 %collective-permute-start.22 = (bf16[8,288,128]{2,1,0:T(8,128)(2,1)S(1)}, bf16[8,288,128]{2,1,0:T(8,128)(2,1)S(1)}, u32[]{:S(2)}, u32[]{:S(2)}) collective-permute-start(bf16[8,288,128]{2,1,0:T(8,128)(2,1)S(1)} %get-tuple-element.161), channel_id=1, source_target_pairs={{0,2},{2,0},{4,6},{6,4},{8,10},{10,8},{12,14},{14,12},{16,18},{18,... | collective-permute-start | bytes 1769480 | tf_op jit(solution)/shard_map/ppermute | solution.py:50
  66.9 8.6 %collective-permute-start.19 = (bf16[8,128,128]{2,1,0:T(8,128)(2,1)S(1)}, bf16[8,128,128]{2,1,0:T(8,128)(2,1)S(1)}, u32[]{:S(2)}, u32[]{:S(2)}) collective-permute-start(bf16[8,128,128]{2,1,0:T(8,128)(2,1)S(1)} %get-tuple-element.158), channel_id=1, source_target_pairs={{0,8},{2,10},{4,12},{6,14},{8,0},{10,2},{12,4},{14,6},{16,24},{18,... | collective-permute-start | bytes 786440 | tf_op jit(solution)/shard_map/ppermute | solution.py:50
  68.0 9.1 %collective-permute-start.20 = (bf16[8,128,128]{2,1,0:T(8,128)(2,1)S(1)}, bf16[8,128,128]{2,1,0:T(8,128)(2,1)S(1)}, u32[]{:S(2)}, u32[]{:S(2)}) collective-permute-start(bf16[8,128,128]{2,1,0:T(8,128)(2,1)S(1)} %get-tuple-element.159), channel_id=1, source_target_pairs={{0,4},{2,6},{4,0},{6,2},{8,12},{10,14},{12,8},{14,10},{16,20},{18,... | collective-permute-start | bytes 786440 | tf_op jit(solution)/shard_map/ppermute | solution.py:50
  68.1 12.7 %collective-permute-start.21 = (bf16[8,128,128]{2,1,0:T(8,128)(2,1)S(1)}, bf16[8,128,128]{2,1,0:T(8,128)(2,1)S(1)}, u32[]{:S(2)}, u32[]{:S(2)}) collective-permute-start(bf16[8,128,128]{2,1,0:T(8,128)(2,1)S(1)} %get-tuple-element.160), channel_id=1, source_target_pairs={{0,8},{2,10},{4,12},{6,14},{8,0},{10,2},{12,4},{14,6},{16,24},{18,... | collective-permute-start | bytes 786440 | tf_op jit(solution)/shard_map/ppermute | solution.py:50
  81.2 9.5 %collective-permute-start.23 = (bf16[4,416,128]{2,1,0:T(8,128)(2,1)S(1)}, bf16[4,416,128]{2,1,0:T(8,128)(2,1)S(1)}, u32[]{:S(2)}, u32[]{:S(2)}) collective-permute-start(bf16[4,416,128]{2,1,0:T(8,128)(2,1)S(1)} %pad_maximum_fusion.6), channel_id=1, source_target_pairs={{0,4},{2,6},{4,0},{6,2},{8,12},{10,14},{12,8},{14,10},{16,20},{18,... | collective-permute-start | bytes 1277960 | tf_op jit(solution)/shard_map/ppermute | solution.py:50
  81.4 9.4 %collective-permute-start.24 = (bf16[4,416,128]{2,1,0:T(8,128)(2,1)S(1)}, bf16[4,416,128]{2,1,0:T(8,128)(2,1)S(1)}, u32[]{:S(2)}, u32[]{:S(2)}) collective-permute-start(bf16[4,416,128]{2,1,0:T(8,128)(2,1)S(1)} %pad_maximum_fusion.7), channel_id=1, source_target_pairs={{0,8},{2,10},{4,12},{6,14},{8,0},{10,2},{12,4},{14,6},{16,24},{18,... | collective-permute-start | bytes 1277960 | tf_op jit(solution)/shard_map/ppermute | solution.py:50
  82.5 7.7 %collective-permute-start.25 = (bf16[4,368,128]{2,1,0:T(8,128)(2,1)S(1)}, bf16[4,368,128]{2,1,0:T(8,128)(2,1)S(1)}, u32[]{:S(2)}, u32[]{:S(2)}) collective-permute-start(bf16[4,368,128]{2,1,0:T(8,128)(2,1)S(1)} %pad_maximum_fusion.9), channel_id=1, source_target_pairs={{0,2},{2,0},{4,6},{6,4},{8,10},{10,8},{12,14},{14,12},{16,18},{18,... | collective-permute-start | bytes 1130504 | tf_op jit(solution)/shard_map/ppermute | solution.py:50
  97.7 12.3 %collective-permute-start.29 = (bf16[2,816,128]{2,1,0:T(8,128)(2,1)S(1)}, bf16[2,816,128]{2,1,0:T(8,128)(2,1)S(1)}, u32[]{:S(2)}, u32[]{:S(2)}) collective-permute-start(bf16[2,816,128]{2,1,0:T(8,128)(2,1)S(1)} %pad_maximum_fusion.8), channel_id=1, source_target_pairs={{0,16},{2,18},{4,20},{6,22},{8,24},{10,26},{12,28},{14,30},{16,0},... | collective-permute-start | bytes 1253384 | tf_op jit(solution)/shard_map/ppermute | solution.py:50
  120.2 8.9 %collective-permute-start.37 = (bf16[4,240,128]{2,1,0:T(8,128)(2,1)S(1)}, bf16[4,240,128]{2,1,0:T(8,128)(2,1)S(1)}, u32[]{:S(2)}, u32[]{:S(2)}) collective-permute-start(bf16[4,240,128]{2,1,0:T(8,128)(2,1)S(1)} %pad_maximum_fusion.15), channel_id=1, source_target_pairs={{0,2},{2,0},{4,6},{6,4},{8,10},{10,8},{12,14},{14,12},{16,18},{18,... | collective-permute-start | bytes 737288 | tf_op jit(solution)/shard_map/ppermute | solution.py:50
  121.0 9.9 %collective-permute-start.36 = (bf16[4,288,128]{2,1,0:T(8,128)(2,1)S(1)}, bf16[4,288,128]{2,1,0:T(8,128)(2,1)S(1)}, u32[]{:S(2)}, u32[]{:S(2)}) collective-permute-start(bf16[4,288,128]{2,1,0:T(8,128)(2,1)S(1)} %pad_maximum_fusion.11), channel_id=1, source_target_pairs={{0,8},{2,10},{4,12},{6,14},{8,0},{10,2},{12,4},{14,6},{16,24},{18,... | collective-permute-start | bytes 884744 | tf_op jit(solution)/shard_map/ppermute | solution.py:50
  121.8 9.9 %collective-permute-start.35 = (bf16[4,288,128]{2,1,0:T(8,128)(2,1)S(1)}, bf16[4,288,128]{2,1,0:T(8,128)(2,1)S(1)}, u32[]{:S(2)}, u32[]{:S(2)}) collective-permute-start(bf16[4,288,128]{2,1,0:T(8,128)(2,1)S(1)} %pad_maximum_fusion.10), channel_id=1, source_target_pairs={{0,4},{2,6},{4,0},{6,2},{8,12},{10,14},{12,8},{14,10},{16,20},{18,... | collective-permute-start | bytes 884744 | tf_op jit(solution)/shard_map/ppermute | solution.py:50
  132.0 9.3 %collective-permute-start.38 = (bf16[2,128,384]{2,1,0:T(8,128)(2,1)S(1)}, bf16[2,128,384]{2,1,0:T(8,128)(2,1)S(1)}, u32[]{:S(2)}, u32[]{:S(2)}) collective-permute-start(bf16[2,128,384]{2,1,0:T(8,128)(2,1)S(1)} %pad_maximum_fusion.16), channel_id=1, source_target_pairs={{0,16},{2,18},{4,20},{6,22},{8,24},{10,26},{12,28},{14,30},{16,0},... | collective-permute-start | bytes 589832 | tf_op jit(solution)/shard_map/ppermute | solution.py:50
  135.5 10.2 %collective-permute-start.41 = (bf16[8,240,128]{2,1,0:T(8,128)(2,1)S(1)}, bf16[8,240,128]{2,1,0:T(8,128)(2,1)S(1)}, u32[]{:S(2)}, u32[]{:S(2)}) collective-permute-start(bf16[8,240,128]{2,1,0:T(8,128)(2,1)S(1)} %pad_maximum_fusion.5.refs_2_), channel_id=1, source_target_pairs={{0,8},{2,10},{4,12},{6,14},{8,0},{10,2},{12,4},{14,6},{16,24},{18,... | collective-permute-start | bytes 1474568 | tf_op jit(solution)/shard_map/ppermute | solution.py:50
  135.6 10.1 %collective-permute-start.39 = (bf16[8,288,128]{2,1,0:T(8,128)(2,1)S(1)}, bf16[8,288,128]{2,1,0:T(8,128)(2,1)S(1)}, u32[]{:S(2)}, u32[]{:S(2)}) collective-permute-start(bf16[8,288,128]{2,1,0:T(8,128)(2,1)S(1)} %pad_maximum_fusion.refs_0_), channel_id=1, source_target_pairs={{0,2},{2,0},{4,6},{6,4},{8,10},{10,8},{12,14},{14,12},{16,18},{18,... | collective-permute-start | bytes 1769480 | tf_op jit(solution)/shard_map/ppermute | solution.py:50
  135.8 9.9 %collective-permute-start.40 = (bf16[8,288,128]{2,1,0:T(8,128)(2,1)S(1)}, bf16[8,288,128]{2,1,0:T(8,128)(2,1)S(1)}, u32[]{:S(2)}, u32[]{:S(2)}) collective-permute-start(bf16[8,288,128]{2,1,0:T(8,128)(2,1)S(1)} %pad_maximum_fusion.1.refs_1_), channel_id=1, source_target_pairs={{0,4},{2,6},{4,0},{6,2},{8,12},{10,14},{12,8},{14,10},{16,20},{18,... | collective-permute-start | bytes 1769480 | tf_op jit(solution)/shard_map/ppermute | solution.py:50
  (37 other events, 236.5 us)
